TPU v7x, 512 devices: a whole 4x4x16 slice. The times are simulated.
512 devices in a mesh: ctx: 128 (over z, x, y_hi), head: 4 (over y_lo, core).
Axes of the slice: x: 4, y: 4 (y_hi: 2, y_lo: 2; y = y_hi * 2 + y_lo), z: 16, core: 2. Of those that a mesh axis runs over, the one named last changes fastest.
Arguments:
- inputs: bfloat16 [65536, 4096], P('ctx', 'head'), may hold values from -6 to 6
- queries: bfloat16 [65536, 2048], P('ctx', 'head'), may hold values from -112 to 112
- keys: bfloat16 [65536, 2048], P('ctx', 'head'), may hold values from -4 to 4
- values: bfloat16 [65536, 2048], P('ctx', 'head'), may hold values from -6 to 6
- output_gradient: bfloat16 [65536, 2048], P('ctx', 'head'), may hold values from -6 to 6
- adapter_down_maps: bfloat16 [3, 4096, 16], P(None, 'head'), may hold values from -0.09375 to 0.09375
- adapter_up_maps: bfloat16 [3, 16, 2048], P(None, None, 'head'), may hold values from -0.125 to 0.125
- shifted_head_flags: int32 [16], P('head'), may hold values from 0 to 1, as said below
Outputs:
- qkv_input_gradients: bfloat16 [3, 65536, 2048], P(None, 'ctx', 'head')
- grad_down: float32 [3, 4096, 16], P(None, 'head')
- grad_up: float32 [3, 16, 2048], P(None, None, 'head')
Inputs may be any that keep to these rules, and one draw needn't show every extreme that they name: `shifted_head_flags`: exactly half of the 16 heads have flag 1.
All inputs are finite; a program needn't handle non-finite values.
Results may differ from a plain program's by a relative error of at most 0.02.
Values may be sent and summed in bfloat16 or wider, within the bound.
No kernel may reach another device: no remote copies, remote signals or barrier semaphores. Data moves between devices by JAX's collectives and lax.ppermute only.
A program may use at most 64 MiB of HBM per device.

v0:
```python
import math

import jax
import jax.numpy as jnp
from jax import lax
from jax.sharding import PartitionSpec as P

GROUP = 1024
SHIFT = 512


def from_behind(value, axis, steps):
    count = lax.axis_size(axis)
    pairs = [(source, (source + steps) % count) for source in range(count)]
    return lax.ppermute(value, axis, pairs)


def unroll(positions, head_flags, seq_total):
    return (positions[None, :] - SHIFT * head_flags[:, None]) % seq_total


def visible(query_pos, key_pos, head_flags, seq_total):
    upper = unroll(query_pos, head_flags, seq_total)
    lower = unroll(key_pos, head_flags, seq_total)
    same_group = upper[:, :, None] // GROUP == lower[:, None, :] // GROUP
    return same_group & (lower[:, None, :] <= upper[:, :, None])


def scores_of(query_rows, key_rows, allowed, score_scale):
    scores = jnp.dot(query_rows, key_rows.T, preferred_element_type=jnp.float32) * score_scale
    return jnp.where(allowed, scores, -jnp.inf)


def query_side(query_rows, key_rows, value_rows, grad_rows, allowed, score_scale):
    scores = scores_of(query_rows, key_rows, allowed, score_scale)
    row_top = jnp.max(scores, axis=1, keepdims=True)
    exponent = jnp.exp(scores - row_top)
    row_sum = jnp.sum(exponent, axis=1, keepdims=True)
    soft_weights = exponent / row_sum
    weights_low = soft_weights.astype(jnp.bfloat16)
    attn_out = jnp.dot(weights_low, value_rows, preferred_element_type=jnp.float32)
    row_delta = jnp.sum(grad_rows.astype(jnp.float32) * attn_out, axis=1, keepdims=True)
    dprobs = jnp.dot(grad_rows, value_rows.T, preferred_element_type=jnp.float32)
    dscores = (soft_weights * (dprobs - row_delta)).astype(jnp.bfloat16)
    query_grad = jnp.dot(dscores, key_rows, preferred_element_type=jnp.float32) * score_scale
    key_grad = (
        jnp.einsum("qk,qd->kd", dscores, query_rows, preferred_element_type=jnp.float32)
        * score_scale
    )
    value_grad = jnp.einsum("qk,qd->kd", weights_low, grad_rows, preferred_element_type=jnp.float32)
    return (query_grad, key_grad, value_grad, row_top[:, 0], row_sum[:, 0], row_delta[:, 0])


def local(
    inputs,
    queries,
    keys,
    values,
    output_gradient,
    adapter_down_maps,
    adapter_up_maps,
    shifted_head_flags,
):
    tok_rows, col_width = queries.shape
    head_count = shifted_head_flags.shape[0]
    head_dim = col_width // head_count
    rank_extent = adapter_down_maps.shape[2]
    score_scale = 1.0 / math.sqrt(head_dim)
    ctx_size = lax.axis_size("ctx")
    ctx_index = lax.axis_index("ctx")
    seq_total = ctx_size * tok_rows
    back_reach = (GROUP + tok_rows - 1) // tok_rows - 1 + min(SHIFT % tok_rows, 1)
    reduced_rank_part = jnp.concatenate(
        [
            jnp.dot(inputs, adapter_down_maps[projection_index], preferred_element_type=jnp.float32)
            for projection_index in range(3)
        ],
        axis=1,
    )
    reduced_rank_part = lax.psum(reduced_rank_part, "head").astype(jnp.bfloat16)

    def split_heads(matrix):
        return matrix.reshape(matrix.shape[0], head_count, head_dim).transpose(1, 0, 2)

    key_blocks = [keys]
    value_blocks = [values]
    distance = 1
    moved_keys, moved_values = from_behind((keys, values), "ctx", distance)
    key_blocks.append(moved_keys)
    value_blocks.append(moved_values)
    all_keys = split_heads(jnp.concatenate(key_blocks, 0))
    all_values = split_heads(jnp.concatenate(value_blocks, 0))
    offsets = jnp.arange(tok_rows, dtype=jnp.int32)
    own_pos = ctx_index * tok_rows + offsets
    key_pos = jnp.concatenate(
        [
            (ctx_index - distance) % ctx_size * tok_rows + offsets
            for distance in range(back_reach + 1)
        ]
    )
    allowed = visible(own_pos, key_pos, shifted_head_flags, seq_total)
    query_heads = split_heads(queries)
    grad_heads = split_heads(output_gradient)

    def run_query(head_items):
        return query_side(
            head_items[0], head_items[1], head_items[2], head_items[3], head_items[4], score_scale
        )

    query_grad, key_part, value_part, row_top, row_sum, row_delta = lax.map(
        run_query, (query_heads, all_keys, all_values, grad_heads, allowed)
    )
    key_grad = key_part[:, :tok_rows]
    value_grad = value_part[:, :tok_rows]
    distance = 1
    start_col = distance * tok_rows
    back_keys, back_values = from_behind(
        (
            key_part[:, start_col : start_col + tok_rows],
            value_part[:, start_col : start_col + tok_rows],
        ),
        "ctx",
        -distance,
    )
    key_grad = key_grad + back_keys
    value_grad = value_grad + back_values

    def merge_heads(stacked):
        return stacked.transpose(1, 0, 2).reshape(tok_rows, col_width).astype(jnp.bfloat16)

    qkv_input_gradients = jnp.stack(
        [merge_heads(query_grad), merge_heads(key_grad), merge_heads(value_grad)]
    )
    backward_projection = jnp.concatenate(
        [
            jnp.dot(
                qkv_input_gradients[projection_index],
                adapter_up_maps[projection_index].T,
                preferred_element_type=jnp.float32,
            )
            for projection_index in range(3)
        ],
        axis=1,
    )
    backward_projection = lax.psum(backward_projection, "head").astype(jnp.bfloat16)
    grad_down = jnp.stack(
        [
            jnp.einsum(
                "td,tr->dr",
                inputs,
                backward_projection[
                    :, projection_index * rank_extent : (projection_index + 1) * rank_extent
                ],
                preferred_element_type=jnp.float32,
            )
            for projection_index in range(3)
        ]
    )
    grad_up = jnp.stack(
        [
            jnp.einsum(
                "tr,tc->rc",
                reduced_rank_part[
                    :, projection_index * rank_extent : (projection_index + 1) * rank_extent
                ],
                qkv_input_gradients[projection_index],
                preferred_element_type=jnp.float32,
            )
            for projection_index in range(3)
        ]
    )
    grad_down, grad_up = lax.psum((grad_down, grad_up), "ctx")
    norm_factor = 1.0 / math.sqrt(seq_total)
    return (qkv_input_gradients, grad_down * norm_factor, grad_up * norm_factor)


def solution(mesh):
    in_specs = (
        P("ctx", "head"),
        P("ctx", "head"),
        P("ctx", "head"),
        P("ctx", "head"),
        P("ctx", "head"),
        P(None, "head", None),
        P(None, None, "head"),
        P("head"),
    )
    out_specs = (P(None, "ctx", "head"), P(None, "head", None), P(None, None, "head"))
    return jax.shard_map(local, mesh=mesh, in_specs=in_specs, out_specs=out_specs, check_vma=False)
```

profile of v0, /device:TPU:2, one launch (start us, length us, event | category | flops | bytes accessed | tf_op | source)
XLA Modules:
  0.0 1438.3 jit_solution(6800035928123611106)
XLA Ops:
  8.6 5.1 collective-permute-start
  15.0 3.2 collective-permute-start.1
  20.6 3.1 compare_and_fusion
  23.7 4.2 collective-permute-done
  27.9 2.1 pad_maximum_fusion.1
  30.0 8.0 collective-permute-done.1
  37.9 2.1 pad_maximum_fusion.2
  40.1 50.6 %while.14 = (s32[]{:T(128)}, bf16[4,512,128]{1,2,0:T(8,128)(2,1)}, f32[4,1024,128]{1,2,0:T(8,128)}, f32[4,1024,128]{1,2,0:T(8,128)}, pred[4,512,1024]{2,1,0:T(32...) while((s32[]{:T(128)}, bf16[4,512,128]{1,2,0:T(8,128)(2,1)}, ...), condition=%wide.region_4.5_spmd, body=%wide.region_0.4_spmd.sunk | while | flops 814152192 | bytes 19690084 | solution.py:110
  40.1 1.8 fusion.103
  42.4 2.4 fusion.108
  44.8 1.7 fusion.105
  46.4 1.7 multiply_convert_fusion.2
  52.8 1.8 fusion.103
  55.1 2.3 fusion.108
  57.4 1.7 fusion.105
  59.1 1.7 multiply_convert_fusion.2
  65.4 1.8 fusion.103
  67.7 2.4 fusion.108
  70.1 1.7 fusion.105
  71.7 1.7 multiply_convert_fusion.2
  78.0 1.8 fusion.103
  80.4 2.3 fusion.108
  82.7 1.7 fusion.105
  84.3 1.7 multiply_convert_fusion.2
  92.0 4.2 collective-permute-start.2
  98.4 13.3 collective-permute-start.3
  112.3 9.1 collective-permute-done.2
  121.9 20.0 %collective-permute-done.3 = f32[4,512,128]{1,2,0:T(8,128)S(1)} collective-permute-done((f32[4,512,128]{1,2,0:T(8,128)S(1)}, f32[4,512,128]{1,2,0:T(8,128)S(1)}, u32[]{:S(2)}, u32[]{:S(2)}) %collective-permute-start.3) | collective-permute-done | bytes 1048608 | tf_op jit(solution)/shard_map/ppermute | solution.py:15
  143.5 12.2 all-reduce.6
  160.5 1267.8 %all-reduce.5.cloned.1.call-done = (f32[3,1024,16]{1,2,0:T(8,128)}, f32[3,16,512]{2,1,0:T(8,128)}) async-done(((f32[3,1024,16]{1,2,0:T(8,128)}, f32[3,16,512]{2,1,0:T(8,128)}), (f32[3,1024,16]{1,2,0:T(8,128)}, f32[3,16,512]{2,1,0:T(8,128)})) %all-reduce.5.cloned.1.call-update) | async-done | bytes 294928 | tf_op jit(solution)/shard_map/psum | solution.py:172
  1428.3 1.6 broadcast_multiply_fusion
  1429.9 1.5 broadcast_multiply_fusion.1
  (83 shorter events, 36.3 us)
Async XLA Ops:
  7.2 89.0 %copy-start = (bf16[512,1024]{1,0:T(8,128)(2,1)S(1)}, bf16[512,1024]{1,0:T(8,128)(2,1)}, u32[]{:S(2)}) copy-start(bf16[512,1024]{1,0:T(8,128)(2,1)} %param.10) | copy-start | bytes 3145732
  7.2 11.1 copy-start.7
  7.2 11.3 copy-start.3
  7.2 12.4 copy-start.4
  7.2 1421.1 %all-reduce.5.cloned.1.call-start = ((), (), s32[]{:S(2)}) async-start(), calls=%async_computation | async-start | bytes 589824 | tf_op jit(solution)/shard_map/psum | solution.py:172
  8.6 19.2 %collective-permute-start = (bf16[512,512]{0,1:T(8,128)(2,1)S(1)}, bf16[512,512]{0,1:T(8,128)(2,1)}, u32[]{:S(2)}, u32[]{:S(2)}) collective-permute-start(bf16[512,512]{0,1:T(8,128)(2,1)S(1)} %copy.17), channel_id=1, source_target_pairs={{0,4},{4,8},{8,12},{12,16},{16,20},{20,24},{24,28},{28,32},{32,36}... | collective-permute-start | bytes 1572872 | tf_op jit(solution)/shard_map/ppermute | solution.py:15
  15.0 22.9 %collective-permute-start.1 = (bf16[512,512]{0,1:T(8,128)(2,1)S(1)}, bf16[512,512]{0,1:T(8,128)(2,1)}, u32[]{:S(2)}, u32[]{:S(2)}) collective-permute-start(bf16[512,512]{0,1:T(8,128)(2,1)S(1)} %copy.20), channel_id=1, source_target_pairs={{0,4},{4,8},{8,12},{12,16},{16,20},{20,24},{24,28},{28,32},{32,36}... | collective-permute-start | bytes 1572872 | tf_op jit(solution)/shard_map/ppermute | solution.py:15
  90.7 5.5 copy-start.5
  92.0 29.5 %collective-permute-start.2 = (f32[4,512,128]{1,2,0:T(8,128)S(1)}, f32[4,512,128]{1,2,0:T(8,128)S(1)}, u32[]{:S(2)}, u32[]{:S(2)}) collective-permute-start(f32[4,512,128]{1,2,0:T(8,128)S(1)} %slice.49), channel_id=1, source_target_pairs={{0,508},{4,0},{8,4},{12,8},{16,12},{20,16},{24,20},{28,24},{32,28}... | collective-permute-start | bytes 3145736 | tf_op jit(solution)/shard_map/ppermute | solution.py:15
  96.6 15.6 %copy-start.1 = (bf16[4,512,128]{1,2,0:T(8,128)(2,1)S(1)}, bf16[4,512,128]{1,2,0:T(8,128)(2,1)}, u32[]{:S(2)}) copy-start(bf16[4,512,128]{1,2,0:T(8,128)(2,1)} %get-tuple-element.52) | copy-start | bytes 1572868
  96.6 15.6 %copy-start.6 = (bf16[3,16,512]{2,1,0:T(8,128)(2,1)S(1)}, bf16[3,16,512]{2,1,0:T(8,128)(2,1)}, u32[]{:S(2)}) copy-start(bf16[3,16,512]{2,1,0:T(8,128)(2,1)} %param.16) | copy-start | bytes 147460
  96.9 24.5 %copy-start.2 = (f32[4,1024,128]{1,2,0:T(8,128)S(1)}, f32[4,1024,128]{1,2,0:T(8,128)}, u32[]{:S(2)}) copy-start(f32[4,1024,128]{1,2,0:T(8,128)} %get-tuple-element.53) | copy-start | bytes 6291460
  98.4 43.5 %collective-permute-start.3 = (f32[4,512,128]{1,2,0:T(8,128)S(1)}, f32[4,512,128]{1,2,0:T(8,128)S(1)}, u32[]{:S(2)}, u32[]{:S(2)}) collective-permute-start(f32[4,512,128]{1,2,0:T(8,128)S(1)} %slice.51), channel_id=1, source_target_pairs={{0,508},{4,0},{8,4},{12,8},{16,12},{20,16},{24,20},{28,24},{32,28}... | collective-permute-start | bytes 3145736 | tf_op jit(solution)/shard_map/ppermute | solution.py:15
Sparse Core Ops, SparseCore 0:
  158.6 1269.6 all-reduce.4
where the time goes:
time: 1440 us
  waiting for transfers between devices  1310 us (91%)
  matrix products  44.2 us (3%)
  starting transfers between devices  25.8 us (2%)
  other arithmetic  17.1 us (1%)
  local copies, waits for them, and re-layouts  15.4 us (1%)
    psum x1, waiting for transfers between devices, local(): grad_down, grad_up = lax.psum((grad_down, grad_up), 'ctx')  1270 us
    ppermute x4, waiting for transfers between devices, from_behind(): return lax.ppermute(value, axis, pairs)  41.2 us
  transfers between devices with their start and end apart: 5, of which 5 were waited for; matrix products, arithmetic and copies ran while one was open for 1% of the time, Pallas kernels for 0%

commit v1 on v0

v1 whole, which is shorter than its diff:
```python
import functools
import math

import jax
import jax.numpy as jnp
from jax import lax
from jax.experimental import pallas as pl
from jax.experimental.pallas import tpu as pltpu
from jax.sharding import Mesh, PartitionSpec as P

HEAD = 128
RANK = 16
TILE = 256
CTX = ("z", "x", "yh")
NEAR = ("x", "yh")
F32 = jnp.float32
BF16 = jnp.bfloat16
VMEM_BYTES = 48 * 1024 * 1024


def dot_nt(left, right):
    return lax.dot_general(left, right, (((1,), (1,)), ((), ())), preferred_element_type=F32)


def dot_tn(left, right):
    return lax.dot_general(left, right, (((0,), (0,)), ((), ())), preferred_element_type=F32)


def dot_nn(left, right):
    return lax.dot_general(left, right, (((1,), (0,)), ((), ())), preferred_element_type=F32)


def list_heads(role_ref, order_ref, wanted):
    count = jnp.int32(0)
    for head in range(role_ref.shape[0]):
        chosen = role_ref[head] == wanted

        @pl.when(chosen)
        def _():
            order_ref[count] = head

        count = count + chosen.astype(jnp.int32)
    return count


def columns_of(head):
    return pl.ds(pl.multiple_of(head * HEAD, HEAD), HEAD)


def causal_mask(rows):
    keys = lax.broadcasted_iota(jnp.int32, (rows, rows), 0)
    queries = lax.broadcasted_iota(jnp.int32, (rows, rows), 1)
    return keys <= queries


def scores_t(key_rows, query_rows, masked):
    scores = dot_nt(key_rows, query_rows)
    if masked:
        scores = jnp.where(causal_mask(TILE), scores, -jnp.inf)
    return scores


def tile_pieces(tile, own, before):
    pieces = [] if before is None else [(before, 0, before[0].shape[0], False)]
    if own is not None:
        if tile:
            pieces.append((own, 0, tile * TILE, False))
        pieces.append((own, tile * TILE, TILE, True))
    return pieces


def row_stats(pieces, query_rows, grad_rows, factor):
    scores = [
        scores_t(pair[0][start : start + rows], query_rows, masked)
        for pair, start, rows, masked in pieces
    ]
    top = functools.reduce(jnp.maximum, [jnp.max(s, axis=0, keepdims=True) for s in scores])
    total = jnp.zeros_like(top)
    mixed = jnp.zeros_like(top)
    for s, (pair, start, rows, _) in zip(scores, pieces):
        exponent = jnp.exp2((s - top) * factor)
        dprobs = dot_nt(pair[1][start : start + rows], grad_rows)
        total = total + jnp.sum(exponent, axis=0, keepdims=True)
        mixed = mixed + jnp.sum(exponent * dprobs, axis=0, keepdims=True)
    inverse = 1.0 / total
    return top, inverse, mixed * inverse


def piece_back(piece, query_rows, grad_rows, stats, factor):
    pair, start, rows, masked = piece
    top, inverse, delta = stats
    scores = scores_t(pair[0][start : start + rows], query_rows, masked)
    probs = jnp.exp2((scores - top) * factor) * inverse
    dprobs = dot_nt(pair[1][start : start + rows], grad_rows)
    dscores = (probs * (dprobs - delta)).astype(BF16)
    return probs.astype(BF16), dscores


def head_back(queries, grads, own, before, stats_of, factor, scale, want_query):
    tok_rows = queries.shape[0]
    key_grad, value_grad = {}, {}
    query_grad = []
    for tile in range(tok_rows // TILE):
        query_rows = queries[tile * TILE : (tile + 1) * TILE]
        grad_rows = grads[tile * TILE : (tile + 1) * TILE]
        stats = stats_of(tile)
        query_t = None
        for piece in tile_pieces(tile, own, before):
            pair, start, rows, masked = piece
            probs, dscores = piece_back(piece, query_rows, grad_rows, stats, factor)
            if want_query:
                term = dot_tn(pair[0][start : start + rows], dscores)
                query_t = term if query_t is None else query_t + term
            if want_query and pair is before:
                continue
            key_term = dot_nn(dscores, query_rows)
            value_term = dot_nn(probs, grad_rows)
            for part in range(rows // TILE):
                cut = slice(part * TILE, (part + 1) * TILE)
                block = start // TILE + part
                if block in key_grad:
                    key_grad[block] = key_grad[block] + key_term[cut]
                    value_grad[block] = value_grad[block] + value_term[cut]
                else:
                    key_grad[block] = key_term[cut]
                    value_grad[block] = value_term[cut]
        if want_query:
            query_grad.append(query_t.T * scale)
    blocks = range(tok_rows // TILE)
    key_grad = jnp.concatenate([key_grad[b] for b in blocks], 0) * scale
    value_grad = jnp.concatenate([value_grad[b] for b in blocks], 0)
    return (jnp.concatenate(query_grad, 0) if want_query else None), key_grad, value_grad


def pack_kernel(wanted, role_ref, a_ref, b_ref, out_ref, order_ref):
    count = list_heads(role_ref, order_ref, wanted)

    def step(slot, _):
        cols = columns_of(order_ref[slot])
        out_ref[slot, 0] = a_ref[:, cols]
        out_ref[slot, 1] = b_ref[:, cols]
        return 0

    lax.fori_loop(0, count, step, 0)


def first_kernel(factor, scale, role_ref, q_ref, k_ref, v_ref, g_ref, dq_ref, dk_ref, dv_ref, order_ref):
    count = list_heads(role_ref, order_ref, 0)

    def step(slot, _):
        cols = columns_of(order_ref[slot])
        queries, grads = q_ref[:, cols], g_ref[:, cols]
        own = (k_ref[:, cols], v_ref[:, cols])

        def stats_of(tile):
            cut = slice(tile * TILE, (tile + 1) * TILE)
            return row_stats(tile_pieces(tile, own, None), queries[cut], grads[cut], factor)

        dq, dk, dv = head_back(queries, grads, own, None, stats_of, factor, scale, True)
        dq_ref[slot] = dq.astype(BF16)
        dk_ref[slot] = dk
        dv_ref[slot] = dv
        return 0

    lax.fori_loop(0, count, step, 0)


def stats_kernel(factor, role_ref, q_ref, k_ref, v_ref, g_ref, kv_ref, stats_ref, order_ref):
    count = list_heads(role_ref, order_ref, 1)

    def step(slot, _):
        cols = columns_of(order_ref[slot])
        own = (k_ref[:, cols], v_ref[:, cols])
        before = (kv_ref[slot, 0], kv_ref[slot, 1])
        for tile in range(q_ref.shape[0] // TILE):
            cut = slice(tile * TILE, (tile + 1) * TILE)
            rows = row_stats(
                tile_pieces(tile, own, before), q_ref[cut, cols], g_ref[cut, cols], factor
            )
            for index in range(3):
                stats_ref[slot, index : index + 1, cut] = rows[index]
        return 0

    lax.fori_loop(0, count, step, 0)


def second_kernel(factor, scale, role_ref, q_ref, k_ref, v_ref, g_ref, kv_ref, stats_ref, out_ref, order_ref):
    count = list_heads(role_ref, order_ref, 1)

    def step(slot, _):
        cols = columns_of(order_ref[slot])
        own = (k_ref[:, cols], v_ref[:, cols])
        before = (kv_ref[slot, 0], kv_ref[slot, 1])

        def stats_of(tile):
            cut = slice(tile * TILE, (tile + 1) * TILE)
            return tuple(stats_ref[slot, index : index + 1, cut] for index in range(3))

        grads = head_back(
            q_ref[:, cols], g_ref[:, cols], own, before, stats_of, factor, scale, True
        )
        for index in range(3):
            out_ref[slot, index] = grads[index].astype(BF16)
        return 0

    lax.fori_loop(0, count, step, 0)


def last_kernel(
    factor, scale, role_ref, k_ref, v_ref, qg_ref, stats_ref, dq_ref, dk_ref, dv_ref, second_ref,
    up_ref, out_ref, back_ref, order_ref,
):
    count = list_heads(role_ref, order_ref, 1)

    def copy(slot, _):
        cols = columns_of(order_ref[slot])
        for index in range(3):
            out_ref[index, :, cols] = second_ref[slot, index]
        return 0

    lax.fori_loop(0, count, copy, 0)
    count = list_heads(role_ref, order_ref, 0)

    def step(slot, _):
        cols = columns_of(order_ref[slot])
        before = (k_ref[:, cols], v_ref[:, cols])

        def stats_of(tile):
            cut = slice(tile * TILE, (tile + 1) * TILE)
            return tuple(stats_ref[slot, index : index + 1, cut] for index in range(3))

        _, dk, dv = head_back(
            qg_ref[slot, 0], qg_ref[slot, 1], None, before, stats_of, factor, scale, False
        )
        out_ref[0, :, cols] = dq_ref[slot]
        out_ref[1, :, cols] = (dk_ref[slot] + dk).astype(BF16)
        out_ref[2, :, cols] = (dv_ref[slot] + dv).astype(BF16)
        return 0

    lax.fori_loop(0, count, step, 0)
    for index in range(3):
        back_ref[index * RANK : (index + 1) * RANK] = dot_nt(up_ref[index], out_ref[index]).astype(BF16)


def adapter_kernel(norm_factor, parts_ref, inputs_ref, qkv_ref, out_ref):
    summed = functools.reduce(
        jnp.add, [parts_ref[index].astype(F32) for index in range(parts_ref.shape[0])]
    ).astype(BF16)
    rows = 3 * RANK
    down = dot_nn(summed[:rows], inputs_ref[...]) * norm_factor
    up = jnp.concatenate(
        [
            dot_nn(summed[rows + index * RANK : rows + (index + 1) * RANK], qkv_ref[index])
            for index in range(3)
        ],
        0,
    ) * norm_factor
    place = 0
    for total in (down, up):
        for start in range(0, total.shape[1], HEAD):
            out_ref[place : place + rows] = total[:, start : start + HEAD].astype(BF16)
            place += rows


VMEM = pl.BlockSpec(memory_space=pltpu.VMEM)
SMEM = pl.BlockSpec(memory_space=pltpu.SMEM)


def call(kernel, outs, in_specs, flops, heads=0):
    many = isinstance(outs, (list, tuple))
    return pl.pallas_call(
        kernel,
        out_shape=outs,
        in_specs=in_specs,
        out_specs=[VMEM] * len(outs) if many else VMEM,
        scratch_shapes=[pltpu.SMEM((heads,), jnp.int32)] if heads else [],
        compiler_params=pltpu.CompilerParams(vmem_limit_bytes=VMEM_BYTES),
        cost_estimate=pl.CostEstimate(flops=flops, bytes_accessed=4 << 20, transcendentals=0),
    )


def shape(dims, dtype):
    return jax.ShapeDtypeStruct(dims, dtype)


def attention(slots, role, queries, keys, values, grads, inputs, down_t, up):
    tok_rows = queries.shape[0]
    heads = role.shape[0]
    scale = 1.0 / math.sqrt(HEAD)
    factor = scale * math.log2(math.e)
    count = lax.axis_size(CTX)
    ahead = [(source, (source + 1) % count) for source in range(count)]
    behind = [(source, (source - 1) % count) for source in range(count)]
    pair = shape((slots, 2, tok_rows, HEAD), BF16)
    low = shape((slots, tok_rows, HEAD), BF16)
    full = shape((slots, tok_rows, HEAD), F32)
    unit = 2 * tok_rows * tok_rows * HEAD * slots

    kv = call(functools.partial(pack_kernel, 0), pair, [SMEM, VMEM, VMEM], 1000, heads)(role, keys, values)
    kv = lax.ppermute(kv, CTX, ahead)
    qg = call(functools.partial(pack_kernel, 1), pair, [SMEM, VMEM, VMEM], 1000, heads)(role, queries, grads)
    qg = lax.ppermute(qg, CTX, behind)
    low_rank = dot_nt(down_t, inputs).astype(BF16)
    first = call(
        functools.partial(first_kernel, factor, scale), [low, full, full], [SMEM] + [VMEM] * 4, 6 * unit, heads
    )(role, queries, keys, values, grads)
    stats = call(
        functools.partial(stats_kernel, factor),
        shape((slots, 8, tok_rows), F32),
        [SMEM] + [VMEM] * 5,
        4 * unit,
        heads,
    )(role, queries, keys, values, grads, kv)
    moved = lax.ppermute(stats, CTX, behind)
    second = call(
        functools.partial(second_kernel, factor, scale),
        shape((slots, 3, tok_rows, HEAD), BF16),
        [SMEM] + [VMEM] * 6,
        8 * unit,
        heads,
    )(role, queries, keys, values, grads, kv, stats)
    qkv, back = call(
        functools.partial(last_kernel, factor, scale),
        [shape((3,) + queries.shape, BF16), shape((3 * RANK, tok_rows), BF16)],
        [SMEM] + [VMEM] * 9,
        4 * unit,
        heads,
    )(role, keys, values, qg, moved, *first, second, up)
    return qkv, jnp.concatenate([back, low_rank], 0)


def local(inputs, queries, keys, values, grads, down, up, flags):
    tok_rows = queries.shape[0]
    heads = flags.shape[0]
    width = inputs.shape[1]
    seq_total = lax.axis_size(CTX) * tok_rows
    role = (lax.axis_index(CTX) + flags) % 2
    shifted = jnp.sum(flags)
    slots = jnp.maximum(shifted, heads - shifted)
    least = (heads + 1) // 2
    down_t = down.transpose(0, 2, 1).reshape(3 * RANK, width)
    qkv, parts = lax.switch(
        slots - least,
        [functools.partial(attention, number) for number in range(least, heads + 1)],
        role, queries, keys, values, grads, inputs, down_t, up,
    )
    parts = lax.all_gather(parts, "head")
    rows = 3 * RANK * (width + queries.shape[1]) // HEAD
    near = lax.axis_size(NEAR)
    grad = call(
        functools.partial(adapter_kernel, 1.0 / math.sqrt(seq_total)),
        shape((rows, HEAD), BF16),
        [VMEM] * 3,
        1 << 28,
    )(parts, inputs, qkv)
    grad = lax.all_to_all(grad.reshape(near, rows // near, HEAD), NEAR, 0, 0)
    grad = jnp.sum(grad.astype(F32), 0).astype(BF16)
    far = lax.axis_size("z")
    grad = lax.all_to_all(jnp.broadcast_to(grad, (far,) + grad.shape), "z", 0, 0)
    grad = jnp.sum(grad.astype(F32), 0).astype(BF16)
    grad = lax.all_to_all(jnp.broadcast_to(grad, (near,) + grad.shape), NEAR, 0, 0)
    grad = grad.reshape(-1, 3, RANK, HEAD).astype(F32)
    split = width // HEAD
    grad_down = grad[:split].transpose(1, 0, 3, 2).reshape(3, width, RANK)
    grad_up = grad[split:].transpose(1, 2, 0, 3).reshape(3, RANK, -1)
    return qkv, grad_down, grad_up


def solution(mesh):
    count, columns = mesh.devices.shape
    across = 4 if count >= 128 else 2
    fine = Mesh(mesh.devices.reshape(count // (2 * across), across, 2, columns), CTX + ("head",))
    in_specs = (
        P(CTX, "head"),
        P(CTX, "head"),
        P(CTX, "head"),
        P(CTX, "head"),
        P(CTX, "head"),
        P(None, "head", None),
        P(None, None, "head"),
        P("head"),
    )
    out_specs = (P(None, CTX, "head"), P(None, "head", None), P(None, None, "head"))
    return jax.shard_map(local, mesh=fine, in_specs=in_specs, out_specs=out_specs, check_vma=False)
```

time: 1440 us -> 123 us (0.09)
  the two profiles are of different devices: /device:TPU:2 before, /device:TPU:64 now
where the time goes in v1:
time: 123 us
  blocking collectives  65.8 us (53%)
  waiting for transfers between devices  19.8 us (16%)
  starting transfers between devices  16.6 us (13%)
  Pallas kernels  15.2 us (12%)
  between operations  1.98 us (2%)
  local copies, waits for them, and re-layouts  1.45 us (1%)
  other arithmetic  1.41 us (1%)
    all_to_all x1, blocking collectives, local(): lax.all_to_all(jnp.broadcast_to(grad, (far,) + grad.shape), 'z', 0, 0)  33.4 us
    ppermute x1, waiting for transfers between devices, attention(): kv = lax.ppermute(kv, CTX, ahead)  19.8 us
    all_to_all x1, blocking collectives, local(): grad = lax.all_to_all(grad.reshape(near, rows // near, HEAD), NEAR, 0, 0)  15.3 us
    all_to_all x1, blocking collectives, local(): lax.all_to_all(jnp.broadcast_to(grad, (near,) + grad.shape), NEAR, 0, 0)  11 us
    ppermute x1, starting transfers between devices, attention(): moved = lax.ppermute(stats, CTX, behind)  6.2 us
    all_gather x1, blocking collectives, local(): parts = lax.all_gather(parts, 'head')  6.15 us
    ppermute x1, starting transfers between devices, attention(): kv = lax.ppermute(kv, CTX, ahead)  5.21 us
    ppermute x1, starting transfers between devices, attention(): qg = lax.ppermute(qg, CTX, behind)  5.17 us
  transfers between devices with their start and end apart: 3, of which 1 were waited for; matrix products, arithmetic and copies ran while one was open for 0% of the time, Pallas kernels for 8%

profile of v1, /device:TPU:64, one launch (start us, length us, event | category | flops | bytes accessed | tf_op | source)
XLA Modules:
  0.0 123.0 jit_solution(11589538558085769614)
XLA Ops:
  0.6 1.3 %and_select_fusion = (s32[4]{0:T(128)S(1)}, s32[]{:T(128)}) fusion(s32[4]{0:T(128)} %param.18, s32[]{:T(128)S(6)} %add.20), kind=kLoop, calls=%fused_computation.12 | loop fusion | flops 51 | bytes 40 | tf_op jit(solution)/shard_map/jit(remainder)/select_n | solution.py:337
  3.2 50.8 %conditional.1 = (bf16[3,512,512]{2,1,0:T(8,128)(2,1)S(1)}, bf16[96,512]{1,0:T(8,128)(2,1)S(1)}) conditional(s32[]{:T(128)} %clamp.3, (s32[4]{0:T(128)S(1)}, bf16[512,512]{1,0:T(8,128)(2,1)}, bf16[512,512]{1,0:T(8,128)(2,1)}, bf16[512,512]{1,0:T(8,128)(2,1)}, bf16[512,512]{1,0:T(8,128)(2,1)}, ...), branch_computations={%region_1.2_spmd, %region_2.3_spmd, %region_3.4_spmd} | conditional | flops 5956134912 | bytes 48382284 | solution.py:342
  3.3 0.0 copy-start.10
  3.3 0.0 copy-start.13
  3.3 0.0 copy-start.1
  3.3 0.0 copy-start.4
  3.3 1.4 %branch_1_fun.7 = bf16[3,2,512,128]{3,2,1,0:T(8,128)(2,1)S(1)} custom-call(s32[4]{0:T(128)S(1)} %get-tuple-element.61.role_ref, bf16[512,512]{1,0:T(8,128)(2,1)} %get-tuple-element.62.a_ref.k_ref, bf16[512,512]{1,0:T(8,128)(2,1)} %get-tuple-element.63.b_ref.v_ref), custom_call_target="tpu_custom_call" | custom-call | flops 1000 | bytes 4194304 | tf_op jit(solution)/shard_map/cond/branch_1_fun/pallas_call | solution.py:299
  4.7 5.2 %collective-permute-start.4 = (bf16[3,2,512,128]{3,2,1,0:T(8,128)(2,1)S(1)}, bf16[3,2,512,128]{3,2,1,0:T(8,128)(2,1)S(1)}, u32[]{:S(2)}, u32[]{:S(2)}) collective-permute-start(bf16[3,2,512,128]{3,2,1,0:T(8,128)(2,1)S(1)} %branch_1_fun.7), channel_id=1, source_target_pairs={{0,4},{4,8},{8,12},{12,16},{16,20},{20,24},{24,28},{28,32},{32,36}... | collective-permute-start | bytes 2359304 | tf_op jit(solution)/shard_map/cond/branch_1_fun/ppermute | solution.py:300
  9.9 0.0 copy-done.10
  10.0 0.0 copy-done.13
  10.0 0.7 branch_1_fun.6
  10.7 0.0 copy-start.7
  10.7 0.0 copy-start.17
  10.7 5.2 %collective-permute-start.3 = (bf16[3,2,512,128]{3,2,1,0:T(8,128)(2,1)S(1)}, bf16[3,2,512,128]{3,2,1,0:T(8,128)(2,1)S(1)}, u32[]{:S(2)}, u32[]{:S(2)}) collective-permute-start(bf16[3,2,512,128]{3,2,1,0:T(8,128)(2,1)S(1)} %branch_1_fun.6), channel_id=1, source_target_pairs={{0,508},{4,0},{8,4},{12,8},{16,12},{20,16},{24,20},{28,24},{32,28}... | collective-permute-start | bytes 2359304 | tf_op jit(solution)/shard_map/cond/branch_1_fun/ppermute | solution.py:302
  15.9 1.7 %branch_1_fun.9 = (bf16[3,512,128]{2,1,0:T(8,128)(2,1)S(1)}, f32[3,512,128]{2,1,0:T(8,128)S(1)}, f32[3,512,128]{2,1,0:T(8,128)S(1)}) custom-call(s32[4]{0:T(128)S(1)} %get-tuple-element.61.role_ref, bf16[512,512]{1,0:T(8,128)(2,1)S(1)} %copy-done.10, bf16[512,512]{1,0:T(8,128)(2,1)S(1)} %copy-done.1, bf16[512,512]{1,0:T(8,128)(2,1)S(1)} %copy-done.4, ...), custom_call_target="tpu_custom_call" | custom-call | flops 1207959552 | bytes 4194304 | tf_op jit(solution)/shard_map/cond/branch_1_fun/pallas_call | solution.py:304
  17.7 0.4 convolution_convert_fusion.1
  18.1 19.8 %collective-permute-done.4.kv_ref = bf16[3,2,512,128]{3,2,1,0:T(8,128)(2,1)S(1)} collective-permute-done((bf16[3,2,512,128]{3,2,1,0:T(8,128)(2,1)S(1)}, bf16[3,2,512,128]{3,2,1,0:T(8,128)(2,1)S(1)}, u32[]{:S(2)}, u32[]{:S(2)}) %collective-permute-start.4) | collective-permute-done | bytes 786464 | tf_op jit(solution)/shard_map/cond/branch_1_fun/ppermute | solution.py:300
  37.9 2.9 %branch_1_fun.8.stats_ref = f32[3,8,512]{2,1,0:T(8,128)S(1)} custom-call(s32[4]{0:T(128)S(1)} %get-tuple-element.61.role_ref, bf16[512,512]{1,0:T(8,128)(2,1)S(1)} %copy-done.10, bf16[512,512]{1,0:T(8,128)(2,1)S(1)} %copy-done.1, bf16[512,512]{1,0:T(8,128)(2,1)S(1)} %copy-done.4, bf16[512,512]{1,0:T(8,128)(2,1)S(1)} %copy-done.13, ...), custom_call_target="tpu_custom_call" | custom-call | flops 805306368 | bytes 4194304 | tf_op jit(solution)/shard_map/cond/branch_1_fun/pallas_call | solution.py:307
  40.8 0.0 copy-start.20
  40.8 6.2 %collective-permute-start.5 = (f32[3,8,512]{2,1,0:T(8,128)S(1)}, f32[3,8,512]{2,1,0:T(8,128)S(1)}, u32[]{:S(2)}, u32[]{:S(2)}) collective-permute-start(f32[3,8,512]{2,1,0:T(8,128)S(1)} %branch_1_fun.8.stats_ref), channel_id=1, source_target_pairs={{0,508},{4,0},{8,4},{12,8},{16,12},{20,16},{24,20},{28,24},{32,28}... | collective-permute-start | bytes 147464 | tf_op jit(solution)/shard_map/cond/branch_1_fun/ppermute | solution.py:314
  47.1 4.6 %branch_1_fun.10.second_ref = bf16[3,3,512,128]{3,2,1,0:T(8,128)(2,1)S(1)} custom-call(s32[4]{0:T(128)S(1)} %get-tuple-element.61.role_ref, bf16[512,512]{1,0:T(8,128)(2,1)S(1)} %copy-done.10, bf16[512,512]{1,0:T(8,128)(2,1)S(1)} %copy-done.1, bf16[512,512]{1,0:T(8,128)(2,1)S(1)} %copy-done.4, bf16[512,512]{1,0:T(8,128)(2,1)S(1)} %copy-done.13, ...), custom_call_target="tpu_custom_call" | custom-call | flops 1610612736 | bytes 4194304 | tf_op jit(solution)/shard_map/cond/branch_1_fun/pallas_call | solution.py:315
  51.7 0.0 collective-permute-done.3.qg_ref
  51.7 0.0 collective-permute-done.5.stats_ref
  51.7 2.0 %branch_1_fun.11 = (bf16[3,512,512]{2,1,0:T(8,128)(2,1)S(1)}, bf16[48,512]{1,0:T(8,128)(2,1)S(1)}) custom-call(s32[4]{0:T(128)S(1)} %get-tuple-element.61.role_ref, bf16[512,512]{1,0:T(8,128)(2,1)S(1)} %copy-done.1, bf16[512,512]{1,0:T(8,128)(2,1)S(1)} %copy-done.4, bf16[3,2,512,128]{3,2,1,0:T(8,128)(2,1)S(1)} %collective-permute-done.3.qg_ref, ...), custom_call_target="tpu_custom_call" | custom-call | flops 805306368 | bytes 4194304 | tf_op jit(solution)/shard_map/cond/branch_1_fun/pallas_call | solution.py:322
  54.0 0.0 copy-start.15
  54.0 6.1 %all-gather = bf16[384,512]{1,0:T(8,128)(2,1)S(1)} all-gather(bf16[96,512]{1,0:T(8,128)(2,1)S(1)} %get-tuple-element.93), channel_id=2, replica_groups=mesh['z'=16,'x'=4,'yh'=2,'head'=4] {'head'}, dimensions={0}, use_global_device_ids=true | all-gather | bytes 491520 | tf_op jit(solution)/shard_map/all_gather | solution.py:347
  60.2 1.7 %shard_map.103 = bf16[576,128]{1,0:T(8,128)(2,1)S(1)} custom-call(bf16[4,96,512]{2,1,0:T(8,128)(2,1)S(1)} %bitcast.25, bf16[512,1024]{1,0:T(8,128)(2,1)} %inputs_ref.1, bf16[3,512,512]{2,1,0:T(8,128)(2,1)S(1)} %get-tuple-element.89.qkv_ref), custom_call_target="tpu_custom_call" | custom-call | flops 268435456 | bytes 4194304 | tf_op jit(solution)/shard_map/pallas_call | solution.py:350
  61.9 15.3 %all_to_all.15 = bf16[8,72,128]{2,1,0:T(8,128)(2,1)S(1)} all-to-all(bf16[8,72,128]{2,1,0:T(8,128)(2,1)S(1)} %bitcast.26), channel_id=1, replica_groups=mesh['z'=16,'x'=4,'yh'=2,'head'=4] {'x','yh'}, dimensions={0} | all-to-all | bytes 294912 | tf_op jit(solution)/shard_map/all_to_all | solution.py:356
  77.2 33.4 %all_to_all.16 = bf16[16,72,128]{2,1,0:T(8,128)(2,1)S(1)} all-to-all(bf16[16,72,128]{2,1,0:T(8,128)(2,1)S(1)} %broadcast_in_dim.6), channel_id=1, replica_groups=mesh['z'=16,'x'=4,'yh'=2,'head'=4] {'z'}, dimensions={0} | all-to-all | bytes 589824 | tf_op jit(solution)/shard_map/all_to_all | solution.py:359
  110.7 11.0 %all_to_all.17 = bf16[8,72,128]{2,1,0:T(8,128)(2,1)S(1)} all-to-all(bf16[8,72,128]{2,1,0:T(8,128)(2,1)S(1)} %broadcast_in_dim.7), channel_id=1, replica_groups=mesh['z'=16,'x'=4,'yh'=2,'head'=4] {'x','yh'}, dimensions={0} | all-to-all | bytes 294912 | tf_op jit(solution)/shard_map/all_to_all | solution.py:361
  121.7 0.7 copy_bitcast_fusion
  122.4 0.6 copy_bitcast_fusion.1
  (12 shorter events, 0.2 us)
Async XLA Ops:
  3.3 6.7 %copy-start.10 = (bf16[512,512]{1,0:T(8,128)(2,1)S(1)}, bf16[512,512]{1,0:T(8,128)(2,1)}, u32[]{:S(2)}) copy-start(bf16[512,512]{1,0:T(8,128)(2,1)} %get-tuple-element.64.a_ref.q_ref) | copy-start | bytes 1572868 | tf_op jit(solution)/shard_map/cond
  3.3 6.7 %copy-start.13 = (bf16[512,512]{1,0:T(8,128)(2,1)S(1)}, bf16[512,512]{1,0:T(8,128)(2,1)}, u32[]{:S(2)}) copy-start(bf16[512,512]{1,0:T(8,128)(2,1)} %get-tuple-element.65.b_ref.g_ref) | copy-start | bytes 1572868 | tf_op jit(solution)/shard_map/cond
  3.3 12.6 %copy-start.1 = (bf16[512,512]{1,0:T(8,128)(2,1)S(1)}, bf16[512,512]{1,0:T(8,128)(2,1)}, u32[]{:S(2)}) copy-start(bf16[512,512]{1,0:T(8,128)(2,1)} %get-tuple-element.62.a_ref.k_ref) | copy-start | bytes 1572868 | tf_op jit(solution)/shard_map/cond
  3.3 12.6 %copy-start.4 = (bf16[512,512]{1,0:T(8,128)(2,1)S(1)}, bf16[512,512]{1,0:T(8,128)(2,1)}, u32[]{:S(2)}) copy-start(bf16[512,512]{1,0:T(8,128)(2,1)} %get-tuple-element.63.b_ref.v_ref) | copy-start | bytes 1572868 | tf_op jit(solution)/shard_map/cond
  4.7 33.2 %collective-permute-start.4 = (bf16[3,2,512,128]{3,2,1,0:T(8,128)(2,1)S(1)}, bf16[3,2,512,128]{3,2,1,0:T(8,128)(2,1)S(1)}, u32[]{:S(2)}, u32[]{:S(2)}) collective-permute-start(bf16[3,2,512,128]{3,2,1,0:T(8,128)(2,1)S(1)} %branch_1_fun.7), channel_id=1, source_target_pairs={{0,4},{4,8},{8,12},{12,16},{16,20},{20,24},{24,28},{28,32},{32,36}... | collective-permute-start | bytes 2359304 | tf_op jit(solution)/shard_map/cond/branch_1_fun/ppermute | solution.py:300
  10.7 6.9 %copy-start.7 = (bf16[512,1024]{1,0:T(8,128)(2,1)S(1)}, bf16[512,1024]{1,0:T(8,128)(2,1)}, u32[]{:S(2)}) copy-start(bf16[512,1024]{1,0:T(8,128)(2,1)} %get-tuple-element.73) | copy-start | bytes 3145732 | tf_op jit(solution)/shard_map/cond
  10.7 6.9 %copy-start.17 = (bf16[48,1024]{1,0:T(8,128)(2,1)S(1)}, bf16[48,1024]{1,0:T(8,128)(2,1)}, u32[]{:S(2)}) copy-start(bf16[48,1024]{1,0:T(8,128)(2,1)} %get-tuple-element.72) | copy-start | bytes 294916 | tf_op jit(solution)/shard_map/cond
  10.7 41.0 %collective-permute-start.3 = (bf16[3,2,512,128]{3,2,1,0:T(8,128)(2,1)S(1)}, bf16[3,2,512,128]{3,2,1,0:T(8,128)(2,1)S(1)}, u32[]{:S(2)}, u32[]{:S(2)}) collective-permute-start(bf16[3,2,512,128]{3,2,1,0:T(8,128)(2,1)S(1)} %branch_1_fun.6), channel_id=1, source_target_pairs={{0,508},{4,0},{8,4},{12,8},{16,12},{20,16},{24,20},{28,24},{32,28}... | collective-permute-start | bytes 2359304 | tf_op jit(solution)/shard_map/cond/branch_1_fun/ppermute | solution.py:302
  40.8 10.9 %copy-start.20 = (bf16[3,16,512]{2,1,0:T(8,128)(2,1)S(1)}, bf16[3,16,512]{2,1,0:T(8,128)(2,1)}, u32[]{:S(2)}) copy-start(bf16[3,16,512]{2,1,0:T(8,128)(2,1)} %get-tuple-element.69.up_ref) | copy-start | bytes 147460 | tf_op jit(solution)/shard_map/cond
  40.8 10.9 %collective-permute-start.5 = (f32[3,8,512]{2,1,0:T(8,128)S(1)}, f32[3,8,512]{2,1,0:T(8,128)S(1)}, u32[]{:S(2)}, u32[]{:S(2)}) collective-permute-start(f32[3,8,512]{2,1,0:T(8,128)S(1)} %branch_1_fun.8.stats_ref), channel_id=1, source_target_pairs={{0,508},{4,0},{8,4},{12,8},{16,12},{20,16},{24,20},{28,24},{32,28}... | collective-permute-start | bytes 147464 | tf_op jit(solution)/shard_map/cond/branch_1_fun/ppermute | solution.py:314
  54.0 7.9 %copy-start.15 = (bf16[3,512,512]{2,1,0:T(8,128)(2,1)}, bf16[3,512,512]{2,1,0:T(8,128)(2,1)S(1)}, u32[]{:S(2)}) copy-start(bf16[3,512,512]{2,1,0:T(8,128)(2,1)S(1)} %get-tuple-element.89.qkv_ref) | copy-start | bytes 4718596

commit v2 on v1

--- a/solution.py
+++ b/solution.py
@@ -32,7 +32,7 @@
 
 def list_heads(role_ref, order_ref, wanted):
     count = jnp.int32(0)
-    for head in range(role_ref.shape[0]):
+    for head in range(role_ref.shape[0] - 1):
         chosen = role_ref[head] == wanted
 
         @pl.when(chosen)
@@ -132,8 +132,19 @@
     return (jnp.concatenate(query_grad, 0) if want_query else None), key_grad, value_grad
 
 
+def run_sides(role_ref, sides, step):
+    for parity, ref, count in sides:
+        if parity is None:
+            lax.fori_loop(0, count, functools.partial(step, ref), 0)
+        else:
+
+            @pl.when(role_ref[role_ref.shape[0] - 1] == parity)
+            def _():
+                lax.fori_loop(0, count, functools.partial(step, ref), 0)
+
+
 def pack_kernel(wanted, role_ref, a_ref, b_ref, out_ref, order_ref):
-    count = list_heads(role_ref, order_ref, wanted)
+    list_heads(role_ref, order_ref, wanted)
 
     def step(slot, _):
         cols = columns_of(order_ref[slot])
@@ -141,7 +152,22 @@
         out_ref[slot, 1] = b_ref[:, cols]
         return 0
 
-    lax.fori_loop(0, count, step, 0)
+    lax.fori_loop(0, out_ref.shape[0], step, 0)
+
+
+def pack_pairs_kernel(flags, role_ref, q_ref, k_ref, v_ref, g_ref, *refs):
+    *out_refs, order_ref = refs
+    for wanted, sent in ((0, (k_ref, v_ref)), (1, (q_ref, g_ref))):
+        list_heads(role_ref, order_ref, wanted)
+
+        def step(out_ref, slot, _):
+            cols = columns_of(order_ref[slot])
+            out_ref[slot, 0] = sent[0][:, cols]
+            out_ref[slot, 1] = sent[1][:, cols]
+            return 0
+
+        sides = [((wanted + flag) % 2, ref, ref.shape[0]) for flag, ref in zip(flags, out_refs)]
+        run_sides(role_ref, sides, step)
 
 
 def first_kernel(factor, scale, role_ref, q_ref, k_ref, v_ref, g_ref, dq_ref, dk_ref, dv_ref, order_ref):
@@ -165,10 +191,15 @@
     lax.fori_loop(0, count, step, 0)
 
 
-def stats_kernel(factor, role_ref, q_ref, k_ref, v_ref, g_ref, kv_ref, stats_ref, order_ref):
-    count = list_heads(role_ref, order_ref, 1)
-
-    def step(slot, _):
+def side_refs(refs, parities):
+    return [(parity, ref, ref.shape[0]) for parity, ref in zip(parities, refs)]
+
+
+def stats_kernel(factor, parities, role_ref, q_ref, k_ref, v_ref, g_ref, *refs):
+    *kv_refs, stats_ref, order_ref = refs
+    list_heads(role_ref, order_ref, 1)
+
+    def step(kv_ref, slot, _):
         cols = columns_of(order_ref[slot])
         own = (k_ref[:, cols], v_ref[:, cols])
         before = (kv_ref[slot, 0], kv_ref[slot, 1])
@@ -181,13 +212,14 @@
                 stats_ref[slot, index : index + 1, cut] = rows[index]
         return 0
 
-    lax.fori_loop(0, count, step, 0)
-
-
-def second_kernel(factor, scale, role_ref, q_ref, k_ref, v_ref, g_ref, kv_ref, stats_ref, out_ref, order_ref):
-    count = list_heads(role_ref, order_ref, 1)
-
-    def step(slot, _):
+    run_sides(role_ref, side_refs(kv_refs, parities), step)
+
+
+def second_kernel(factor, scale, parities, role_ref, q_ref, k_ref, v_ref, g_ref, stats_ref, *refs):
+    *kv_refs, out_ref, order_ref = refs
+    list_heads(role_ref, order_ref, 1)
+
+    def step(kv_ref, slot, _):
         cols = columns_of(order_ref[slot])
         own = (k_ref[:, cols], v_ref[:, cols])
         before = (kv_ref[slot, 0], kv_ref[slot, 1])
@@ -203,13 +235,14 @@
             out_ref[slot, index] = grads[index].astype(BF16)
         return 0
 
-    lax.fori_loop(0, count, step, 0)
+    run_sides(role_ref, side_refs(kv_refs, parities), step)
 
 
 def last_kernel(
-    factor, scale, role_ref, k_ref, v_ref, qg_ref, stats_ref, dq_ref, dk_ref, dv_ref, second_ref,
-    up_ref, out_ref, back_ref, order_ref,
+    factor, scale, parities, role_ref, k_ref, v_ref, stats_ref, dq_ref, dk_ref, dv_ref, second_ref,
+    up_ref, *refs
 ):
+    *qg_refs, out_ref, back_ref, order_ref = refs
     count = list_heads(role_ref, order_ref, 1)
 
     def copy(slot, _):
@@ -219,9 +252,9 @@
         return 0
 
     lax.fori_loop(0, count, copy, 0)
-    count = list_heads(role_ref, order_ref, 0)
-
-    def step(slot, _):
+    list_heads(role_ref, order_ref, 0)
+
+    def step(qg_ref, slot, _):
         cols = columns_of(order_ref[slot])
         before = (k_ref[:, cols], v_ref[:, cols])
 
@@ -237,7 +270,7 @@
         out_ref[2, :, cols] = (dv_ref[slot] + dv).astype(BF16)
         return 0
 
-    lax.fori_loop(0, count, step, 0)
+    run_sides(role_ref, side_refs(qg_refs, parities), step)
     for index in range(3):
         back_ref[index * RANK : (index + 1) * RANK] = dot_nt(up_ref[index], out_ref[index]).astype(BF16)
 
@@ -283,49 +316,77 @@
     return jax.ShapeDtypeStruct(dims, dtype)
 
 
-def attention(slots, role, queries, keys, values, grads, inputs, down_t, up):
+def ring(count, parity, step):
+    return [(source, (source + step) % count) for source in range(parity, count, 2)]
+
+
+def attention(shifted, role, queries, keys, values, grads, inputs, down_t, up):
     tok_rows = queries.shape[0]
-    heads = role.shape[0]
+    heads = role.shape[0] - 1
+    plain = heads - shifted
+    slots = max(plain, shifted)
     scale = 1.0 / math.sqrt(HEAD)
     factor = scale * math.log2(math.e)
     count = lax.axis_size(CTX)
-    ahead = [(source, (source + 1) % count) for source in range(count)]
-    behind = [(source, (source - 1) % count) for source in range(count)]
-    pair = shape((slots, 2, tok_rows, HEAD), BF16)
+    ahead = ring(count, 0, 1) + ring(count, 1, 1)
+    behind = ring(count, 0, -1) + ring(count, 1, -1)
     low = shape((slots, tok_rows, HEAD), BF16)
     full = shape((slots, tok_rows, HEAD), F32)
     unit = 2 * tok_rows * tok_rows * HEAD * slots
 
-    kv = call(functools.partial(pack_kernel, 0), pair, [SMEM, VMEM, VMEM], 1000, heads)(role, keys, values)
-    kv = lax.ppermute(kv, CTX, ahead)
-    qg = call(functools.partial(pack_kernel, 1), pair, [SMEM, VMEM, VMEM], 1000, heads)(role, queries, grads)
-    qg = lax.ppermute(qg, CTX, behind)
+    def pair(number):
+        return shape((number, 2, tok_rows, HEAD), BF16)
+
+    if plain == shifted:
+        pack = [SMEM, VMEM, VMEM]
+        kv = call(functools.partial(pack_kernel, 0), pair(slots), pack, 1000, heads)(role, keys, values)
+        kv = [lax.ppermute(kv, CTX, ahead)]
+        qg = call(functools.partial(pack_kernel, 1), pair(slots), pack, 1000, heads)(role, queries, grads)
+        qg = [lax.ppermute(qg, CTX, behind)]
+        kv_parities = qg_parities = [None]
+    else:
+        numbers = (plain, shifted)
+        flags = [flag for flag in range(2) if numbers[flag]]
+        packed = call(
+            functools.partial(pack_pairs_kernel, flags),
+            [pair(numbers[flag]) for flag in flags],
+            [SMEM] + [VMEM] * 4,
+            1000,
+            heads,
+        )(role, queries, keys, values, grads)
+        moved = dict(zip(flags, packed))
+        for flag in sorted(flags, key=lambda flag: -numbers[flag]):
+            swap = ring(count, flag, 1) + ring(count, (flag + 1) % 2, -1)
+            moved[flag] = lax.ppermute(moved[flag], CTX, swap)
+        kv = qg = [moved[flag] for flag in flags]
+        kv_parities = [(flag + 1) % 2 for flag in flags]
+        qg_parities = flags
     low_rank = dot_nt(down_t, inputs).astype(BF16)
     first = call(
         functools.partial(first_kernel, factor, scale), [low, full, full], [SMEM] + [VMEM] * 4, 6 * unit, heads
     )(role, queries, keys, values, grads)
     stats = call(
-        functools.partial(stats_kernel, factor),
+        functools.partial(stats_kernel, factor, kv_parities),
         shape((slots, 8, tok_rows), F32),
-        [SMEM] + [VMEM] * 5,
+        [SMEM] + [VMEM] * (4 + len(kv)),
         4 * unit,
         heads,
-    )(role, queries, keys, values, grads, kv)
+    )(role, queries, keys, values, grads, *kv)
     moved = lax.ppermute(stats, CTX, behind)
     second = call(
-        functools.partial(second_kernel, factor, scale),
+        functools.partial(second_kernel, factor, scale, kv_parities),
         shape((slots, 3, tok_rows, HEAD), BF16),
-        [SMEM] + [VMEM] * 6,
+        [SMEM] + [VMEM] * (5 + len(kv)),
         8 * unit,
         heads,
-    )(role, queries, keys, values, grads, kv, stats)
+    )(role, queries, keys, values, grads, stats, *kv)
     qkv, back = call(
-        functools.partial(last_kernel, factor, scale),
+        functools.partial(last_kernel, factor, scale, qg_parities),
         [shape((3,) + queries.shape, BF16), shape((3 * RANK, tok_rows), BF16)],
-        [SMEM] + [VMEM] * 9,
+        [SMEM] + [VMEM] * (8 + len(qg)),
         4 * unit,
         heads,
-    )(role, keys, values, qg, moved, *first, second, up)
+    )(role, keys, values, moved, *first, second, up, *qg)
     return qkv, jnp.concatenate([back, low_rank], 0)
 
 
@@ -334,14 +395,12 @@
     heads = flags.shape[0]
     width = inputs.shape[1]
     seq_total = lax.axis_size(CTX) * tok_rows
-    role = (lax.axis_index(CTX) + flags) % 2
-    shifted = jnp.sum(flags)
-    slots = jnp.maximum(shifted, heads - shifted)
-    least = (heads + 1) // 2
+    place = lax.axis_index(CTX)
+    role = (place + jnp.concatenate([flags, jnp.zeros((1,), jnp.int32)])) & 1
     down_t = down.transpose(0, 2, 1).reshape(3 * RANK, width)
     qkv, parts = lax.switch(
-        slots - least,
-        [functools.partial(attention, number) for number in range(least, heads + 1)],
+        jnp.sum(flags),
+        [functools.partial(attention, number) for number in range(heads + 1)],
         role, queries, keys, values, grads, inputs, down_t, up,
     )
     parts = lax.all_gather(parts, "head")

time: 123 us -> 120 us (0.976)
  waiting for transfers between devices: 19.8 us -> 15.7 us
    ppermute x2, waiting for transfers between devices: 19.8 us -> 15.7 us  [attention(): moved[flag] = lax.ppermute(moved[flag], CTX, swap)]
    pallas_call x5 -> x4, Pallas kernels: 11.7 us -> 8.52 us  [the longest x1 3.36 us: attention(): call(functools.partial(last_kernel, factor, scale, qg_parities), [shape((...]
    ppermute x1, starting transfers between devices: 6.2 us -> 8.61 us  [attention(): moved = lax.ppermute(stats, CTX, behind)]
    pallas_call x1, Pallas kernels: 1.72 us -> 4.02 us  [attention(): call(functools.partial(first_kernel, factor, scale), [low, full, full], [...]
    select_n x1 -> x0, other arithmetic: 1.29 us -> none  [local(): role = (lax.axis_index(CTX) + flags) % 2]
    reduce_sum x0 -> x1, other arithmetic: none -> 1.29 us  [local(): jnp.sum(flags)]
  transfers between devices with their start and end apart: 3 -> 3, of which waited for: 1 -> 2; matrix products, arithmetic and copies ran while one was open for 0% -> 0% of each run, Pallas kernels for 8% -> 5%
where the time goes in v2:
time: 120 us; the launch traced here: 119 us
  blocking collectives  65.5 us (55%)
  starting transfers between devices  17.8 us (15%)
  waiting for transfers between devices  15.7 us (13%)
  Pallas kernels  14.3 us (12%)
  other arithmetic  2.14 us (2%)
  local copies, waits for them, and re-layouts  1.45 us (1%)
  between operations  1.34 us (1%)
    all_to_all x1, blocking collectives, local(): lax.all_to_all(jnp.broadcast_to(grad, (far,) + grad.shape), 'z', 0, 0)  33.4 us
    ppermute x2, waiting for transfers between devices, attention(): moved[flag] = lax.ppermute(moved[flag], CTX, swap)  15.7 us
    all_to_all x1, blocking collectives, local(): grad = lax.all_to_all(grad.reshape(near, rows // near, HEAD), NEAR, 0, 0)  15 us
    all_to_all x1, blocking collectives, local(): lax.all_to_all(jnp.broadcast_to(grad, (near,) + grad.shape), NEAR, 0, 0)  11 us
    ppermute x2, starting transfers between devices, attention(): moved[flag] = lax.ppermute(moved[flag], CTX, swap)  9.22 us
    ppermute x1, starting transfers between devices, attention(): moved = lax.ppermute(stats, CTX, behind)  8.61 us
    all_gather x1, blocking collectives, local(): parts = lax.all_gather(parts, 'head')  6.15 us
    pallas_call x1, Pallas kernels, attention(): call(functools.partial(first_kernel, factor, scale), [low, full, full], [...  4.02 us
  transfers between devices with their start and end apart: 3, of which 2 were waited for; matrix products, arithmetic and copies ran while one was open for 0% of the time, Pallas kernels for 5%

profile of v2, /device:TPU:64, one launch (start us, length us, event | category | flops | bytes accessed | tf_op | source)
XLA Modules:
  0.0 119.2 jit_solution(4421118990353316516)
XLA Ops:
  0.6 0.7 fusion
  1.4 1.3 %reduce_sum.33 = s32[]{:T(128)} reduce(s32[4]{0:T(128)} %param.20, s32[]{:T(128)} %constant.8.clone.1), dimensions={0}, to_apply=%region_0.0 | reduce | flops 3 | bytes 24 | tf_op jit(solution)/shard_map/reduce_sum | solution.py:402
  3.3 47.2 %conditional.1 = (bf16[3,512,512]{2,1,0:T(8,128)(2,1)S(1)}, bf16[96,512]{1,0:T(8,128)(2,1)S(1)}) conditional(s32[]{:T(128)} %clamp.3, (s32[5]{0:T(128)S(1)}, bf16[512,512]{1,0:T(8,128)(2,1)}, bf16[512,512]{1,0:T(8,128)(2,1)}, bf16[512,512]{1,0:T(8,128)(2,1)}, bf16[512,512]{1,0:T(8,128)(2,1)}, ...), branch_computations={%region_1.0_spmd, %region_2.0_spmd, %region_3.0_spmd, %region_4.0_... | conditional | flops 5956133888 | bytes 44056908 | solution.py:401
  3.3 0.0 copy-start.1
  3.4 0.0 copy-start.6
  3.4 0.0 copy-start.16
  3.4 0.0 copy-start.21
  3.4 1.9 %branch_1_fun.5 = (bf16[3,2,512,128]{3,2,1,0:T(8,128)(2,1)S(1)}, bf16[1,2,512,128]{3,2,1,0:T(8,128)(2,1)S(1)}) custom-call(s32[5]{0:T(128)S(1)} %get-tuple-element.93.role_ref, bf16[512,512]{1,0:T(8,128)(2,1)} %get-tuple-element.96.q_ref, bf16[512,512]{1,0:T(8,128)(2,1)} %get-tuple-element.94.k_ref, bf16[512,512]{1,0:T(8,128)(2,1)} %get-tuple-element.95.v_ref, ...), custom_call_target="tpu_custom_call" | custom-call | flops 1000 | bytes 4194304 | tf_op jit(solution)/shard_map/cond/branch_1_fun/pallas_call | solution.py:350
  5.3 5.1 %collective-permute-start.2 = (bf16[3,2,512,128]{3,2,1,0:T(8,128)(2,1)S(1)}, bf16[3,2,512,128]{3,2,1,0:T(8,128)(2,1)S(1)}, u32[]{:S(2)}, u32[]{:S(2)}) collective-permute-start(bf16[3,2,512,128]{3,2,1,0:T(8,128)(2,1)S(1)} %get-tuple-element.98), channel_id=1, source_target_pairs={{0,4},{8,12},{16,20},{24,28},{32,36},{40,44},{48,52},{56,60},{64,6... | collective-permute-start | bytes 2359304 | tf_op jit(solution)/shard_map/cond/branch_1_fun/ppermute | solution.py:360
  10.4 0.0 copy-start.11
  10.4 0.0 copy-start.26
  10.4 4.1 %collective-permute-start.3 = (bf16[1,2,512,128]{3,2,1,0:T(8,128)(2,1)S(1)}, bf16[1,2,512,128]{3,2,1,0:T(8,128)(2,1)S(1)}, u32[]{:S(2)}, u32[]{:S(2)}) collective-permute-start(bf16[1,2,512,128]{3,2,1,0:T(8,128)(2,1)S(1)} %get-tuple-element.99), channel_id=1, source_target_pairs={{4,8},{12,16},{20,24},{28,32},{36,40},{44,48},{52,56},{60,64},{68,... | collective-permute-start | bytes 786440 | tf_op jit(solution)/shard_map/cond/branch_1_fun/ppermute | solution.py:360
  14.6 0.0 copy-done.1
  14.6 0.0 copy-done.6
  14.6 4.0 %branch_1_fun.7 = (bf16[3,512,128]{2,1,0:T(8,128)(2,1)S(1)}, f32[3,512,128]{2,1,0:T(8,128)S(1)}, f32[3,512,128]{2,1,0:T(8,128)S(1)}) custom-call(s32[5]{0:T(128)S(1)} %get-tuple-element.93.role_ref, bf16[512,512]{1,0:T(8,128)(2,1)S(1)} %copy-done.16, bf16[512,512]{1,0:T(8,128)(2,1)S(1)} %copy-done.1, bf16[512,512]{1,0:T(8,128)(2,1)S(1)} %copy-done.6, ...), custom_call_target="tpu_custom_call" | custom-call | flops 1207959552 | bytes 4194304 | tf_op jit(solution)/shard_map/cond/branch_1_fun/pallas_call | solution.py:365
  18.7 0.4 convolution_convert_fusion.1
  19.1 6.6 %collective-permute-done.3.refs_1_ = bf16[1,2,512,128]{3,2,1,0:T(8,128)(2,1)S(1)} collective-permute-done((bf16[1,2,512,128]{3,2,1,0:T(8,128)(2,1)S(1)}, bf16[1,2,512,128]{3,2,1,0:T(8,128)(2,1)S(1)}, u32[]{:S(2)}, u32[]{:S(2)}) %collective-permute-start.3) | collective-permute-done | bytes 262176 | tf_op jit(solution)/shard_map/cond/branch_1_fun/ppermute | solution.py:360
  25.7 9.1 %collective-permute-done.2.refs_0_ = bf16[3,2,512,128]{3,2,1,0:T(8,128)(2,1)S(1)} collective-permute-done((bf16[3,2,512,128]{3,2,1,0:T(8,128)(2,1)S(1)}, bf16[3,2,512,128]{3,2,1,0:T(8,128)(2,1)S(1)}, u32[]{:S(2)}, u32[]{:S(2)}) %collective-permute-start.2) | collective-permute-done | bytes 786464 | tf_op jit(solution)/shard_map/cond/branch_1_fun/ppermute | solution.py:360
  34.7 1.3 %branch_1_fun.6.stats_ref = f32[3,8,512]{2,1,0:T(8,128)S(1)} custom-call(s32[5]{0:T(128)S(1)} %get-tuple-element.93.role_ref, bf16[512,512]{1,0:T(8,128)(2,1)S(1)} %copy-done.16, bf16[512,512]{1,0:T(8,128)(2,1)S(1)} %copy-done.1, bf16[512,512]{1,0:T(8,128)(2,1)S(1)} %copy-done.6, bf16[512,512]{1,0:T(8,128)(2,1)S(1)} %copy-done.21, ...), custom_call_target="tpu_custom_call" | custom-call | flops 805306368 | bytes 4194304 | tf_op jit(solution)/shard_map/cond/branch_1_fun/pallas_call | solution.py:368
  36.1 0.0 copy-start.32
  36.1 8.6 %collective-permute-start.4 = (f32[3,8,512]{2,1,0:T(8,128)S(1)}, f32[3,8,512]{2,1,0:T(8,128)S(1)}, u32[]{:S(2)}, u32[]{:S(2)}) collective-permute-start(f32[3,8,512]{2,1,0:T(8,128)S(1)} %branch_1_fun.6.stats_ref), channel_id=1, source_target_pairs={{0,508},{8,4},{16,12},{24,20},{32,28},{40,36},{48,44},{56,52},{64,... | collective-permute-start | bytes 147464 | tf_op jit(solution)/shard_map/cond/branch_1_fun/ppermute | solution.py:375
  44.7 1.9 %branch_1_fun.8.second_ref = bf16[3,3,512,128]{3,2,1,0:T(8,128)(2,1)S(1)} custom-call(s32[5]{0:T(128)S(1)} %get-tuple-element.93.role_ref, bf16[512,512]{1,0:T(8,128)(2,1)S(1)} %copy-done.16, bf16[512,512]{1,0:T(8,128)(2,1)S(1)} %copy-done.1, bf16[512,512]{1,0:T(8,128)(2,1)S(1)} %copy-done.6, bf16[512,512]{1,0:T(8,128)(2,1)S(1)} %copy-done.21, ...), custom_call_target="tpu_custom_call" | custom-call | flops 1610612736 | bytes 4194304 | tf_op jit(solution)/shard_map/cond/branch_1_fun/pallas_call | solution.py:376
  46.6 0.0 collective-permute-done.4.stats_ref
  46.7 3.4 %branch_1_fun.9 = (bf16[3,512,512]{2,1,0:T(8,128)(2,1)S(1)}, bf16[48,512]{1,0:T(8,128)(2,1)S(1)}) custom-call(s32[5]{0:T(128)S(1)} %get-tuple-element.93.role_ref, bf16[512,512]{1,0:T(8,128)(2,1)S(1)} %copy-done.1, bf16[512,512]{1,0:T(8,128)(2,1)S(1)} %copy-done.6, f32[3,8,512]{2,1,0:T(8,128)S(1)} %collective-permute-done.4.stats_ref, ...), custom_call_target="tpu_custom_call" | custom-call | flops 805306368 | bytes 4194304 | tf_op jit(solution)/shard_map/cond/branch_1_fun/pallas_call | solution.py:383
  50.5 0.0 copy-start.30
  50.5 6.1 %all-gather = bf16[384,512]{1,0:T(8,128)(2,1)S(1)} all-gather(bf16[96,512]{1,0:T(8,128)(2,1)S(1)} %get-tuple-element.155), channel_id=2, replica_groups=mesh['z'=16,'x'=4,'yh'=2,'head'=4] {'head'}, dimensions={0}, use_global_device_ids=true | all-gather | bytes 491520 | tf_op jit(solution)/shard_map/all_gather | solution.py:406
  56.7 1.7 %shard_map.103 = bf16[576,128]{1,0:T(8,128)(2,1)S(1)} custom-call(bf16[4,96,512]{2,1,0:T(8,128)(2,1)S(1)} %bitcast.29, bf16[512,1024]{1,0:T(8,128)(2,1)} %inputs_ref.1, bf16[3,512,512]{2,1,0:T(8,128)(2,1)S(1)} %get-tuple-element.151.qkv_ref), custom_call_target="tpu_custom_call" | custom-call | flops 268435456 | bytes 4194304 | tf_op jit(solution)/shard_map/pallas_call | solution.py:409
  58.4 15.0 %all_to_all.15 = bf16[8,72,128]{2,1,0:T(8,128)(2,1)S(1)} all-to-all(bf16[8,72,128]{2,1,0:T(8,128)(2,1)S(1)} %bitcast.30), channel_id=1, replica_groups=mesh['z'=16,'x'=4,'yh'=2,'head'=4] {'x','yh'}, dimensions={0} | all-to-all | bytes 294912 | tf_op jit(solution)/shard_map/all_to_all | solution.py:415
  73.4 33.4 %all_to_all.16 = bf16[16,72,128]{2,1,0:T(8,128)(2,1)S(1)} all-to-all(bf16[16,72,128]{2,1,0:T(8,128)(2,1)S(1)} %broadcast_in_dim.6), channel_id=1, replica_groups=mesh['z'=16,'x'=4,'yh'=2,'head'=4] {'z'}, dimensions={0} | all-to-all | bytes 589824 | tf_op jit(solution)/shard_map/all_to_all | solution.py:418
  106.9 11.0 %all_to_all.17 = bf16[8,72,128]{2,1,0:T(8,128)(2,1)S(1)} all-to-all(bf16[8,72,128]{2,1,0:T(8,128)(2,1)S(1)} %broadcast_in_dim.7), channel_id=1, replica_groups=mesh['z'=16,'x'=4,'yh'=2,'head'=4] {'x','yh'}, dimensions={0} | all-to-all | bytes 294912 | tf_op jit(solution)/shard_map/all_to_all | solution.py:420
  117.9 0.7 copy_bitcast_fusion
  118.6 0.6 copy_bitcast_fusion.1
  (12 shorter events, 0.2 us)
Async XLA Ops:
  3.3 11.2 %copy-start.1 = (bf16[512,512]{1,0:T(8,128)(2,1)S(1)}, bf16[512,512]{1,0:T(8,128)(2,1)}, u32[]{:S(2)}) copy-start(bf16[512,512]{1,0:T(8,128)(2,1)} %get-tuple-element.94.k_ref) | copy-start | bytes 1572868 | tf_op jit(solution)/shard_map/cond
  3.4 11.2 %copy-start.6 = (bf16[512,512]{1,0:T(8,128)(2,1)S(1)}, bf16[512,512]{1,0:T(8,128)(2,1)}, u32[]{:S(2)}) copy-start(bf16[512,512]{1,0:T(8,128)(2,1)} %get-tuple-element.95.v_ref) | copy-start | bytes 1572868 | tf_op jit(solution)/shard_map/cond
  3.4 11.2 %copy-start.16 = (bf16[512,512]{1,0:T(8,128)(2,1)S(1)}, bf16[512,512]{1,0:T(8,128)(2,1)}, u32[]{:S(2)}) copy-start(bf16[512,512]{1,0:T(8,128)(2,1)} %get-tuple-element.96.q_ref) | copy-start | bytes 1572868 | tf_op jit(solution)/shard_map/cond
  3.4 11.2 %copy-start.21 = (bf16[512,512]{1,0:T(8,128)(2,1)S(1)}, bf16[512,512]{1,0:T(8,128)(2,1)}, u32[]{:S(2)}) copy-start(bf16[512,512]{1,0:T(8,128)(2,1)} %get-tuple-element.97.g_ref) | copy-start | bytes 1572868 | tf_op jit(solution)/shard_map/cond
  5.3 29.4 %collective-permute-start.2 = (bf16[3,2,512,128]{3,2,1,0:T(8,128)(2,1)S(1)}, bf16[3,2,512,128]{3,2,1,0:T(8,128)(2,1)S(1)}, u32[]{:S(2)}, u32[]{:S(2)}) collective-permute-start(bf16[3,2,512,128]{3,2,1,0:T(8,128)(2,1)S(1)} %get-tuple-element.98), channel_id=1, source_target_pairs={{0,4},{8,12},{16,20},{24,28},{32,36},{40,44},{48,52},{56,60},{64,6... | collective-permute-start | bytes 2359304 | tf_op jit(solution)/shard_map/cond/branch_1_fun/ppermute | solution.py:360
  10.4 8.2 %copy-start.11 = (bf16[512,1024]{1,0:T(8,128)(2,1)S(1)}, bf16[512,1024]{1,0:T(8,128)(2,1)}, u32[]{:S(2)}) copy-start(bf16[512,1024]{1,0:T(8,128)(2,1)} %get-tuple-element.107) | copy-start | bytes 3145732 | tf_op jit(solution)/shard_map/cond
  10.4 8.2 %copy-start.26 = (bf16[48,1024]{1,0:T(8,128)(2,1)S(1)}, bf16[48,1024]{1,0:T(8,128)(2,1)}, u32[]{:S(2)}) copy-start(bf16[48,1024]{1,0:T(8,128)(2,1)} %get-tuple-element.106) | copy-start | bytes 294916 | tf_op jit(solution)/shard_map/cond
  10.4 15.2 %collective-permute-start.3 = (bf16[1,2,512,128]{3,2,1,0:T(8,128)(2,1)S(1)}, bf16[1,2,512,128]{3,2,1,0:T(8,128)(2,1)S(1)}, u32[]{:S(2)}, u32[]{:S(2)}) collective-permute-start(bf16[1,2,512,128]{3,2,1,0:T(8,128)(2,1)S(1)} %get-tuple-element.99), channel_id=1, source_target_pairs={{4,8},{12,16},{20,24},{28,32},{36,40},{44,48},{52,56},{60,64},{68,... | collective-permute-start | bytes 786440 | tf_op jit(solution)/shard_map/cond/branch_1_fun/ppermute | solution.py:360
  36.1 10.6 %copy-start.32 = (bf16[3,16,512]{2,1,0:T(8,128)(2,1)S(1)}, bf16[3,16,512]{2,1,0:T(8,128)(2,1)}, u32[]{:S(2)}) copy-start(bf16[3,16,512]{2,1,0:T(8,128)(2,1)} %get-tuple-element.103.up_ref) | copy-start | bytes 147460 | tf_op jit(solution)/shard_map/cond
  36.1 10.5 %collective-permute-start.4 = (f32[3,8,512]{2,1,0:T(8,128)S(1)}, f32[3,8,512]{2,1,0:T(8,128)S(1)}, u32[]{:S(2)}, u32[]{:S(2)}) collective-permute-start(f32[3,8,512]{2,1,0:T(8,128)S(1)} %branch_1_fun.6.stats_ref), channel_id=1, source_target_pairs={{0,508},{8,4},{16,12},{24,20},{32,28},{40,36},{48,44},{56,52},{64,... | collective-permute-start | bytes 147464 | tf_op jit(solution)/shard_map/cond/branch_1_fun/ppermute | solution.py:375
  50.5 7.9 %copy-start.30 = (bf16[3,512,512]{2,1,0:T(8,128)(2,1)}, bf16[3,512,512]{2,1,0:T(8,128)(2,1)S(1)}, u32[]{:S(2)}) copy-start(bf16[3,512,512]{2,1,0:T(8,128)(2,1)S(1)} %get-tuple-element.151.qkv_ref) | copy-start | bytes 4718596

commit v3 on v2

--- a/solution.py
+++ b/solution.py
@@ -11,8 +11,9 @@
 HEAD = 128
 RANK = 16
 TILE = 256
-CTX = ("z", "x", "yh")
-NEAR = ("x", "yh")
+CTX = ("zh", "zl", "x", "yh")
+FAR = "zh"
+NEAR = ("zl", "x", "yh")
 F32 = jnp.float32
 BF16 = jnp.bfloat16
 VMEM_BYTES = 48 * 1024 * 1024
@@ -143,21 +144,12 @@
                 lax.fori_loop(0, count, functools.partial(step, ref), 0)
 
 
-def pack_kernel(wanted, role_ref, a_ref, b_ref, out_ref, order_ref):
-    list_heads(role_ref, order_ref, wanted)
-
-    def step(slot, _):
-        cols = columns_of(order_ref[slot])
-        out_ref[slot, 0] = a_ref[:, cols]
-        out_ref[slot, 1] = b_ref[:, cols]
-        return 0
-
-    lax.fori_loop(0, out_ref.shape[0], step, 0)
-
-
-def pack_pairs_kernel(flags, role_ref, q_ref, k_ref, v_ref, g_ref, *refs):
+def pack_kernel(plans, role_ref, q_ref, k_ref, v_ref, g_ref, *refs):
     *out_refs, order_ref = refs
     for wanted, sent in ((0, (k_ref, v_ref)), (1, (q_ref, g_ref))):
+        chosen = [(ref, plan[1]) for ref, plan in zip(out_refs, plans) if plan[0] in (wanted, None)]
+        if not chosen:
+            continue
         list_heads(role_ref, order_ref, wanted)
 
         def step(out_ref, slot, _):
@@ -166,7 +158,10 @@
             out_ref[slot, 1] = sent[1][:, cols]
             return 0
 
-        sides = [((wanted + flag) % 2, ref, ref.shape[0]) for flag, ref in zip(flags, out_refs)]
+        sides = []
+        for ref, parity in chosen:
+            swapped = parity is not None and wanted == 1
+            sides.append(((parity + 1) % 2 if swapped else parity, ref, ref.shape[0]))
         run_sides(role_ref, sides, step)
 
 
@@ -337,34 +332,52 @@
     def pair(number):
         return shape((number, 2, tok_rows, HEAD), BF16)
 
-    if plain == shifted:
-        pack = [SMEM, VMEM, VMEM]
-        kv = call(functools.partial(pack_kernel, 0), pair(slots), pack, 1000, heads)(role, keys, values)
-        kv = [lax.ppermute(kv, CTX, ahead)]
-        qg = call(functools.partial(pack_kernel, 1), pair(slots), pack, 1000, heads)(role, queries, grads)
-        qg = [lax.ppermute(qg, CTX, behind)]
-        kv_parities = qg_parities = [None]
-    else:
-        numbers = (plain, shifted)
-        flags = [flag for flag in range(2) if numbers[flag]]
-        packed = call(
-            functools.partial(pack_pairs_kernel, flags),
-            [pair(numbers[flag]) for flag in flags],
+    def packed(plans, numbers):
+        return call(
+            functools.partial(pack_kernel, plans),
+            [pair(number) for number in numbers],
             [SMEM] + [VMEM] * 4,
             1000,
             heads,
         )(role, queries, keys, values, grads)
-        moved = dict(zip(flags, packed))
-        for flag in sorted(flags, key=lambda flag: -numbers[flag]):
-            swap = ring(count, flag, 1) + ring(count, (flag + 1) % 2, -1)
-            moved[flag] = lax.ppermute(moved[flag], CTX, swap)
-        kv = qg = [moved[flag] for flag in flags]
+
+    def after(value, other):
+        return lax.optimization_barrier((value, other))[0]
+
+    def first_halves():
+        return call(
+            functools.partial(first_kernel, factor, scale), [low, full, full], [SMEM] + [VMEM] * 4, 6 * unit, heads
+        )(role, queries, keys, values, grads)
+
+    numbers = (plain, shifted)
+    flags = [flag for flag in range(2) if numbers[flag]]
+    if len(flags) == 1:
+        flag = flags[0]
+        swap = ring(count, flag, 1) + ring(count, (flag + 1) % 2, -1)
+        sent = packed([(None, flag)], [heads])[0]
+        kv = qg = [lax.ppermute(sent, CTX, swap)]
+        first = first_halves()
+        kv_parities, qg_parities = [(flag + 1) % 2], [flag]
+    elif plain == shifted:
+        sent = packed([(0, None), (1, None)], numbers)
+        kv = [lax.ppermute(sent[0], CTX, ahead)]
+        first = first_halves()
+        qg = [lax.ppermute(after(sent[1], first[0]), CTX, behind)]
+        kv_parities = qg_parities = [None]
+    else:
+        flags = sorted(flags, key=lambda flag: -numbers[flag])
+        sizes = [numbers[flag] for flag in flags]
+        sent = packed([(role_, flag) for role_ in range(2) for flag in flags], sizes * 2)
+        kv = [lax.ppermute(sent[at], CTX, ring(count, flag, 1)) for at, flag in enumerate(flags)]
+        first = first_halves()
+        late = lax.optimization_barrier((sent[2], sent[3], first[0]))
+        qg = [
+            lax.ppermute(late[at], CTX, ring(count, (flag + 1) % 2, -1))
+            for at, flag in enumerate(flags)
+        ]
         kv_parities = [(flag + 1) % 2 for flag in flags]
         qg_parities = flags
     low_rank = dot_nt(down_t, inputs).astype(BF16)
-    first = call(
-        functools.partial(first_kernel, factor, scale), [low, full, full], [SMEM] + [VMEM] * 4, 6 * unit, heads
-    )(role, queries, keys, values, grads)
     stats = call(
         functools.partial(stats_kernel, factor, kv_parities),
         shape((slots, 8, tok_rows), F32),
@@ -405,17 +418,17 @@
     )
     parts = lax.all_gather(parts, "head")
     rows = 3 * RANK * (width + queries.shape[1]) // HEAD
-    near = lax.axis_size(NEAR)
     grad = call(
         functools.partial(adapter_kernel, 1.0 / math.sqrt(seq_total)),
         shape((rows, HEAD), BF16),
         [VMEM] * 3,
         1 << 28,
     )(parts, inputs, qkv)
+    near = lax.axis_size(NEAR)
     grad = lax.all_to_all(grad.reshape(near, rows // near, HEAD), NEAR, 0, 0)
     grad = jnp.sum(grad.astype(F32), 0).astype(BF16)
-    far = lax.axis_size("z")
-    grad = lax.all_to_all(jnp.broadcast_to(grad, (far,) + grad.shape), "z", 0, 0)
+    far = lax.axis_size(FAR)
+    grad = lax.all_to_all(jnp.broadcast_to(grad, (far,) + grad.shape), FAR, 0, 0)
     grad = jnp.sum(grad.astype(F32), 0).astype(BF16)
     grad = lax.all_to_all(jnp.broadcast_to(grad, (near,) + grad.shape), NEAR, 0, 0)
     grad = grad.reshape(-1, 3, RANK, HEAD).astype(F32)
@@ -428,7 +441,7 @@
 def solution(mesh):
     count, columns = mesh.devices.shape
     across = 4 if count >= 128 else 2
-    fine = Mesh(mesh.devices.reshape(count // (2 * across), across, 2, columns), CTX + ("head",))
+    fine = Mesh(mesh.devices.reshape(-1, 2, across, 2, columns), CTX + ("head",))
     in_specs = (
         P(CTX, "head"),
         P(CTX, "head"),

time: 120 us -> 117 us (0.975)
  the two profiles are of different devices: /device:TPU:64 before, /device:TPU:8 now
where the time goes in v3:
time: 117 us; the launch traced here: 116 us
  blocking collectives  54.7 us (47%)
  starting transfers between devices  39.1 us (33%)
  Pallas kernels  14.3 us (12%)
  other arithmetic  2.1 us (2%)
  waiting for transfers between devices  2.04 us (2%)
  local copies, waits for them, and re-layouts  1.5 us (1%)
  between operations  1.34 us (1%)
    all_to_all x1, blocking collectives, local(): lax.all_to_all(jnp.broadcast_to(grad, (far,) + grad.shape), FAR, 0, 0)  22.4 us
    ppermute x2, starting transfers between devices, attention(): lax.ppermute(late[at], CTX, ring(count, (flag + 1) % 2, -1))  18.5 us
    ppermute x1, starting transfers between devices, attention(): moved = lax.ppermute(stats, CTX, behind)  14.9 us
    all_to_all x1, blocking collectives, local(): lax.all_to_all(jnp.broadcast_to(grad, (near,) + grad.shape), NEAR, 0, 0)  12.1 us
    all_to_all x1, blocking collectives, local(): grad = lax.all_to_all(grad.reshape(near, rows // near, HEAD), NEAR, 0, 0)  11.9 us
    all_gather x1, blocking collectives, local(): parts = lax.all_gather(parts, 'head')  8.27 us
    ppermute x2, starting transfers between devices, attention(): lax.ppermute(sent[at], CTX, ring(count, flag, 1))  5.67 us
    pallas_call x1, Pallas kernels, first_halves(): call(functools.partial(first_kernel, factor, scale), [low, full, full], [...  3.99 us
  transfers between devices with their start and end apart: 5, of which 1 were waited for; matrix products, arithmetic and copies ran while one was open for 0% of the time, Pallas kernels for 6%

profile of v3, /device:TPU:8, one launch (start us, length us, event | category | flops | bytes accessed | tf_op | source)
XLA Modules:
  0.0 116.2 jit_solution(11240518149674262662)
XLA Ops:
  0.6 1.3 %reduce_sum.33 = s32[]{:T(128)} reduce(s32[4]{0:T(128)} %param.20, s32[]{:T(128)} %constant.10.clone.1), dimensions={0}, to_apply=%region_0.0 | reduce | flops 3 | bytes 24 | tf_op jit(solution)/shard_map/reduce_sum | solution.py:415
  1.9 0.7 fusion
  3.3 54.9 %conditional.1 = (bf16[3,512,512]{2,1,0:T(8,128)(2,1)S(1)}, bf16[96,512]{1,0:T(8,128)(2,1)S(1)}) conditional(s32[]{:T(128)} %clamp.3, (s32[5]{0:T(128)S(1)}, bf16[512,512]{1,0:T(8,128)(2,1)}, bf16[512,512]{1,0:T(8,128)(2,1)}, bf16[512,512]{1,0:T(8,128)(2,1)}, bf16[512,512]{1,0:T(8,128)(2,1)}, ...), branch_computations={%region_1.0_spmd, %region_2.0_spmd, %region_3.0_spmd, %region_4.0_... | conditional | flops 5956133888 | bytes 44122524 | solution.py:414
  3.3 0.0 copy-start.1
  3.4 0.0 copy-start.6
  3.4 0.0 copy-start.16
  3.4 0.0 copy-start.21
  3.4 1.9 %branch_1_fun.5 = (bf16[3,2,512,128]{3,2,1,0:T(8,128)(2,1)S(1)}, bf16[1,2,512,128]{3,2,1,0:T(8,128)(2,1)S(1)}, bf16[3,2,512,128]{3,2,1,0:T(8,128)(2,1)S(1)}, bf16[1,2,512,128]{3,2,1,0:T(8,128)(2,1)S(1)}) custom-call(s32[5]{0:T(128)S(1)} %get-tuple-element.93.role_ref, bf16[512,512]{1,0:T(8,128)(2,1)} %get-tuple-element.96.q_ref, ...), custom_call_target="tpu_custom_call" | custom-call | flops 1000 | bytes 4194304 | tf_op jit(solution)/shard_map/cond/branch_1_fun/pallas_call | solution.py:336
  5.3 0.0 copy-start.11
  5.3 0.0 copy-start.26
  5.3 4.4 %collective-permute-start.2 = (bf16[3,2,512,128]{3,2,1,0:T(8,128)(2,1)S(1)}, bf16[3,2,512,128]{3,2,1,0:T(8,128)(2,1)S(1)}, u32[]{:S(2)}, u32[]{:S(2)}) collective-permute-start(bf16[3,2,512,128]{3,2,1,0:T(8,128)(2,1)S(1)} %get-tuple-element.98), channel_id=1, source_target_pairs={{0,4},{8,12},{16,20},{24,28},{32,36},{40,44},{48,52},{56,60},{64,6... | collective-permute-start | bytes 2359304 | tf_op jit(solution)/shard_map/cond/branch_1_fun/ppermute | solution.py:371
  9.8 4.0 %branch_1_fun.7 = (bf16[3,512,128]{2,1,0:T(8,128)(2,1)S(1)}, f32[3,512,128]{2,1,0:T(8,128)S(1)}, f32[3,512,128]{2,1,0:T(8,128)S(1)}) custom-call(s32[5]{0:T(128)S(1)} %get-tuple-element.93.role_ref, bf16[512,512]{1,0:T(8,128)(2,1)S(1)} %copy-done.16, bf16[512,512]{1,0:T(8,128)(2,1)S(1)} %copy-done.1, bf16[512,512]{1,0:T(8,128)(2,1)S(1)} %copy-done.6, ...), custom_call_target="tpu_custom_call" | custom-call | flops 1207959552 | bytes 4194304 | tf_op jit(solution)/shard_map/cond/branch_1_fun/pallas_call | solution.py:348
  13.8 1.3 %collective-permute-start.5 = (bf16[3,2,512,128]{3,2,1,0:T(8,128)(2,1)S(1)}, bf16[3,2,512,128]{3,2,1,0:T(8,128)(2,1)S(1)}, u32[]{:S(2)}, u32[]{:S(2)}) collective-permute-start(bf16[3,2,512,128]{3,2,1,0:T(8,128)(2,1)S(1)} %get-tuple-element.106), channel_id=1, source_target_pairs={{4,0},{12,8},{20,16},{28,24},{36,32},{44,40},{52,48},{60,56},{68,6... | collective-permute-start | bytes 2359304 | tf_op jit(solution)/shard_map/cond/branch_1_fun/ppermute | solution.py:375
  15.1 1.3 %collective-permute-start.3 = (bf16[1,2,512,128]{3,2,1,0:T(8,128)(2,1)S(1)}, bf16[1,2,512,128]{3,2,1,0:T(8,128)(2,1)S(1)}, u32[]{:S(2)}, u32[]{:S(2)}) collective-permute-start(bf16[1,2,512,128]{3,2,1,0:T(8,128)(2,1)S(1)} %get-tuple-element.99), channel_id=1, source_target_pairs={{4,8},{12,16},{20,24},{28,32},{36,40},{44,48},{52,56},{60,64},{68,... | collective-permute-start | bytes 786440 | tf_op jit(solution)/shard_map/cond/branch_1_fun/ppermute | solution.py:371
  16.4 17.2 %collective-permute-start.6 = (bf16[1,2,512,128]{3,2,1,0:T(8,128)(2,1)S(1)}, bf16[1,2,512,128]{3,2,1,0:T(8,128)(2,1)S(1)}, u32[]{:S(2)}, u32[]{:S(2)}) collective-permute-start(bf16[1,2,512,128]{3,2,1,0:T(8,128)(2,1)S(1)} %get-tuple-element.107), channel_id=1, source_target_pairs={{0,508},{8,4},{16,12},{24,20},{32,28},{40,36},{48,44},{56,52},{64,... | collective-permute-start | bytes 786440 | tf_op jit(solution)/shard_map/cond/branch_1_fun/ppermute | solution.py:375
  33.6 0.4 convolution_convert_fusion.1
  34.1 2.0 %collective-permute-done.3.refs_1_ = bf16[1,2,512,128]{3,2,1,0:T(8,128)(2,1)S(1)} collective-permute-done((bf16[1,2,512,128]{3,2,1,0:T(8,128)(2,1)S(1)}, bf16[1,2,512,128]{3,2,1,0:T(8,128)(2,1)S(1)}, u32[]{:S(2)}, u32[]{:S(2)}) %collective-permute-start.3) | collective-permute-done | bytes 262176 | tf_op jit(solution)/shard_map/cond/branch_1_fun/ppermute | solution.py:371
  36.1 1.4 %branch_1_fun.6.stats_ref = f32[3,8,512]{2,1,0:T(8,128)S(1)} custom-call(s32[5]{0:T(128)S(1)} %get-tuple-element.93.role_ref, bf16[512,512]{1,0:T(8,128)(2,1)S(1)} %copy-done.16, bf16[512,512]{1,0:T(8,128)(2,1)S(1)} %copy-done.1, bf16[512,512]{1,0:T(8,128)(2,1)S(1)} %copy-done.6, bf16[512,512]{1,0:T(8,128)(2,1)S(1)} %copy-done.21, ...), custom_call_target="tpu_custom_call" | custom-call | flops 805306368 | bytes 4194304 | tf_op jit(solution)/shard_map/cond/branch_1_fun/pallas_call | solution.py:381
  37.5 0.0 copy-start.32
  37.5 14.9 %collective-permute-start.4 = (f32[3,8,512]{2,1,0:T(8,128)S(1)}, f32[3,8,512]{2,1,0:T(8,128)S(1)}, u32[]{:S(2)}, u32[]{:S(2)}) collective-permute-start(f32[3,8,512]{2,1,0:T(8,128)S(1)} %branch_1_fun.6.stats_ref), channel_id=1, source_target_pairs={{0,508},{8,4},{16,12},{24,20},{32,28},{40,36},{48,44},{56,52},{64,... | collective-permute-start | bytes 147464 | tf_op jit(solution)/shard_map/cond/branch_1_fun/ppermute | solution.py:388
  52.4 1.9 %branch_1_fun.8.second_ref = bf16[3,3,512,128]{3,2,1,0:T(8,128)(2,1)S(1)} custom-call(s32[5]{0:T(128)S(1)} %get-tuple-element.93.role_ref, bf16[512,512]{1,0:T(8,128)(2,1)S(1)} %copy-done.16, bf16[512,512]{1,0:T(8,128)(2,1)S(1)} %copy-done.1, bf16[512,512]{1,0:T(8,128)(2,1)S(1)} %copy-done.6, bf16[512,512]{1,0:T(8,128)(2,1)S(1)} %copy-done.21, ...), custom_call_target="tpu_custom_call" | custom-call | flops 1610612736 | bytes 4194304 | tf_op jit(solution)/shard_map/cond/branch_1_fun/pallas_call | solution.py:389
  54.3 0.0 collective-permute-done.6.refs_1_
  54.3 0.0 collective-permute-done.5.refs_0_
  54.3 3.4 %branch_1_fun.9 = (bf16[3,512,512]{2,1,0:T(8,128)(2,1)S(1)}, bf16[48,512]{1,0:T(8,128)(2,1)S(1)}) custom-call(s32[5]{0:T(128)S(1)} %get-tuple-element.93.role_ref, bf16[512,512]{1,0:T(8,128)(2,1)S(1)} %copy-done.1, bf16[512,512]{1,0:T(8,128)(2,1)S(1)} %copy-done.6, f32[3,8,512]{2,1,0:T(8,128)S(1)} %collective-permute-done.4.stats_ref, ...), custom_call_target="tpu_custom_call" | custom-call | flops 805306368 | bytes 4194304 | tf_op jit(solution)/shard_map/cond/branch_1_fun/pallas_call | solution.py:396
  58.2 0.0 copy-start.30
  58.2 8.3 %all-gather = bf16[384,512]{1,0:T(8,128)(2,1)S(1)} all-gather(bf16[96,512]{1,0:T(8,128)(2,1)S(1)} %get-tuple-element.166), channel_id=2, replica_groups=mesh['zh'=8,'zl'=2,'x'=4,'yh'=2,'head'=4] {'head'}, dimensions={0}, use_global_device_ids=true | all-gather | bytes 491520 | tf_op jit(solution)/shard_map/all_gather | solution.py:419
  66.5 1.7 %shard_map.103 = bf16[576,128]{1,0:T(8,128)(2,1)S(1)} custom-call(bf16[4,96,512]{2,1,0:T(8,128)(2,1)S(1)} %bitcast.26, bf16[512,1024]{1,0:T(8,128)(2,1)} %inputs_ref.1, bf16[3,512,512]{2,1,0:T(8,128)(2,1)S(1)} %get-tuple-element.162.qkv_ref), custom_call_target="tpu_custom_call" | custom-call | flops 268435456 | bytes 4194304 | tf_op jit(solution)/shard_map/pallas_call | solution.py:421
  68.2 11.9 %all_to_all.15 = bf16[16,36,128]{2,1,0:T(8,128)(2,1)S(1)} all-to-all(bf16[16,36,128]{2,1,0:T(8,128)(2,1)S(1)} %reshape.22), channel_id=1, replica_groups=mesh['zh'=8,'zl'=2,'x'=4,'yh'=2,'head'=4] {'zl','x','yh'}, dimensions={0} | all-to-all | bytes 294912 | tf_op jit(solution)/shard_map/all_to_all | solution.py:428
  80.2 22.4 %all_to_all.16 = bf16[8,36,128]{2,1,0:T(8,128)(2,1)S(1)} all-to-all(bf16[8,36,128]{2,1,0:T(8,128)(2,1)S(1)} %broadcast_in_dim.6), channel_id=1, replica_groups=mesh['zh'=8,'zl'=2,'x'=4,'yh'=2,'head'=4] {'zh'}, dimensions={0} | all-to-all | bytes 147456 | tf_op jit(solution)/shard_map/all_to_all | solution.py:431
  102.7 12.1 %all_to_all.17 = bf16[16,36,128]{2,1,0:T(8,128)(2,1)S(1)} all-to-all(bf16[16,36,128]{2,1,0:T(8,128)(2,1)S(1)} %broadcast_in_dim.7), channel_id=1, replica_groups=mesh['zh'=8,'zl'=2,'x'=4,'yh'=2,'head'=4] {'zl','x','yh'}, dimensions={0} | all-to-all | bytes 294912 | tf_op jit(solution)/shard_map/all_to_all | solution.py:433
  114.8 0.7 copy_bitcast_fusion
  115.5 0.6 copy_bitcast_fusion.1
  (17 shorter events, 0.2 us)
Async XLA Ops:
  3.3 6.4 %copy-start.1 = (bf16[512,512]{1,0:T(8,128)(2,1)S(1)}, bf16[512,512]{1,0:T(8,128)(2,1)}, u32[]{:S(2)}) copy-start(bf16[512,512]{1,0:T(8,128)(2,1)} %get-tuple-element.94.k_ref) | copy-start | bytes 1572868 | tf_op jit(solution)/shard_map/cond
  3.4 6.4 %copy-start.6 = (bf16[512,512]{1,0:T(8,128)(2,1)S(1)}, bf16[512,512]{1,0:T(8,128)(2,1)}, u32[]{:S(2)}) copy-start(bf16[512,512]{1,0:T(8,128)(2,1)} %get-tuple-element.95.v_ref) | copy-start | bytes 1572868 | tf_op jit(solution)/shard_map/cond
  3.4 6.4 %copy-start.16 = (bf16[512,512]{1,0:T(8,128)(2,1)S(1)}, bf16[512,512]{1,0:T(8,128)(2,1)}, u32[]{:S(2)}) copy-start(bf16[512,512]{1,0:T(8,128)(2,1)} %get-tuple-element.96.q_ref) | copy-start | bytes 1572868 | tf_op jit(solution)/shard_map/cond
  3.4 6.4 %copy-start.21 = (bf16[512,512]{1,0:T(8,128)(2,1)S(1)}, bf16[512,512]{1,0:T(8,128)(2,1)}, u32[]{:S(2)}) copy-start(bf16[512,512]{1,0:T(8,128)(2,1)} %get-tuple-element.97.g_ref) | copy-start | bytes 1572868 | tf_op jit(solution)/shard_map/cond
  5.3 28.3 %copy-start.11 = (bf16[512,1024]{1,0:T(8,128)(2,1)S(1)}, bf16[512,1024]{1,0:T(8,128)(2,1)}, u32[]{:S(2)}) copy-start(bf16[512,1024]{1,0:T(8,128)(2,1)} %get-tuple-element.111) | copy-start | bytes 3145732 | tf_op jit(solution)/shard_map/cond
  5.3 28.3 %copy-start.26 = (bf16[48,1024]{1,0:T(8,128)(2,1)S(1)}, bf16[48,1024]{1,0:T(8,128)(2,1)}, u32[]{:S(2)}) copy-start(bf16[48,1024]{1,0:T(8,128)(2,1)} %get-tuple-element.110) | copy-start | bytes 294916 | tf_op jit(solution)/shard_map/cond
  5.3 30.8 %collective-permute-start.2 = (bf16[3,2,512,128]{3,2,1,0:T(8,128)(2,1)S(1)}, bf16[3,2,512,128]{3,2,1,0:T(8,128)(2,1)S(1)}, u32[]{:S(2)}, u32[]{:S(2)}) collective-permute-start(bf16[3,2,512,128]{3,2,1,0:T(8,128)(2,1)S(1)} %get-tuple-element.98), channel_id=1, source_target_pairs={{0,4},{8,12},{16,20},{24,28},{32,36},{40,44},{48,52},{56,60},{64,6... | collective-permute-start | bytes 2359304 | tf_op jit(solution)/shard_map/cond/branch_1_fun/ppermute | solution.py:371
  13.8 40.5 %collective-permute-start.5 = (bf16[3,2,512,128]{3,2,1,0:T(8,128)(2,1)S(1)}, bf16[3,2,512,128]{3,2,1,0:T(8,128)(2,1)S(1)}, u32[]{:S(2)}, u32[]{:S(2)}) collective-permute-start(bf16[3,2,512,128]{3,2,1,0:T(8,128)(2,1)S(1)} %get-tuple-element.106), channel_id=1, source_target_pairs={{4,0},{12,8},{20,16},{28,24},{36,32},{44,40},{52,48},{60,56},{68,6... | collective-permute-start | bytes 2359304 | tf_op jit(solution)/shard_map/cond/branch_1_fun/ppermute | solution.py:375
  15.1 21.0 %collective-permute-start.3 = (bf16[1,2,512,128]{3,2,1,0:T(8,128)(2,1)S(1)}, bf16[1,2,512,128]{3,2,1,0:T(8,128)(2,1)S(1)}, u32[]{:S(2)}, u32[]{:S(2)}) collective-permute-start(bf16[1,2,512,128]{3,2,1,0:T(8,128)(2,1)S(1)} %get-tuple-element.99), channel_id=1, source_target_pairs={{4,8},{12,16},{20,24},{28,32},{36,40},{44,48},{52,56},{60,64},{68,... | collective-permute-start | bytes 786440 | tf_op jit(solution)/shard_map/cond/branch_1_fun/ppermute | solution.py:371
  16.4 37.9 %collective-permute-start.6 = (bf16[1,2,512,128]{3,2,1,0:T(8,128)(2,1)S(1)}, bf16[1,2,512,128]{3,2,1,0:T(8,128)(2,1)S(1)}, u32[]{:S(2)}, u32[]{:S(2)}) collective-permute-start(bf16[1,2,512,128]{3,2,1,0:T(8,128)(2,1)S(1)} %get-tuple-element.107), channel_id=1, source_target_pairs={{0,508},{8,4},{16,12},{24,20},{32,28},{40,36},{48,44},{56,52},{64,... | collective-permute-start | bytes 786440 | tf_op jit(solution)/shard_map/cond/branch_1_fun/ppermute | solution.py:375
  37.5 16.8 %copy-start.32 = (bf16[3,16,512]{2,1,0:T(8,128)(2,1)S(1)}, bf16[3,16,512]{2,1,0:T(8,128)(2,1)}, u32[]{:S(2)}) copy-start(bf16[3,16,512]{2,1,0:T(8,128)(2,1)} %get-tuple-element.103.up_ref) | copy-start | bytes 147460 | tf_op jit(solution)/shard_map/cond
  37.5 16.8 %collective-permute-start.4 = (f32[3,8,512]{2,1,0:T(8,128)S(1)}, f32[3,8,512]{2,1,0:T(8,128)S(1)}, u32[]{:S(2)}, u32[]{:S(2)}) collective-permute-start(f32[3,8,512]{2,1,0:T(8,128)S(1)} %branch_1_fun.6.stats_ref), channel_id=1, source_target_pairs={{0,508},{8,4},{16,12},{24,20},{32,28},{40,36},{48,44},{56,52},{64,... | collective-permute-start | bytes 147464 | tf_op jit(solution)/shard_map/cond/branch_1_fun/ppermute | solution.py:388
  58.2 8.3 %copy-start.30 = (bf16[3,512,512]{2,1,0:T(8,128)(2,1)}, bf16[3,512,512]{2,1,0:T(8,128)(2,1)S(1)}, u32[]{:S(2)}) copy-start(bf16[3,512,512]{2,1,0:T(8,128)(2,1)S(1)} %get-tuple-element.162.qkv_ref) | copy-start | bytes 4718596

commit v4 on v3

v4 whole, which is shorter than its diff:
```python
import functools
import math

import jax
import jax.numpy as jnp
from jax import lax
from jax.experimental import pallas as pl
from jax.experimental.pallas import tpu as pltpu
from jax.sharding import Mesh, PartitionSpec as P

HEAD = 128
RANK = 16
TILE = 256
CTX = ("zh", "zl", "x", "yh")
FAR = "zh"
NEAR = ("zl", "x", "yh")
F32 = jnp.float32
BF16 = jnp.bfloat16
VMEM_BYTES = 48 * 1024 * 1024


def dot_nt(left, right):
    return lax.dot_general(left, right, (((1,), (1,)), ((), ())), preferred_element_type=F32)


def dot_tn(left, right):
    return lax.dot_general(left, right, (((0,), (0,)), ((), ())), preferred_element_type=F32)


def dot_nn(left, right):
    return lax.dot_general(left, right, (((1,), (0,)), ((), ())), preferred_element_type=F32)


def list_heads(role_ref, order_ref, wanted):
    count = jnp.int32(0)
    for head in range(role_ref.shape[0] - 1):
        chosen = role_ref[head] == wanted

        @pl.when(chosen)
        def _():
            order_ref[count] = head

        count = count + chosen.astype(jnp.int32)
    return count


def columns_of(head):
    return pl.ds(pl.multiple_of(head * HEAD, HEAD), HEAD)


def causal_mask(rows):
    keys = lax.broadcasted_iota(jnp.int32, (rows, rows), 0)
    queries = lax.broadcasted_iota(jnp.int32, (rows, rows), 1)
    return keys <= queries


def row_stats(scores, dprobs, factor):
    top = functools.reduce(jnp.maximum, [jnp.max(s, axis=0, keepdims=True) for s in scores])
    exponents = [jnp.exp2((s - top) * factor) for s in scores]
    total = sum(jnp.sum(e, axis=0, keepdims=True) for e in exponents)
    mixed = sum(jnp.sum(e * d, axis=0, keepdims=True) for e, d in zip(exponents, dprobs))
    return exponents, (top, total, mixed)


def merge_stats(one, other, factor):
    top = jnp.maximum(one[0], other[0])
    weights = [jnp.exp2((stats[0] - top) * factor) for stats in (one, other)]
    total = one[1] * weights[0] + other[1] * weights[1]
    mixed = one[2] * weights[0] + other[2] * weights[1]
    return top, total, mixed


def low_parts(probs, dprobs, delta):
    return probs.astype(BF16), (probs * (dprobs - delta)).astype(BF16)


class Tile:
    def __init__(self, queries, grads, index, factor):
        cut = slice(index * TILE, (index + 1) * TILE)
        self.queries, self.grads = queries[cut], grads[cut]
        self.index, self.factor = index, factor

    def products(self, pair, start, rows, masked):
        scores = dot_nt(pair[0][start : start + rows], self.queries)
        if masked:
            scores = jnp.where(causal_mask(TILE), scores, -jnp.inf)
        return scores, dot_nt(pair[1][start : start + rows], self.grads)

    def own_pieces(self):
        before = [(0, self.index * TILE, False)] if self.index else []
        return before + [(self.index * TILE, TILE, True)]

    def own_stats(self, own):
        products = [self.products(own, *piece) for piece in self.own_pieces()]
        exponents, stats = row_stats(*zip(*products), self.factor)
        return exponents, [dprobs for _, dprobs in products], stats

    def full_block(self, pair, own_stats):
        scores, dprobs = self.products(pair, 0, pair[0].shape[0], False)
        (exponent,), stats = row_stats([scores], [dprobs], self.factor)
        top, total, mixed = merge_stats(stats, own_stats, self.factor)
        inverse = 1.0 / total
        delta = mixed * inverse
        probs = exponent * (jnp.exp2((stats[0] - top) * self.factor) * inverse)
        return low_parts(probs, dprobs, delta), (top, inverse, delta)


class Sums:
    def __init__(self):
        self.parts = {}

    def add(self, start, value):
        for at in range(0, value.shape[0], TILE):
            part = value[at : at + TILE]
            held = self.parts.get(start + at)
            self.parts[start + at] = part if held is None else held + part

    def whole(self):
        return jnp.concatenate([self.parts[at] for at in sorted(self.parts)], 0)


def plan_kernel(flags_ref, role_ref, shifted_ref):
    parity = lax.axis_index("yh")
    total = jnp.int32(0)
    for head in range(flags_ref.shape[0]):
        role_ref[head] = (flags_ref[head] + parity) & 1
        total = total + flags_ref[head]
    role_ref[flags_ref.shape[0]] = parity
    shifted_ref[0] = total


def run_sides(role_ref, sides, step):
    for parity, ref, count in sides:
        if parity is None:
            lax.fori_loop(0, count, functools.partial(step, ref), 0)
        else:

            @pl.when(role_ref[role_ref.shape[0] - 1] == parity)
            def _():
                lax.fori_loop(0, count, functools.partial(step, ref), 0)


def pack_kernel(plans, role_ref, q_ref, k_ref, v_ref, g_ref, *refs):
    *out_refs, order_ref = refs
    for wanted, sent in ((0, (k_ref, v_ref)), (1, (q_ref, g_ref))):
        chosen = [(ref, plan[1]) for ref, plan in zip(out_refs, plans) if plan[0] in (wanted, None)]
        if not chosen:
            continue
        list_heads(role_ref, order_ref, wanted)

        def step(out_ref, slot, _):
            cols = columns_of(order_ref[slot])
            out_ref[slot, 0] = sent[0][:, cols]
            out_ref[slot, 1] = sent[1][:, cols]
            return 0

        sides = []
        for ref, parity in chosen:
            swapped = parity is not None and wanted == 1
            sides.append(((parity + 1) % 2 if swapped else parity, ref, ref.shape[0]))
        run_sides(role_ref, sides, step)


def early_kernel(factor, scale, role_ref, q_ref, k_ref, v_ref, g_ref, dq_ref, dk_ref, dv_ref, stats_ref, order_ref):
    tiles = range(q_ref.shape[0] // TILE)
    count = list_heads(role_ref, order_ref, 1)

    def rows(slot, _):
        cols = columns_of(order_ref[slot])
        own = (k_ref[:, cols], v_ref[:, cols])
        for index in tiles:
            tile = Tile(q_ref[:, cols], g_ref[:, cols], index, factor)
            _, _, stats = tile.own_stats(own)
            for row in range(3):
                stats_ref[slot, row : row + 1, index * TILE : (index + 1) * TILE] = stats[row]
        return 0

    lax.fori_loop(0, count, rows, 0)
    count = list_heads(role_ref, order_ref, 0)

    def step(slot, _):
        cols = columns_of(order_ref[slot])
        own = (k_ref[:, cols], v_ref[:, cols])
        key_sums, value_sums = Sums(), Sums()
        for index in tiles:
            tile = Tile(q_ref[:, cols], g_ref[:, cols], index, factor)
            exponents, dprobs, (_, total, mixed) = tile.own_stats(own)
            inverse = 1.0 / total
            query_t = 0.0
            for (start, length, _), e, d in zip(tile.own_pieces(), exponents, dprobs):
                probs, dscores = low_parts(e * inverse, d, mixed * inverse)
                query_t = query_t + dot_tn(own[0][start : start + length], dscores)
                key_sums.add(start, dot_nn(dscores, tile.queries))
                value_sums.add(start, dot_nn(probs, tile.grads))
            dq_ref[slot, index * TILE : (index + 1) * TILE] = (query_t.T * scale).astype(BF16)
        dk_ref[slot] = key_sums.whole()
        dv_ref[slot] = value_sums.whole()
        return 0

    lax.fori_loop(0, count, step, 0)


def side_refs(refs, parities):
    return [(parity, ref, ref.shape[0]) for parity, ref in zip(parities, refs)]


def tile_stats(stats_ref, slot, index):
    return tuple(
        stats_ref[slot, row : row + 1, index * TILE : (index + 1) * TILE] for row in range(3)
    )


def late_kernel(
    factor, scale, kv_parities, qg_parities, role_ref, q_ref, k_ref, v_ref, g_ref, stats_ref,
    moved_ref, dq_ref, dk_ref, dv_ref, up_ref, *refs
):
    *other_refs, out_ref, back_ref, order_ref = refs
    kv_refs, qg_refs = other_refs[: len(kv_parities)], other_refs[-len(qg_parities) :]
    tiles = range(q_ref.shape[0] // TILE)
    list_heads(role_ref, order_ref, 1)

    def second(kv_ref, slot, _):
        cols = columns_of(order_ref[slot])
        own = (k_ref[:, cols], v_ref[:, cols])
        before = (kv_ref[slot, 0], kv_ref[slot, 1])
        key_sums, value_sums = Sums(), Sums()
        for index in tiles:
            tile = Tile(q_ref[:, cols], g_ref[:, cols], index, factor)
            (_, dscores), (top, inverse, delta) = tile.full_block(
                before, tile_stats(stats_ref, slot, index)
            )
            query_t = dot_tn(before[0], dscores)
            for piece in tile.own_pieces():
                start, length, _ = piece
                scores, dprobs = tile.products(own, *piece)
                probs, dscores = low_parts(
                    jnp.exp2((scores - top) * factor) * inverse, dprobs, delta
                )
                query_t = query_t + dot_tn(own[0][start : start + length], dscores)
                key_sums.add(start, dot_nn(dscores, tile.queries))
                value_sums.add(start, dot_nn(probs, tile.grads))
            out_ref[0, index * TILE : (index + 1) * TILE, cols] = (query_t.T * scale).astype(BF16)
        out_ref[1, :, cols] = (key_sums.whole() * scale).astype(BF16)
        out_ref[2, :, cols] = value_sums.whole().astype(BF16)
        return 0

    run_sides(role_ref, side_refs(kv_refs, kv_parities), second)
    list_heads(role_ref, order_ref, 0)

    def first(qg_ref, slot, _):
        cols = columns_of(order_ref[slot])
        own = (k_ref[:, cols], v_ref[:, cols])
        dk, dv = dk_ref[slot], dv_ref[slot]
        for index in tiles:
            tile = Tile(qg_ref[slot, 0], qg_ref[slot, 1], index, factor)
            (probs, dscores), _ = tile.full_block(own, tile_stats(moved_ref, slot, index))
            dk = dk + dot_nn(dscores, tile.queries)
            dv = dv + dot_nn(probs, tile.grads)
        out_ref[0, :, cols] = dq_ref[slot]
        out_ref[1, :, cols] = (dk * scale).astype(BF16)
        out_ref[2, :, cols] = dv.astype(BF16)
        return 0

    run_sides(role_ref, side_refs(qg_refs, qg_parities), first)
    for index in range(3):
        back_ref[index * RANK : (index + 1) * RANK] = dot_nt(up_ref[index], out_ref[index]).astype(BF16)


def adapter_kernel(norm_factor, parts_ref, inputs_ref, qkv_ref, out_ref):
    summed = functools.reduce(
        jnp.add, [parts_ref[index].astype(F32) for index in range(parts_ref.shape[0])]
    ).astype(BF16)
    rows = 3 * RANK
    down = dot_nn(summed[:rows], inputs_ref[...]) * norm_factor
    up = jnp.concatenate(
        [
            dot_nn(summed[rows + index * RANK : rows + (index + 1) * RANK], qkv_ref[index])
            for index in range(3)
        ],
        0,
    ) * norm_factor
    place = 0
    for total in (down, up):
        for start in range(0, total.shape[1], HEAD):
            out_ref[place : place + rows] = total[:, start : start + HEAD].astype(BF16)
            place += rows


def finish_kernel(sums_ref, *out_refs):
    place = 0
    for out_ref in out_refs:
        for start in range(0, out_ref.shape[1], HEAD):
            rows = out_ref.shape[0]
            out_ref[:, start : start + HEAD] = sums_ref[place : place + rows].astype(F32)
            place += rows


VMEM = pl.BlockSpec(memory_space=pltpu.VMEM)
SMEM = pl.BlockSpec(memory_space=pltpu.SMEM)


def call(kernel, outs, in_specs, flops, heads=0):
    many = isinstance(outs, (list, tuple))
    return pl.pallas_call(
        kernel,
        out_shape=outs,
        in_specs=in_specs,
        out_specs=[VMEM] * len(outs) if many else VMEM,
        scratch_shapes=[pltpu.SMEM((heads,), jnp.int32)] if heads else [],
        compiler_params=pltpu.CompilerParams(vmem_limit_bytes=VMEM_BYTES),
        cost_estimate=pl.CostEstimate(flops=flops, bytes_accessed=flops >> 8, transcendentals=0),
    )


def shape(dims, dtype):
    return jax.ShapeDtypeStruct(dims, dtype)


def ring(count, parity, step):
    return [(source, (source + step) % count) for source in range(parity, count, 2)]


def attention(shifted, role, queries, keys, values, grads, inputs, down_t, up):
    tok_rows = queries.shape[0]
    heads = role.shape[0] - 1
    plain = heads - shifted
    slots = max(plain, shifted)
    scale = 1.0 / math.sqrt(HEAD)
    factor = scale * math.log2(math.e)
    count = lax.axis_size(CTX)
    ahead = ring(count, 0, 1) + ring(count, 1, 1)
    behind = ring(count, 0, -1) + ring(count, 1, -1)
    low = shape((slots, tok_rows, HEAD), BF16)
    full = shape((slots, tok_rows, HEAD), F32)
    unit = 2 * tok_rows * tok_rows * HEAD * slots

    def pair(number):
        return shape((number, 2, tok_rows, HEAD), BF16)

    def packed(plans, numbers):
        return call(
            functools.partial(pack_kernel, plans),
            [pair(number) for number in numbers],
            [SMEM] + [VMEM] * 4,
            1000,
            heads,
        )(role, queries, keys, values, grads)

    *first, stats = call(
        functools.partial(early_kernel, factor, scale),
        [low, full, full, shape((slots, 8, tok_rows), F32)],
        [SMEM] + [VMEM] * 4,
        1,
        heads,
    )(role, queries, keys, values, grads)

    stats, moved = lax.optimization_barrier((stats, lax.ppermute(stats, CTX, behind)))

    numbers = (plain, shifted)
    flags = [flag for flag in range(2) if numbers[flag]]
    if plain == shifted:
        sent = packed([(0, None)], [slots])[0]
        kv = [lax.ppermute(sent, CTX, ahead)]
        sent = packed([(1, None)], [slots])[0]
        qg = [lax.ppermute(sent, CTX, behind)]
        kv_parities = qg_parities = [None]
    else:
        flags = sorted(flags, key=lambda flag: -numbers[flag])
        sent = packed([(None, flag) for flag in flags], [numbers[flag] for flag in flags])
        kv = qg = [
            lax.ppermute(sent[at], CTX, ring(count, flag, 1) + ring(count, (flag + 1) % 2, -1))
            for at, flag in enumerate(flags)
        ]
        kv_parities = [(flag + 1) % 2 for flag in flags]
        qg_parities = flags
    low_rank = dot_nt(down_t, inputs).astype(BF16)
    arrived = kv if kv is qg else kv + qg
    qkv, back = call(
        functools.partial(late_kernel, factor, scale, kv_parities, qg_parities),
        [shape((3,) + queries.shape, BF16), shape((3 * RANK, tok_rows), BF16)],
        [SMEM] + [VMEM] * (10 + len(arrived)),
        12 * unit,
        heads,
    )(role, queries, keys, values, grads, stats, moved, *first, up, *arrived)
    return qkv, jnp.concatenate([back, low_rank], 0)


def local(inputs, queries, keys, values, grads, down, up, flags):
    tok_rows = queries.shape[0]
    heads = flags.shape[0]
    width = inputs.shape[1]
    seq_total = lax.axis_size(CTX) * tok_rows
    role, shifted = pl.pallas_call(
        plan_kernel,
        out_shape=[shape((heads + 1,), jnp.int32), shape((1,), jnp.int32)],
        in_specs=[SMEM],
        out_specs=[SMEM, SMEM],
    )(flags)
    down_t = down.transpose(0, 2, 1).reshape(3 * RANK, width)
    qkv, parts = lax.switch(
        shifted.reshape(()),
        [functools.partial(attention, number) for number in range(heads + 1)],
        role, queries, keys, values, grads, inputs, down_t, up,
    )
    parts = lax.all_gather(parts, "head")
    rows = 3 * RANK * (width + queries.shape[1]) // HEAD
    grad = call(
        functools.partial(adapter_kernel, 1.0 / math.sqrt(seq_total)),
        shape((rows, HEAD), BF16),
        [VMEM] * 3,
        1 << 28,
    )(parts, inputs, qkv)
    near = lax.axis_size(NEAR)
    grad = lax.all_to_all(grad.reshape(near, rows // near, HEAD), NEAR, 0, 0)
    grad = jnp.sum(grad.astype(F32), 0).astype(BF16)
    far = lax.axis_size(FAR)
    grad = lax.all_to_all(jnp.broadcast_to(grad, (far,) + grad.shape), FAR, 0, 0)
    grad = jnp.sum(grad.astype(F32), 0).astype(BF16)
    grad = lax.all_to_all(jnp.broadcast_to(grad, (near,) + grad.shape), NEAR, 0, 0)
    grad_down, grad_up = call(
        finish_kernel,
        [shape((3 * RANK, width), F32), shape((3 * RANK, queries.shape[1]), F32)],
        [VMEM],
        1,
    )(grad.reshape(rows, HEAD))
    grad_down = grad_down.reshape(3, RANK, width).transpose(0, 2, 1)
    grad_up = grad_up.reshape(3, RANK, -1)
    return qkv, grad_down, grad_up


def solution(mesh):
    count, columns = mesh.devices.shape
    across = 4 if count >= 128 else 2
    fine = Mesh(mesh.devices.reshape(-1, 2, across, 2, columns), CTX + ("head",))
    in_specs = (
        P(CTX, "head"),
        P(CTX, "head"),
        P(CTX, "head"),
        P(CTX, "head"),
        P(CTX, "head"),
        P(None, "head", None),
        P(None, None, "head"),
        P("head"),
    )
    out_specs = (P(None, CTX, "head"), P(None, "head", None), P(None, None, "head"))
    return jax.shard_map(local, mesh=fine, in_specs=in_specs, out_specs=out_specs, check_vma=False)
```

time: 117 us -> 107 us (0.915)
  the two profiles are of different devices: /device:TPU:8 before, /device:TPU:2 now
where the time goes in v4:
time: 107 us
  blocking collectives  61.9 us (58%)
  Pallas kernels  17.3 us (16%)
  starting transfers between devices  14.7 us (14%)
  waiting for transfers between devices  10.2 us (10%)
  between operations  1.33 us (1%)
    all_to_all x1, blocking collectives, local(): lax.all_to_all(jnp.broadcast_to(grad, (far,) + grad.shape), FAR, 0, 0)  26.8 us
    all_to_all x1, blocking collectives, local(): grad = lax.all_to_all(grad.reshape(near, rows // near, HEAD), NEAR, 0, 0)  14 us
    all_to_all x1, blocking collectives, local(): lax.all_to_all(jnp.broadcast_to(grad, (near,) + grad.shape), NEAR, 0, 0)  12 us
    ppermute x1, waiting for transfers between devices, attention(): lax.ppermute(stats, CTX, behind)  10.2 us
    all_gather x1, blocking collectives, local(): parts = lax.all_gather(parts, 'head')  9.06 us
    pallas_call x1, Pallas kernels, attention(): call(functools.partial(late_kernel, factor, scale, kv_parities, qg_pariti...  7.4 us
    ppermute x1, starting transfers between devices, attention(): lax.ppermute(stats, CTX, behind)  6.37 us
    ppermute x1, starting transfers between devices, attention(): kv = [lax.ppermute(sent, CTX, ahead)]  5.1 us
  transfers between devices with their start and end apart: 3, of which 1 were waited for; matrix products, arithmetic and copies ran while one was open for 0% of the time, Pallas kernels for 4%

profile of v4, /device:TPU:2, one launch (start us, length us, event | category | flops | bytes accessed | tf_op | source)
XLA Modules:
  0.0 106.8 jit_solution(13670101376386184753)
XLA Ops:
  0.6 1.3 %shard_map.103 = (s32[5]{0:T(128)S(1)}, s32[1]{0:T(128)}) custom-call(s32[4]{0:T(128)} %flags_ref.1), custom_call_target="tpu_custom_call" | custom-call | tf_op jit(solution)/shard_map/pallas_call | solution.py:393
  2.6 39.7 %conditional.1 = (bf16[3,512,512]{2,1,0:T(8,128)(2,1)S(1)}, bf16[96,512]{1,0:T(8,128)(2,1)S(1)}) conditional(s32[]{:T(128)} %bitcast, (s32[5]{0:T(128)S(1)}, bf16[512,512]{1,0:T(8,128)(2,1)}, bf16[512,512]{1,0:T(8,128)(2,1)}, bf16[512,512]{1,0:T(8,128)(2,1)}, bf16[512,512]{1,0:T(8,128)(2,1)}, ...), branch_computations={%region_0.0_spmd, %region_1.0_spmd, %region_2.0_spmd, %region_3.0_... | conditional | flops 3271779328 | bytes 31605032 | solution.py:400
  2.8 0.0 copy-start.2
  2.8 0.0 copy-start.7
  2.8 0.0 copy-start.12
  2.8 0.0 copy-start.17
  2.9 1.8 %branch_2_fun.5 = bf16[2,2,512,128]{3,2,1,0:T(8,128)(2,1)S(1)} custom-call(s32[5]{0:T(128)S(1)} %get-tuple-element.114.role_ref, bf16[512,512]{1,0:T(8,128)(2,1)} %get-tuple-element.115.q_ref, bf16[512,512]{1,0:T(8,128)(2,1)} %get-tuple-element.116.k_ref, bf16[512,512]{1,0:T(8,128)(2,1)} %get-tuple-element.117.v_ref, bf16[512,512]{1,0:T(8,128)(2,1)} %get-tuple-element.118.g_ref), custom_call_target="tpu_custom_call" | custom-call | flops 1000 | bytes 3 | tf_op jit(solution)/shard_map/cond/branch_2_fun/pallas_call | solution.py:341
  4.6 5.1 %collective-permute-start.6 = (bf16[2,2,512,128]{3,2,1,0:T(8,128)(2,1)S(1)}, bf16[2,2,512,128]{3,2,1,0:T(8,128)(2,1)S(1)}, u32[]{:S(2)}, u32[]{:S(2)}) collective-permute-start(bf16[2,2,512,128]{3,2,1,0:T(8,128)(2,1)S(1)} %branch_2_fun.5), channel_id=1, source_target_pairs={{0,4},{8,12},{16,20},{24,28},{32,36},{40,44},{48,52},{56,60},{64,6... | collective-permute-start | bytes 1572872 | tf_op jit(solution)/shard_map/cond/branch_2_fun/ppermute | solution.py:363
  9.8 0.0 copy-done.2
  9.8 0.0 copy-done.7
  9.8 0.0 copy-done.12
  9.8 0.0 copy-done.17
  9.8 0.7 branch_2_fun.6
  10.5 0.0 copy-start.22
  10.5 0.0 copy-start.27
  10.5 0.0 copy-start.33
  10.5 3.3 %collective-permute-start.7 = (bf16[2,2,512,128]{3,2,1,0:T(8,128)(2,1)S(1)}, bf16[2,2,512,128]{3,2,1,0:T(8,128)(2,1)S(1)}, u32[]{:S(2)}, u32[]{:S(2)}) collective-permute-start(bf16[2,2,512,128]{3,2,1,0:T(8,128)(2,1)S(1)} %branch_2_fun.6), channel_id=1, source_target_pairs={{0,508},{8,4},{16,12},{24,20},{32,28},{40,36},{48,44},{56,52},{64,... | collective-permute-start | bytes 1572872 | tf_op jit(solution)/shard_map/cond/branch_2_fun/ppermute | solution.py:365
  13.8 3.7 %branch_2_fun.4 = (bf16[2,512,128]{2,1,0:T(8,128)(2,1)S(1)}, f32[2,512,128]{2,1,0:T(8,128)S(1)}, f32[2,512,128]{2,1,0:T(8,128)S(1)}, f32[2,8,512]{2,1,0:T(8,128)S(1)}) custom-call(s32[5]{0:T(128)S(1)} %get-tuple-element.114.role_ref, bf16[512,512]{1,0:T(8,128)(2,1)S(1)} %copy-done.2, bf16[512,512]{1,0:T(8,128)(2,1)S(1)} %copy-done.7, ...), custom_call_target="tpu_custom_call" | custom-call | flops 1 | tf_op jit(solution)/shard_map/cond/branch_2_fun/pallas_call | solution.py:349
  17.5 6.4 %collective-permute-start.5 = (f32[2,8,512]{2,1,0:T(8,128)S(1)}, f32[2,8,512]{2,1,0:T(8,128)S(1)}, u32[]{:S(2)}, u32[]{:S(2)}) collective-permute-start(f32[2,8,512]{2,1,0:T(8,128)S(1)} %get-tuple-element.120.stats_ref), channel_id=1, source_target_pairs={{0,508},{8,4},{16,12},{24,20},{32,28},{40,36},{48,44},{56,52},{64,... | collective-permute-start | bytes 98312 | tf_op jit(solution)/shard_map/cond/branch_2_fun/ppermute | solution.py:357
  23.9 0.4 convolution_convert_fusion.2
  24.4 10.2 %collective-permute-done.5.moved_ref = f32[2,8,512]{2,1,0:T(8,128)S(1)} collective-permute-done((f32[2,8,512]{2,1,0:T(8,128)S(1)}, f32[2,8,512]{2,1,0:T(8,128)S(1)}, u32[]{:S(2)}, u32[]{:S(2)}) %collective-permute-start.5) | collective-permute-done | bytes 32800 | tf_op jit(solution)/shard_map/cond/branch_2_fun/ppermute | solution.py:357
  34.5 0.0 collective-permute-done.6.refs_0_
  34.5 0.0 collective-permute-done.7.refs_1_
  34.6 7.4 %branch_2_fun.7 = (bf16[3,512,512]{2,1,0:T(8,128)(2,1)S(1)}, bf16[48,512]{1,0:T(8,128)(2,1)S(1)}) custom-call(s32[5]{0:T(128)S(1)} %get-tuple-element.114.role_ref, bf16[512,512]{1,0:T(8,128)(2,1)S(1)} %copy-done.2, bf16[512,512]{1,0:T(8,128)(2,1)S(1)} %copy-done.7, bf16[512,512]{1,0:T(8,128)(2,1)S(1)} %copy-done.12, bf16[512,512]{1,0:T(8,128)(2,1)S(1)} %copy-done.17, ...), custom_call_target="tpu_custom_call" | custom-call | flops 1610612736 | bytes 6291456 | tf_op jit(solution)/shard_map/cond/branch_2_fun/pallas_call | solution.py:378
  42.3 0.0 copy-start.30
  42.3 9.1 %all-gather = bf16[384,512]{1,0:T(8,128)(2,1)S(1)} all-gather(bf16[96,512]{1,0:T(8,128)(2,1)S(1)} %get-tuple-element.176), channel_id=2, replica_groups=mesh['zh'=8,'zl'=2,'x'=4,'yh'=2,'head'=4] {'head'}, dimensions={0}, use_global_device_ids=true | all-gather | bytes 491520 | tf_op jit(solution)/shard_map/all_gather | solution.py:405
  51.4 0.0 copy-done.30
  51.4 1.7 %shard_map.104 = bf16[576,128]{1,0:T(8,128)(2,1)S(1)} custom-call(bf16[4,96,512]{2,1,0:T(8,128)(2,1)S(1)} %bitcast.19, bf16[512,1024]{1,0:T(8,128)(2,1)} %inputs_ref.1, bf16[3,512,512]{2,1,0:T(8,128)(2,1)S(1)} %get-tuple-element.170.qkv_ref), custom_call_target="tpu_custom_call" | custom-call | flops 268435456 | bytes 1048576 | tf_op jit(solution)/shard_map/pallas_call | solution.py:407
  53.1 14.0 %all_to_all.15 = bf16[16,36,128]{2,1,0:T(8,128)(2,1)S(1)} all-to-all(bf16[16,36,128]{2,1,0:T(8,128)(2,1)S(1)} %reshape.26), channel_id=1, replica_groups=mesh['zh'=8,'zl'=2,'x'=4,'yh'=2,'head'=4] {'zl','x','yh'}, dimensions={0} | all-to-all | bytes 294912 | tf_op jit(solution)/shard_map/all_to_all | solution.py:414
  67.2 26.8 %all_to_all.16 = bf16[8,36,128]{2,1,0:T(8,128)(2,1)S(1)} all-to-all(bf16[8,36,128]{2,1,0:T(8,128)(2,1)S(1)} %broadcast_in_dim.6), channel_id=1, replica_groups=mesh['zh'=8,'zl'=2,'x'=4,'yh'=2,'head'=4] {'zh'}, dimensions={0} | all-to-all | bytes 147456 | tf_op jit(solution)/shard_map/all_to_all | solution.py:417
  94.0 12.0 %all_to_all.17 = bf16[16,36,128]{2,1,0:T(8,128)(2,1)S(1)} all-to-all(bf16[16,36,128]{2,1,0:T(8,128)(2,1)S(1)} %broadcast_in_dim.7), channel_id=1, replica_groups=mesh['zh'=8,'zl'=2,'x'=4,'yh'=2,'head'=4] {'zl','x','yh'}, dimensions={0} | all-to-all | bytes 294912 | tf_op jit(solution)/shard_map/all_to_all | solution.py:419
  106.1 0.7 shard_map.105
  (10 shorter events, 0.2 us)
Async XLA Ops:
  2.8 7.0 %copy-start.2 = (bf16[512,512]{1,0:T(8,128)(2,1)S(1)}, bf16[512,512]{1,0:T(8,128)(2,1)}, u32[]{:S(2)}) copy-start(bf16[512,512]{1,0:T(8,128)(2,1)} %get-tuple-element.115.q_ref) | copy-start | bytes 1572868 | tf_op jit(solution)/shard_map/cond
  2.8 7.0 %copy-start.7 = (bf16[512,512]{1,0:T(8,128)(2,1)S(1)}, bf16[512,512]{1,0:T(8,128)(2,1)}, u32[]{:S(2)}) copy-start(bf16[512,512]{1,0:T(8,128)(2,1)} %get-tuple-element.116.k_ref) | copy-start | bytes 1572868 | tf_op jit(solution)/shard_map/cond
  2.8 6.9 %copy-start.12 = (bf16[512,512]{1,0:T(8,128)(2,1)S(1)}, bf16[512,512]{1,0:T(8,128)(2,1)}, u32[]{:S(2)}) copy-start(bf16[512,512]{1,0:T(8,128)(2,1)} %get-tuple-element.117.v_ref) | copy-start | bytes 1572868 | tf_op jit(solution)/shard_map/cond
  2.8 6.9 %copy-start.17 = (bf16[512,512]{1,0:T(8,128)(2,1)S(1)}, bf16[512,512]{1,0:T(8,128)(2,1)}, u32[]{:S(2)}) copy-start(bf16[512,512]{1,0:T(8,128)(2,1)} %get-tuple-element.118.g_ref) | copy-start | bytes 1572868 | tf_op jit(solution)/shard_map/cond
  4.6 29.9 %collective-permute-start.6 = (bf16[2,2,512,128]{3,2,1,0:T(8,128)(2,1)S(1)}, bf16[2,2,512,128]{3,2,1,0:T(8,128)(2,1)S(1)}, u32[]{:S(2)}, u32[]{:S(2)}) collective-permute-start(bf16[2,2,512,128]{3,2,1,0:T(8,128)(2,1)S(1)} %branch_2_fun.5), channel_id=1, source_target_pairs={{0,4},{8,12},{16,20},{24,28},{32,36},{40,44},{48,52},{56,60},{64,6... | collective-permute-start | bytes 1572872 | tf_op jit(solution)/shard_map/cond/branch_2_fun/ppermute | solution.py:363
  10.5 13.4 %copy-start.22 = (bf16[512,1024]{1,0:T(8,128)(2,1)S(1)}, bf16[512,1024]{1,0:T(8,128)(2,1)}, u32[]{:S(2)}) copy-start(bf16[512,1024]{1,0:T(8,128)(2,1)} %get-tuple-element.129) | copy-start | bytes 3145732 | tf_op jit(solution)/shard_map/cond
  10.5 13.4 %copy-start.27 = (bf16[48,1024]{1,0:T(8,128)(2,1)S(1)}, bf16[48,1024]{1,0:T(8,128)(2,1)}, u32[]{:S(2)}) copy-start(bf16[48,1024]{1,0:T(8,128)(2,1)} %get-tuple-element.128) | copy-start | bytes 294916 | tf_op jit(solution)/shard_map/cond
  10.5 24.1 %copy-start.33 = (bf16[3,16,512]{2,1,0:T(8,128)(2,1)S(1)}, bf16[3,16,512]{2,1,0:T(8,128)(2,1)}, u32[]{:S(2)}) copy-start(bf16[3,16,512]{2,1,0:T(8,128)(2,1)} %get-tuple-element.125.up_ref) | copy-start | bytes 147460 | tf_op jit(solution)/shard_map/cond
  10.5 24.1 %collective-permute-start.7 = (bf16[2,2,512,128]{3,2,1,0:T(8,128)(2,1)S(1)}, bf16[2,2,512,128]{3,2,1,0:T(8,128)(2,1)S(1)}, u32[]{:S(2)}, u32[]{:S(2)}) collective-permute-start(bf16[2,2,512,128]{3,2,1,0:T(8,128)(2,1)S(1)} %branch_2_fun.6), channel_id=1, source_target_pairs={{0,508},{8,4},{16,12},{24,20},{32,28},{40,36},{48,44},{56,52},{64,... | collective-permute-start | bytes 1572872 | tf_op jit(solution)/shard_map/cond/branch_2_fun/ppermute | solution.py:365
  17.5 17.0 %collective-permute-start.5 = (f32[2,8,512]{2,1,0:T(8,128)S(1)}, f32[2,8,512]{2,1,0:T(8,128)S(1)}, u32[]{:S(2)}, u32[]{:S(2)}) collective-permute-start(f32[2,8,512]{2,1,0:T(8,128)S(1)} %get-tuple-element.120.stats_ref), channel_id=1, source_target_pairs={{0,508},{8,4},{16,12},{24,20},{32,28},{40,36},{48,44},{56,52},{64,... | collective-permute-start | bytes 98312 | tf_op jit(solution)/shard_map/cond/branch_2_fun/ppermute | solution.py:357
  42.3 9.1 %copy-start.30 = (bf16[3,512,512]{2,1,0:T(8,128)(2,1)}, bf16[3,512,512]{2,1,0:T(8,128)(2,1)S(1)}, u32[]{:S(2)}) copy-start(bf16[3,512,512]{2,1,0:T(8,128)(2,1)S(1)} %get-tuple-element.170.qkv_ref) | copy-start | bytes 4718596

commit v5 on v4

--- a/solution.py
+++ b/solution.py
@@ -48,18 +48,10 @@
     return pl.ds(pl.multiple_of(head * HEAD, HEAD), HEAD)
 
 
-def causal_mask(rows):
-    keys = lax.broadcasted_iota(jnp.int32, (rows, rows), 0)
-    queries = lax.broadcasted_iota(jnp.int32, (rows, rows), 1)
+def causal_mask(rows, columns):
+    keys = lax.broadcasted_iota(jnp.int32, (rows, columns), 0)
+    queries = lax.broadcasted_iota(jnp.int32, (rows, columns), 1)
     return keys <= queries
-
-
-def row_stats(scores, dprobs, factor):
-    top = functools.reduce(jnp.maximum, [jnp.max(s, axis=0, keepdims=True) for s in scores])
-    exponents = [jnp.exp2((s - top) * factor) for s in scores]
-    total = sum(jnp.sum(e, axis=0, keepdims=True) for e in exponents)
-    mixed = sum(jnp.sum(e * d, axis=0, keepdims=True) for e, d in zip(exponents, dprobs))
-    return exponents, (top, total, mixed)
 
 
 def merge_stats(one, other, factor):
@@ -74,49 +66,61 @@
     return probs.astype(BF16), (probs * (dprobs - delta)).astype(BF16)
 
 
-class Tile:
-    def __init__(self, queries, grads, index, factor):
-        cut = slice(index * TILE, (index + 1) * TILE)
-        self.queries, self.grads = queries[cut], grads[cut]
-        self.index, self.factor = index, factor
-
-    def products(self, pair, start, rows, masked):
-        scores = dot_nt(pair[0][start : start + rows], self.queries)
-        if masked:
-            scores = jnp.where(causal_mask(TILE), scores, -jnp.inf)
-        return scores, dot_nt(pair[1][start : start + rows], self.grads)
-
-    def own_pieces(self):
-        before = [(0, self.index * TILE, False)] if self.index else []
-        return before + [(self.index * TILE, TILE, True)]
-
-    def own_stats(self, own):
-        products = [self.products(own, *piece) for piece in self.own_pieces()]
-        exponents, stats = row_stats(*zip(*products), self.factor)
-        return exponents, [dprobs for _, dprobs in products], stats
+def join(function, wide, narrow):
+    if wide is None or wide.shape == narrow.shape:
+        return narrow if wide is None else function(wide, narrow)
+    first = wide.shape[1] - narrow.shape[1]
+    return jnp.concatenate([wide[:, :first], function(wide[:, first:], narrow)], 1)
+
+
+def col_sum(value):
+    return jnp.sum(value, axis=0, keepdims=True)
+
+
+class Head:
+    def __init__(self, queries, grads, factor):
+        self.queries, self.grads, self.factor = queries, grads, factor
 
     def full_block(self, pair, own_stats):
-        scores, dprobs = self.products(pair, 0, pair[0].shape[0], False)
-        (exponent,), stats = row_stats([scores], [dprobs], self.factor)
+        scores = dot_nt(pair[0], self.queries)
+        dprobs = dot_nt(pair[1], self.grads)
+        own_top = jnp.max(scores, axis=0, keepdims=True)
+        exponent = jnp.exp2((scores - own_top) * self.factor)
+        stats = own_top, col_sum(exponent), col_sum(exponent * dprobs)
         top, total, mixed = merge_stats(stats, own_stats, self.factor)
         inverse = 1.0 / total
         delta = mixed * inverse
-        probs = exponent * (jnp.exp2((stats[0] - top) * self.factor) * inverse)
+        probs = exponent * (jnp.exp2((own_top - top) * self.factor) * inverse)
         return low_parts(probs, dprobs, delta), (top, inverse, delta)
 
-
-class Sums:
-    def __init__(self):
-        self.parts = {}
-
-    def add(self, start, value):
-        for at in range(0, value.shape[0], TILE):
-            part = value[at : at + TILE]
-            held = self.parts.get(start + at)
-            self.parts[start + at] = part if held is None else held + part
-
-    def whole(self):
-        return jnp.concatenate([self.parts[at] for at in sorted(self.parts)], 0)
+    def own_products(self, own):
+        pieces = []
+        for start in range(0, self.queries.shape[0], TILE):
+            scores = dot_nt(own[0][start : start + TILE], self.queries[start:])
+            scores = jnp.where(causal_mask(*scores.shape), scores, -jnp.inf)
+            dprobs = dot_nt(own[1][start : start + TILE], self.grads[start:])
+            pieces.append((start, scores, dprobs))
+        return pieces
+
+    def own_stats(self, pieces):
+        top = total = mixed = None
+        for _, scores, _ in pieces:
+            top = join(jnp.maximum, top, jnp.max(scores, axis=0, keepdims=True))
+        exponents = []
+        for start, scores, dprobs in pieces:
+            exponents.append(jnp.exp2((scores - top[:, start:]) * self.factor))
+            total = join(jnp.add, total, col_sum(exponents[-1]))
+            mixed = join(jnp.add, mixed, col_sum(exponents[-1] * dprobs))
+        return exponents, (top, total, mixed)
+
+    def own_block(self, own, weights):
+        query_t, key_grads, value_grads = None, [], []
+        for start, probs, dprobs, delta in weights:
+            probs, dscores = low_parts(probs, dprobs, delta)
+            query_t = join(jnp.add, query_t, dot_tn(own[0][start : start + TILE], dscores))
+            key_grads.append(dot_nn(dscores, self.queries[start:]))
+            value_grads.append(dot_nn(probs, self.grads[start:]))
+        return query_t, jnp.concatenate(key_grads, 0), jnp.concatenate(value_grads, 0)
 
 
 def plan_kernel(flags_ref, role_ref, shifted_ref):
@@ -162,17 +166,14 @@
 
 
 def early_kernel(factor, scale, role_ref, q_ref, k_ref, v_ref, g_ref, dq_ref, dk_ref, dv_ref, stats_ref, order_ref):
-    tiles = range(q_ref.shape[0] // TILE)
     count = list_heads(role_ref, order_ref, 1)
 
     def rows(slot, _):
         cols = columns_of(order_ref[slot])
-        own = (k_ref[:, cols], v_ref[:, cols])
-        for index in tiles:
-            tile = Tile(q_ref[:, cols], g_ref[:, cols], index, factor)
-            _, _, stats = tile.own_stats(own)
-            for row in range(3):
-                stats_ref[slot, row : row + 1, index * TILE : (index + 1) * TILE] = stats[row]
+        head = Head(q_ref[:, cols], g_ref[:, cols], factor)
+        _, stats = head.own_stats(head.own_products((k_ref[:, cols], v_ref[:, cols])))
+        for row in range(3):
+            stats_ref[slot, row : row + 1] = stats[row]
         return 0
 
     lax.fori_loop(0, count, rows, 0)
@@ -181,20 +182,21 @@
     def step(slot, _):
         cols = columns_of(order_ref[slot])
         own = (k_ref[:, cols], v_ref[:, cols])
-        key_sums, value_sums = Sums(), Sums()
-        for index in tiles:
-            tile = Tile(q_ref[:, cols], g_ref[:, cols], index, factor)
-            exponents, dprobs, (_, total, mixed) = tile.own_stats(own)
-            inverse = 1.0 / total
-            query_t = 0.0
-            for (start, length, _), e, d in zip(tile.own_pieces(), exponents, dprobs):
-                probs, dscores = low_parts(e * inverse, d, mixed * inverse)
-                query_t = query_t + dot_tn(own[0][start : start + length], dscores)
-                key_sums.add(start, dot_nn(dscores, tile.queries))
-                value_sums.add(start, dot_nn(probs, tile.grads))
-            dq_ref[slot, index * TILE : (index + 1) * TILE] = (query_t.T * scale).astype(BF16)
-        dk_ref[slot] = key_sums.whole()
-        dv_ref[slot] = value_sums.whole()
+        head = Head(q_ref[:, cols], g_ref[:, cols], factor)
+        pieces = head.own_products(own)
+        exponents, (_, total, mixed) = head.own_stats(pieces)
+        inverse = 1.0 / total
+        delta = mixed * inverse
+        query_t, dk, dv = head.own_block(
+            own,
+            [
+                (start, exponent * inverse[:, start:], dprobs, delta[:, start:])
+                for (start, _, dprobs), exponent in zip(pieces, exponents)
+            ],
+        )
+        dq_ref[slot] = (query_t.T * scale).astype(BF16)
+        dk_ref[slot] = dk
+        dv_ref[slot] = dv
         return 0
 
     lax.fori_loop(0, count, step, 0)
@@ -204,10 +206,8 @@
     return [(parity, ref, ref.shape[0]) for parity, ref in zip(parities, refs)]
 
 
-def tile_stats(stats_ref, slot, index):
-    return tuple(
-        stats_ref[slot, row : row + 1, index * TILE : (index + 1) * TILE] for row in range(3)
-    )
+def head_stats(stats_ref, slot):
+    return tuple(stats_ref[slot, row : row + 1] for row in range(3))
 
 
 def late_kernel(
@@ -216,32 +216,30 @@
 ):
     *other_refs, out_ref, back_ref, order_ref = refs
     kv_refs, qg_refs = other_refs[: len(kv_parities)], other_refs[-len(qg_parities) :]
-    tiles = range(q_ref.shape[0] // TILE)
     list_heads(role_ref, order_ref, 1)
 
     def second(kv_ref, slot, _):
         cols = columns_of(order_ref[slot])
         own = (k_ref[:, cols], v_ref[:, cols])
         before = (kv_ref[slot, 0], kv_ref[slot, 1])
-        key_sums, value_sums = Sums(), Sums()
-        for index in tiles:
-            tile = Tile(q_ref[:, cols], g_ref[:, cols], index, factor)
-            (_, dscores), (top, inverse, delta) = tile.full_block(
-                before, tile_stats(stats_ref, slot, index)
-            )
-            query_t = dot_tn(before[0], dscores)
-            for piece in tile.own_pieces():
-                start, length, _ = piece
-                scores, dprobs = tile.products(own, *piece)
-                probs, dscores = low_parts(
-                    jnp.exp2((scores - top) * factor) * inverse, dprobs, delta
+        head = Head(q_ref[:, cols], g_ref[:, cols], factor)
+        (_, dscores), (top, inverse, delta) = head.full_block(before, head_stats(stats_ref, slot))
+        query_t, dk, dv = head.own_block(
+            own,
+            [
+                (
+                    start,
+                    jnp.exp2((scores - top[:, start:]) * factor) * inverse[:, start:],
+                    dprobs,
+                    delta[:, start:],
                 )
-                query_t = query_t + dot_tn(own[0][start : start + length], dscores)
-                key_sums.add(start, dot_nn(dscores, tile.queries))
-                value_sums.add(start, dot_nn(probs, tile.grads))
-            out_ref[0, index * TILE : (index + 1) * TILE, cols] = (query_t.T * scale).astype(BF16)
-        out_ref[1, :, cols] = (key_sums.whole() * scale).astype(BF16)
-        out_ref[2, :, cols] = value_sums.whole().astype(BF16)
+                for start, scores, dprobs in head.own_products(own)
+            ],
+        )
+        query_t = query_t + dot_tn(before[0], dscores)
+        out_ref[0, :, cols] = (query_t.T * scale).astype(BF16)
+        out_ref[1, :, cols] = (dk * scale).astype(BF16)
+        out_ref[2, :, cols] = dv.astype(BF16)
         return 0
 
     run_sides(role_ref, side_refs(kv_refs, kv_parities), second)
@@ -249,16 +247,13 @@
 
     def first(qg_ref, slot, _):
         cols = columns_of(order_ref[slot])
-        own = (k_ref[:, cols], v_ref[:, cols])
-        dk, dv = dk_ref[slot], dv_ref[slot]
-        for index in tiles:
-            tile = Tile(qg_ref[slot, 0], qg_ref[slot, 1], index, factor)
-            (probs, dscores), _ = tile.full_block(own, tile_stats(moved_ref, slot, index))
-            dk = dk + dot_nn(dscores, tile.queries)
-            dv = dv + dot_nn(probs, tile.grads)
+        head = Head(qg_ref[slot, 0], qg_ref[slot, 1], factor)
+        (probs, dscores), _ = head.full_block(
+            (k_ref[:, cols], v_ref[:, cols]), head_stats(moved_ref, slot)
+        )
         out_ref[0, :, cols] = dq_ref[slot]
-        out_ref[1, :, cols] = (dk * scale).astype(BF16)
-        out_ref[2, :, cols] = dv.astype(BF16)
+        out_ref[1, :, cols] = ((dk_ref[slot] + dot_nn(dscores, head.queries)) * scale).astype(BF16)
+        out_ref[2, :, cols] = (dv_ref[slot] + dot_nn(probs, head.grads)).astype(BF16)
         return 0
 
     run_sides(role_ref, side_refs(qg_refs, qg_parities), first)

time: 107 us -> 107 us (level)
  Pallas kernels: 17.3 us -> 16.1 us
    all_to_all x1, blocking collectives: 14 us -> 19.5 us  [local(): grad = lax.all_to_all(grad.reshape(near, rows // near, HEAD), NEAR, 0, 0)]
    all_gather x1, blocking collectives: 9.06 us -> 6.15 us  [local(): parts = lax.all_gather(parts, 'head')]
    all_to_all x1, blocking collectives: 26.8 us -> 24.3 us  [local(): lax.all_to_all(jnp.broadcast_to(grad, (far,) + grad.shape), FAR, 0, 0)]
where the time goes in v5:
time: 107 us; the launch traced here: 106 us
  blocking collectives  62 us (58%)
  Pallas kernels  16.1 us (15%)
  starting transfers between devices  14.7 us (14%)
  waiting for transfers between devices  10.8 us (10%)
  between operations  1.33 us (1%)
    all_to_all x1, blocking collectives, local(): lax.all_to_all(jnp.broadcast_to(grad, (far,) + grad.shape), FAR, 0, 0)  24.3 us
    all_to_all x1, blocking collectives, local(): grad = lax.all_to_all(grad.reshape(near, rows // near, HEAD), NEAR, 0, 0)  19.5 us
    all_to_all x1, blocking collectives, local(): lax.all_to_all(jnp.broadcast_to(grad, (near,) + grad.shape), NEAR, 0, 0)  12 us
    ppermute x1, waiting for transfers between devices, attention(): lax.ppermute(stats, CTX, behind)  10.8 us
    pallas_call x1, Pallas kernels, attention(): call(functools.partial(late_kernel, factor, scale, kv_parities, qg_pariti...  6.43 us
    ppermute x1, starting transfers between devices, attention(): lax.ppermute(stats, CTX, behind)  6.37 us
    all_gather x1, blocking collectives, local(): parts = lax.all_gather(parts, 'head')  6.15 us
    ppermute x1, starting transfers between devices, attention(): kv = [lax.ppermute(sent, CTX, ahead)]  5.1 us
  transfers between devices with their start and end apart: 3, of which 1 were waited for; matrix products, arithmetic and copies ran while one was open for 0% of the time, Pallas kernels for 4%

profile of v5, /device:TPU:2, one launch (start us, length us, event | category | flops | bytes accessed | tf_op | source)
XLA Modules:
  0.0 106.4 jit_solution(679366748117806289)
XLA Ops:
  0.6 1.3 %shard_map.103 = (s32[5]{0:T(128)S(1)}, s32[1]{0:T(128)}) custom-call(s32[4]{0:T(128)} %flags_ref.1), custom_call_target="tpu_custom_call" | custom-call | tf_op jit(solution)/shard_map/pallas_call | solution.py:388
  2.6 39.1 %conditional.1 = (bf16[3,512,512]{2,1,0:T(8,128)(2,1)S(1)}, bf16[96,512]{1,0:T(8,128)(2,1)S(1)}) conditional(s32[]{:T(128)} %bitcast, (s32[5]{0:T(128)S(1)}, bf16[512,512]{1,0:T(8,128)(2,1)}, bf16[512,512]{1,0:T(8,128)(2,1)}, bf16[512,512]{1,0:T(8,128)(2,1)}, bf16[512,512]{1,0:T(8,128)(2,1)}, ...), branch_computations={%region_0.0_spmd, %region_1.0_spmd, %region_2.0_spmd, %region_3.0_... | conditional | flops 3271779328 | bytes 31605032 | solution.py:395
  2.8 0.0 copy-start.2
  2.8 0.0 copy-start.7
  2.8 0.0 copy-start.12
  2.8 0.0 copy-start.17
  2.8 1.8 %branch_2_fun.5 = bf16[2,2,512,128]{3,2,1,0:T(8,128)(2,1)S(1)} custom-call(s32[5]{0:T(128)S(1)} %get-tuple-element.114.role_ref, bf16[512,512]{1,0:T(8,128)(2,1)} %get-tuple-element.115.q_ref, bf16[512,512]{1,0:T(8,128)(2,1)} %get-tuple-element.116.k_ref, bf16[512,512]{1,0:T(8,128)(2,1)} %get-tuple-element.117.v_ref, bf16[512,512]{1,0:T(8,128)(2,1)} %get-tuple-element.118.g_ref), custom_call_target="tpu_custom_call" | custom-call | flops 1000 | bytes 3 | tf_op jit(solution)/shard_map/cond/branch_2_fun/pallas_call | solution.py:336
  4.6 5.1 %collective-permute-start.6 = (bf16[2,2,512,128]{3,2,1,0:T(8,128)(2,1)S(1)}, bf16[2,2,512,128]{3,2,1,0:T(8,128)(2,1)S(1)}, u32[]{:S(2)}, u32[]{:S(2)}) collective-permute-start(bf16[2,2,512,128]{3,2,1,0:T(8,128)(2,1)S(1)} %branch_2_fun.5), channel_id=1, source_target_pairs={{0,4},{8,12},{16,20},{24,28},{32,36},{40,44},{48,52},{56,60},{64,6... | collective-permute-start | bytes 1572872 | tf_op jit(solution)/shard_map/cond/branch_2_fun/ppermute | solution.py:358
  9.7 0.0 copy-done.2
  9.7 0.0 copy-done.7
  9.7 0.0 copy-done.12
  9.7 0.0 copy-done.17
  9.8 0.7 branch_2_fun.6
  10.4 0.0 copy-start.22
  10.4 0.0 copy-start.27
  10.4 0.0 copy-start.33
  10.5 3.3 %collective-permute-start.7 = (bf16[2,2,512,128]{3,2,1,0:T(8,128)(2,1)S(1)}, bf16[2,2,512,128]{3,2,1,0:T(8,128)(2,1)S(1)}, u32[]{:S(2)}, u32[]{:S(2)}) collective-permute-start(bf16[2,2,512,128]{3,2,1,0:T(8,128)(2,1)S(1)} %branch_2_fun.6), channel_id=1, source_target_pairs={{0,508},{8,4},{16,12},{24,20},{32,28},{40,36},{48,44},{56,52},{64,... | collective-permute-start | bytes 1572872 | tf_op jit(solution)/shard_map/cond/branch_2_fun/ppermute | solution.py:360
  13.7 3.5 %branch_2_fun.4 = (bf16[2,512,128]{2,1,0:T(8,128)(2,1)S(1)}, f32[2,512,128]{2,1,0:T(8,128)S(1)}, f32[2,512,128]{2,1,0:T(8,128)S(1)}, f32[2,8,512]{2,1,0:T(8,128)S(1)}) custom-call(s32[5]{0:T(128)S(1)} %get-tuple-element.114.role_ref, bf16[512,512]{1,0:T(8,128)(2,1)S(1)} %copy-done.2, bf16[512,512]{1,0:T(8,128)(2,1)S(1)} %copy-done.7, ...), custom_call_target="tpu_custom_call" | custom-call | flops 1 | tf_op jit(solution)/shard_map/cond/branch_2_fun/pallas_call | solution.py:344
  17.3 6.4 %collective-permute-start.5 = (f32[2,8,512]{2,1,0:T(8,128)S(1)}, f32[2,8,512]{2,1,0:T(8,128)S(1)}, u32[]{:S(2)}, u32[]{:S(2)}) collective-permute-start(f32[2,8,512]{2,1,0:T(8,128)S(1)} %get-tuple-element.120.stats_ref), channel_id=1, source_target_pairs={{0,508},{8,4},{16,12},{24,20},{32,28},{40,36},{48,44},{56,52},{64,... | collective-permute-start | bytes 98312 | tf_op jit(solution)/shard_map/cond/branch_2_fun/ppermute | solution.py:352
  23.7 0.4 convolution_convert_fusion.2
  24.1 10.8 %collective-permute-done.5.moved_ref = f32[2,8,512]{2,1,0:T(8,128)S(1)} collective-permute-done((f32[2,8,512]{2,1,0:T(8,128)S(1)}, f32[2,8,512]{2,1,0:T(8,128)S(1)}, u32[]{:S(2)}, u32[]{:S(2)}) %collective-permute-start.5) | collective-permute-done | bytes 32800 | tf_op jit(solution)/shard_map/cond/branch_2_fun/ppermute | solution.py:352
  35.0 0.0 collective-permute-done.6.refs_0_
  35.0 0.0 collective-permute-done.7.refs_1_
  35.0 0.0 copy-done.33
  35.0 6.4 %branch_2_fun.7 = (bf16[3,512,512]{2,1,0:T(8,128)(2,1)S(1)}, bf16[48,512]{1,0:T(8,128)(2,1)S(1)}) custom-call(s32[5]{0:T(128)S(1)} %get-tuple-element.114.role_ref, bf16[512,512]{1,0:T(8,128)(2,1)S(1)} %copy-done.2, bf16[512,512]{1,0:T(8,128)(2,1)S(1)} %copy-done.7, bf16[512,512]{1,0:T(8,128)(2,1)S(1)} %copy-done.12, bf16[512,512]{1,0:T(8,128)(2,1)S(1)} %copy-done.17, ...), custom_call_target="tpu_custom_call" | custom-call | flops 1610612736 | bytes 6291456 | tf_op jit(solution)/shard_map/cond/branch_2_fun/pallas_call | solution.py:373
  41.7 0.0 copy-start.30
  41.7 6.1 %all-gather = bf16[384,512]{1,0:T(8,128)(2,1)S(1)} all-gather(bf16[96,512]{1,0:T(8,128)(2,1)S(1)} %get-tuple-element.176), channel_id=2, replica_groups=mesh['zh'=8,'zl'=2,'x'=4,'yh'=2,'head'=4] {'head'}, dimensions={0}, use_global_device_ids=true | all-gather | bytes 491520 | tf_op jit(solution)/shard_map/all_gather | solution.py:400
  47.9 1.7 %shard_map.104 = bf16[576,128]{1,0:T(8,128)(2,1)S(1)} custom-call(bf16[4,96,512]{2,1,0:T(8,128)(2,1)S(1)} %bitcast.19, bf16[512,1024]{1,0:T(8,128)(2,1)} %inputs_ref.1, bf16[3,512,512]{2,1,0:T(8,128)(2,1)S(1)} %get-tuple-element.170.qkv_ref), custom_call_target="tpu_custom_call" | custom-call | flops 268435456 | bytes 1048576 | tf_op jit(solution)/shard_map/pallas_call | solution.py:402
  49.6 19.5 %all_to_all.15 = bf16[16,36,128]{2,1,0:T(8,128)(2,1)S(1)} all-to-all(bf16[16,36,128]{2,1,0:T(8,128)(2,1)S(1)} %reshape.26), channel_id=1, replica_groups=mesh['zh'=8,'zl'=2,'x'=4,'yh'=2,'head'=4] {'zl','x','yh'}, dimensions={0} | all-to-all | bytes 294912 | tf_op jit(solution)/shard_map/all_to_all | solution.py:409
  69.2 24.3 %all_to_all.16 = bf16[8,36,128]{2,1,0:T(8,128)(2,1)S(1)} all-to-all(bf16[8,36,128]{2,1,0:T(8,128)(2,1)S(1)} %broadcast_in_dim.6), channel_id=1, replica_groups=mesh['zh'=8,'zl'=2,'x'=4,'yh'=2,'head'=4] {'zh'}, dimensions={0} | all-to-all | bytes 147456 | tf_op jit(solution)/shard_map/all_to_all | solution.py:412
  93.6 12.0 %all_to_all.17 = bf16[16,36,128]{2,1,0:T(8,128)(2,1)S(1)} all-to-all(bf16[16,36,128]{2,1,0:T(8,128)(2,1)S(1)} %broadcast_in_dim.7), channel_id=1, replica_groups=mesh['zh'=8,'zl'=2,'x'=4,'yh'=2,'head'=4] {'zl','x','yh'}, dimensions={0} | all-to-all | bytes 294912 | tf_op jit(solution)/shard_map/all_to_all | solution.py:414
  105.7 0.7 shard_map.105
  (10 shorter events, 0.2 us)
Async XLA Ops:
  2.8 7.0 %copy-start.2 = (bf16[512,512]{1,0:T(8,128)(2,1)S(1)}, bf16[512,512]{1,0:T(8,128)(2,1)}, u32[]{:S(2)}) copy-start(bf16[512,512]{1,0:T(8,128)(2,1)} %get-tuple-element.115.q_ref) | copy-start | bytes 1572868 | tf_op jit(solution)/shard_map/cond
  2.8 7.0 %copy-start.7 = (bf16[512,512]{1,0:T(8,128)(2,1)S(1)}, bf16[512,512]{1,0:T(8,128)(2,1)}, u32[]{:S(2)}) copy-start(bf16[512,512]{1,0:T(8,128)(2,1)} %get-tuple-element.116.k_ref) | copy-start | bytes 1572868 | tf_op jit(solution)/shard_map/cond
  2.8 6.9 %copy-start.12 = (bf16[512,512]{1,0:T(8,128)(2,1)S(1)}, bf16[512,512]{1,0:T(8,128)(2,1)}, u32[]{:S(2)}) copy-start(bf16[512,512]{1,0:T(8,128)(2,1)} %get-tuple-element.117.v_ref) | copy-start | bytes 1572868 | tf_op jit(solution)/shard_map/cond
  2.8 6.9 %copy-start.17 = (bf16[512,512]{1,0:T(8,128)(2,1)S(1)}, bf16[512,512]{1,0:T(8,128)(2,1)}, u32[]{:S(2)}) copy-start(bf16[512,512]{1,0:T(8,128)(2,1)} %get-tuple-element.118.g_ref) | copy-start | bytes 1572868 | tf_op jit(solution)/shard_map/cond
  4.6 30.4 %collective-permute-start.6 = (bf16[2,2,512,128]{3,2,1,0:T(8,128)(2,1)S(1)}, bf16[2,2,512,128]{3,2,1,0:T(8,128)(2,1)S(1)}, u32[]{:S(2)}, u32[]{:S(2)}) collective-permute-start(bf16[2,2,512,128]{3,2,1,0:T(8,128)(2,1)S(1)} %branch_2_fun.5), channel_id=1, source_target_pairs={{0,4},{8,12},{16,20},{24,28},{32,36},{40,44},{48,52},{56,60},{64,6... | collective-permute-start | bytes 1572872 | tf_op jit(solution)/shard_map/cond/branch_2_fun/ppermute | solution.py:358
  10.4 13.3 %copy-start.22 = (bf16[512,1024]{1,0:T(8,128)(2,1)S(1)}, bf16[512,1024]{1,0:T(8,128)(2,1)}, u32[]{:S(2)}) copy-start(bf16[512,1024]{1,0:T(8,128)(2,1)} %get-tuple-element.129) | copy-start | bytes 3145732 | tf_op jit(solution)/shard_map/cond
  10.4 13.2 %copy-start.27 = (bf16[48,1024]{1,0:T(8,128)(2,1)S(1)}, bf16[48,1024]{1,0:T(8,128)(2,1)}, u32[]{:S(2)}) copy-start(bf16[48,1024]{1,0:T(8,128)(2,1)} %get-tuple-element.128) | copy-start | bytes 294916 | tf_op jit(solution)/shard_map/cond
  10.4 24.5 %copy-start.33 = (bf16[3,16,512]{2,1,0:T(8,128)(2,1)S(1)}, bf16[3,16,512]{2,1,0:T(8,128)(2,1)}, u32[]{:S(2)}) copy-start(bf16[3,16,512]{2,1,0:T(8,128)(2,1)} %get-tuple-element.125.up_ref) | copy-start | bytes 147460 | tf_op jit(solution)/shard_map/cond
  10.5 24.5 %collective-permute-start.7 = (bf16[2,2,512,128]{3,2,1,0:T(8,128)(2,1)S(1)}, bf16[2,2,512,128]{3,2,1,0:T(8,128)(2,1)S(1)}, u32[]{:S(2)}, u32[]{:S(2)}) collective-permute-start(bf16[2,2,512,128]{3,2,1,0:T(8,128)(2,1)S(1)} %branch_2_fun.6), channel_id=1, source_target_pairs={{0,508},{8,4},{16,12},{24,20},{32,28},{40,36},{48,44},{56,52},{64,... | collective-permute-start | bytes 1572872 | tf_op jit(solution)/shard_map/cond/branch_2_fun/ppermute | solution.py:360
  17.3 17.7 %collective-permute-start.5 = (f32[2,8,512]{2,1,0:T(8,128)S(1)}, f32[2,8,512]{2,1,0:T(8,128)S(1)}, u32[]{:S(2)}, u32[]{:S(2)}) collective-permute-start(f32[2,8,512]{2,1,0:T(8,128)S(1)} %get-tuple-element.120.stats_ref), channel_id=1, source_target_pairs={{0,508},{8,4},{16,12},{24,20},{32,28},{40,36},{48,44},{56,52},{64,... | collective-permute-start | bytes 98312 | tf_op jit(solution)/shard_map/cond/branch_2_fun/ppermute | solution.py:352
  41.7 6.2 %copy-start.30 = (bf16[3,512,512]{2,1,0:T(8,128)(2,1)}, bf16[3,512,512]{2,1,0:T(8,128)(2,1)S(1)}, u32[]{:S(2)}) copy-start(bf16[3,512,512]{2,1,0:T(8,128)(2,1)S(1)} %get-tuple-element.170.qkv_ref) | copy-start | bytes 4718596

commit v6 on v5

--- a/solution.py
+++ b/solution.py
@@ -31,10 +31,14 @@
     return lax.dot_general(left, right, (((1,), (0,)), ((), ())), preferred_element_type=F32)
 
 
-def list_heads(role_ref, order_ref, wanted):
-    count = jnp.int32(0)
-    for head in range(role_ref.shape[0] - 1):
-        chosen = role_ref[head] == wanted
+def parity_here():
+    return lax.axis_index("yh")
+
+
+def list_heads(flags_ref, order_ref, key, count=0):
+    count = jnp.int32(count)
+    for head in range(flags_ref.shape[0]):
+        chosen = key(flags_ref[head])
 
         @pl.when(chosen)
         def _():
@@ -42,6 +46,14 @@
 
         count = count + chosen.astype(jnp.int32)
     return count
+
+
+def is_first(flag):
+    return ((flag + parity_here()) & 1) == 0
+
+
+def is_second(flag):
+    return ((flag + parity_here()) & 1) == 1
 
 
 def columns_of(head):
@@ -123,50 +135,51 @@
         return query_t, jnp.concatenate(key_grads, 0), jnp.concatenate(value_grads, 0)
 
 
-def plan_kernel(flags_ref, role_ref, shifted_ref):
-    parity = lax.axis_index("yh")
+def fetch(sides, refs, slot, pair_ref):
+    for at, parity, base in sides:
+        ref = refs[at]
+        here = (slot >= base) & (slot < base + ref.shape[0])
+        if parity is not None:
+            here = here & (parity_here() == parity)
+
+        @pl.when(here)
+        def _():
+            pair_ref[...] = ref[slot - base]
+
+
+def pack_kernel(flags_ref, q_ref, k_ref, v_ref, g_ref, shifted_ref, *refs):
+    *out_refs, order_ref = refs
+    heads = flags_ref.shape[0]
     total = jnp.int32(0)
-    for head in range(flags_ref.shape[0]):
-        role_ref[head] = (flags_ref[head] + parity) & 1
+    for head in range(heads):
         total = total + flags_ref[head]
-    role_ref[flags_ref.shape[0]] = parity
     shifted_ref[0] = total
-
-
-def run_sides(role_ref, sides, step):
-    for parity, ref, count in sides:
-        if parity is None:
-            lax.fori_loop(0, count, functools.partial(step, ref), 0)
-        else:
-
-            @pl.when(role_ref[role_ref.shape[0] - 1] == parity)
-            def _():
-                lax.fori_loop(0, count, functools.partial(step, ref), 0)
-
-
-def pack_kernel(plans, role_ref, q_ref, k_ref, v_ref, g_ref, *refs):
-    *out_refs, order_ref = refs
-    for wanted, sent in ((0, (k_ref, v_ref)), (1, (q_ref, g_ref))):
-        chosen = [(ref, plan[1]) for ref, plan in zip(out_refs, plans) if plan[0] in (wanted, None)]
-        if not chosen:
-            continue
-        list_heads(role_ref, order_ref, wanted)
-
-        def step(out_ref, slot, _):
-            cols = columns_of(order_ref[slot])
-            out_ref[slot, 0] = sent[0][:, cols]
-            out_ref[slot, 1] = sent[1][:, cols]
-            return 0
-
-        sides = []
-        for ref, parity in chosen:
-            swapped = parity is not None and wanted == 1
-            sides.append(((parity + 1) % 2 if swapped else parity, ref, ref.shape[0]))
-        run_sides(role_ref, sides, step)
-
-
-def early_kernel(factor, scale, role_ref, q_ref, k_ref, v_ref, g_ref, dq_ref, dk_ref, dv_ref, stats_ref, order_ref):
-    count = list_heads(role_ref, order_ref, 1)
+    even = 2 * total == heads
+    major = (2 * total > heads).astype(jnp.int32)
+
+    def ahead(flag):
+        return jnp.where(even, (flag + parity_here()) & 1, (flag + major) & 1) == 0
+
+    count = list_heads(flags_ref, order_ref, ahead)
+    list_heads(flags_ref, order_ref, lambda flag: jnp.logical_not(ahead(flag)), count)
+    base = 0
+    for out_ref in out_refs:
+        for slot in range(out_ref.shape[0]):
+            head = order_ref[base + slot]
+            cols = columns_of(head)
+
+            def send(a_ref, b_ref):
+                out_ref[slot, 0] = a_ref[:, cols]
+                out_ref[slot, 1] = b_ref[:, cols]
+
+            first = is_first(flags_ref[head])
+            pl.when(first)(functools.partial(send, k_ref, v_ref))
+            pl.when(jnp.logical_not(first))(functools.partial(send, q_ref, g_ref))
+        base += out_ref.shape[0]
+
+
+def early_kernel(factor, scale, flags_ref, q_ref, k_ref, v_ref, g_ref, dq_ref, dk_ref, dv_ref, stats_ref, order_ref):
+    count = list_heads(flags_ref, order_ref, is_second)
 
     def rows(slot, _):
         cols = columns_of(order_ref[slot])
@@ -177,7 +190,7 @@
         return 0
 
     lax.fori_loop(0, count, rows, 0)
-    count = list_heads(role_ref, order_ref, 0)
+    count = list_heads(flags_ref, order_ref, is_first)
 
     def step(slot, _):
         cols = columns_of(order_ref[slot])
@@ -202,26 +215,22 @@
     lax.fori_loop(0, count, step, 0)
 
 
-def side_refs(refs, parities):
-    return [(parity, ref, ref.shape[0]) for parity, ref in zip(parities, refs)]
-
-
 def head_stats(stats_ref, slot):
     return tuple(stats_ref[slot, row : row + 1] for row in range(3))
 
 
 def late_kernel(
-    factor, scale, kv_parities, qg_parities, role_ref, q_ref, k_ref, v_ref, g_ref, stats_ref,
+    factor, scale, kv_sides, qg_sides, flags_ref, q_ref, k_ref, v_ref, g_ref, stats_ref,
     moved_ref, dq_ref, dk_ref, dv_ref, up_ref, *refs
 ):
-    *other_refs, out_ref, back_ref, order_ref = refs
-    kv_refs, qg_refs = other_refs[: len(kv_parities)], other_refs[-len(qg_parities) :]
-    list_heads(role_ref, order_ref, 1)
-
-    def second(kv_ref, slot, _):
+    *other_refs, out_ref, back_ref, order_ref, pair_ref = refs
+    count = list_heads(flags_ref, order_ref, is_second)
+
+    def second(slot, _):
+        fetch(kv_sides, other_refs, slot, pair_ref)
         cols = columns_of(order_ref[slot])
         own = (k_ref[:, cols], v_ref[:, cols])
-        before = (kv_ref[slot, 0], kv_ref[slot, 1])
+        before = (pair_ref[0], pair_ref[1])
         head = Head(q_ref[:, cols], g_ref[:, cols], factor)
         (_, dscores), (top, inverse, delta) = head.full_block(before, head_stats(stats_ref, slot))
         query_t, dk, dv = head.own_block(
@@ -242,12 +251,13 @@
         out_ref[2, :, cols] = dv.astype(BF16)
         return 0
 
-    run_sides(role_ref, side_refs(kv_refs, kv_parities), second)
-    list_heads(role_ref, order_ref, 0)
-
-    def first(qg_ref, slot, _):
+    lax.fori_loop(0, count, second, 0)
+    count = list_heads(flags_ref, order_ref, is_first)
+
+    def first(slot, _):
+        fetch(qg_sides, other_refs, slot, pair_ref)
         cols = columns_of(order_ref[slot])
-        head = Head(qg_ref[slot, 0], qg_ref[slot, 1], factor)
+        head = Head(pair_ref[0], pair_ref[1], factor)
         (probs, dscores), _ = head.full_block(
             (k_ref[:, cols], v_ref[:, cols]), head_stats(moved_ref, slot)
         )
@@ -256,7 +266,7 @@
         out_ref[2, :, cols] = (dv_ref[slot] + dot_nn(probs, head.grads)).astype(BF16)
         return 0
 
-    run_sides(role_ref, side_refs(qg_refs, qg_parities), first)
+    lax.fori_loop(0, count, first, 0)
     for index in range(3):
         back_ref[index * RANK : (index + 1) * RANK] = dot_nt(up_ref[index], out_ref[index]).astype(BF16)
 
@@ -294,14 +304,14 @@
 SMEM = pl.BlockSpec(memory_space=pltpu.SMEM)
 
 
-def call(kernel, outs, in_specs, flops, heads=0):
+def call(kernel, outs, in_specs, flops, heads=0, scratch=()):
     many = isinstance(outs, (list, tuple))
     return pl.pallas_call(
         kernel,
         out_shape=outs,
         in_specs=in_specs,
         out_specs=[VMEM] * len(outs) if many else VMEM,
-        scratch_shapes=[pltpu.SMEM((heads,), jnp.int32)] if heads else [],
+        scratch_shapes=([pltpu.SMEM((heads,), jnp.int32)] if heads else []) + list(scratch),
         compiler_params=pltpu.CompilerParams(vmem_limit_bytes=VMEM_BYTES),
         cost_estimate=pl.CostEstimate(flops=flops, bytes_accessed=flops >> 8, transcendentals=0),
     )
@@ -315,68 +325,50 @@
     return [(source, (source + step) % count) for source in range(parity, count, 2)]
 
 
-def attention(shifted, role, queries, keys, values, grads, inputs, down_t, up):
+def attention(shifted, flags, queries, keys, values, grads, inputs, down_t, up, *packs):
     tok_rows = queries.shape[0]
-    heads = role.shape[0] - 1
-    plain = heads - shifted
-    slots = max(plain, shifted)
+    heads = flags.shape[0]
+    slots = max(heads - shifted, shifted)
+    major = int(2 * shifted > heads)
     scale = 1.0 / math.sqrt(HEAD)
     factor = scale * math.log2(math.e)
     count = lax.axis_size(CTX)
-    ahead = ring(count, 0, 1) + ring(count, 1, 1)
     behind = ring(count, 0, -1) + ring(count, 1, -1)
     low = shape((slots, tok_rows, HEAD), BF16)
     full = shape((slots, tok_rows, HEAD), F32)
     unit = 2 * tok_rows * tok_rows * HEAD * slots
 
-    def pair(number):
-        return shape((number, 2, tok_rows, HEAD), BF16)
-
-    def packed(plans, numbers):
-        return call(
-            functools.partial(pack_kernel, plans),
-            [pair(number) for number in numbers],
-            [SMEM] + [VMEM] * 4,
-            1000,
-            heads,
-        )(role, queries, keys, values, grads)
-
+    arrived, kv_sides, qg_sides = [], [], []
+    base = 0
+    for at, pack in enumerate(packs):
+        later = base >= slots
+        if 2 * slots == heads:
+            pairs = behind if later else ring(count, 0, 1) + ring(count, 1, 1)
+            (qg_sides if later else kv_sides).append((at, None, base - slots * later))
+        else:
+            flag = major ^ int(later)
+            pairs = ring(count, flag, 1) + ring(count, 1 - flag, -1)
+            kv_sides.append((at, 1 - flag, base - slots * later))
+            qg_sides.append((at, flag, base - slots * later))
+        arrived.append(lax.ppermute(pack, CTX, pairs))
+        base += pack.shape[0]
     *first, stats = call(
         functools.partial(early_kernel, factor, scale),
         [low, full, full, shape((slots, 8, tok_rows), F32)],
         [SMEM] + [VMEM] * 4,
         1,
         heads,
-    )(role, queries, keys, values, grads)
-
+    )(flags, queries, keys, values, grads)
     stats, moved = lax.optimization_barrier((stats, lax.ppermute(stats, CTX, behind)))
-
-    numbers = (plain, shifted)
-    flags = [flag for flag in range(2) if numbers[flag]]
-    if plain == shifted:
-        sent = packed([(0, None)], [slots])[0]
-        kv = [lax.ppermute(sent, CTX, ahead)]
-        sent = packed([(1, None)], [slots])[0]
-        qg = [lax.ppermute(sent, CTX, behind)]
-        kv_parities = qg_parities = [None]
-    else:
-        flags = sorted(flags, key=lambda flag: -numbers[flag])
-        sent = packed([(None, flag) for flag in flags], [numbers[flag] for flag in flags])
-        kv = qg = [
-            lax.ppermute(sent[at], CTX, ring(count, flag, 1) + ring(count, (flag + 1) % 2, -1))
-            for at, flag in enumerate(flags)
-        ]
-        kv_parities = [(flag + 1) % 2 for flag in flags]
-        qg_parities = flags
     low_rank = dot_nt(down_t, inputs).astype(BF16)
-    arrived = kv if kv is qg else kv + qg
     qkv, back = call(
-        functools.partial(late_kernel, factor, scale, kv_parities, qg_parities),
+        functools.partial(late_kernel, factor, scale, kv_sides, qg_sides),
         [shape((3,) + queries.shape, BF16), shape((3 * RANK, tok_rows), BF16)],
         [SMEM] + [VMEM] * (10 + len(arrived)),
         12 * unit,
         heads,
-    )(role, queries, keys, values, grads, stats, moved, *first, up, *arrived)
+        [pltpu.VMEM((2, tok_rows, HEAD), BF16)],
+    )(flags, queries, keys, values, grads, stats, moved, *first, up, *arrived)
     return qkv, jnp.concatenate([back, low_rank], 0)
 
 
@@ -385,17 +377,21 @@
     heads = flags.shape[0]
     width = inputs.shape[1]
     seq_total = lax.axis_size(CTX) * tok_rows
-    role, shifted = pl.pallas_call(
-        plan_kernel,
-        out_shape=[shape((heads + 1,), jnp.int32), shape((1,), jnp.int32)],
-        in_specs=[SMEM],
-        out_specs=[SMEM, SMEM],
-    )(flags)
+    least = (heads + 1) // 2
+    sizes = [least] + [1] * (heads - least)
+    shifted, *packs = pl.pallas_call(
+        pack_kernel,
+        out_shape=[shape((1,), jnp.int32)] + [shape((size, 2, tok_rows, HEAD), BF16) for size in sizes],
+        in_specs=[SMEM] + [VMEM] * 4,
+        out_specs=[SMEM] + [VMEM] * len(sizes),
+        scratch_shapes=[pltpu.SMEM((heads,), jnp.int32)],
+        compiler_params=pltpu.CompilerParams(vmem_limit_bytes=VMEM_BYTES),
+    )(flags, queries, keys, values, grads)
     down_t = down.transpose(0, 2, 1).reshape(3 * RANK, width)
     qkv, parts = lax.switch(
         shifted.reshape(()),
         [functools.partial(attention, number) for number in range(heads + 1)],
-        role, queries, keys, values, grads, inputs, down_t, up,
+        flags, queries, keys, values, grads, inputs, down_t, up, *packs,
     )
     parts = lax.all_gather(parts, "head")
     rows = 3 * RANK * (width + queries.shape[1]) // HEAD

time: 107 us -> 105 us (0.981)
  starting transfers between devices: 14.7 us -> 26.6 us
  waiting for transfers between devices: 10.8 us -> 1.29 us
  blocking collectives: 62 us -> 59.1 us
  Pallas kernels: 16.1 us -> 14.4 us
    ppermute x1, waiting for transfers between devices: 10.8 us -> 1.28 us  [attention(): lax.ppermute(stats, CTX, behind)]
    ppermute x1, starting transfers between devices: 6.37 us -> 13.1 us  [attention(): lax.ppermute(stats, CTX, behind)]
    ppermute x2 -> x3, starting transfers between devices: 8.38 us -> 13.5 us  [attention(): arrived.append(lax.ppermute(pack, CTX, pairs))]
    all_to_all x1, blocking collectives: 19.5 us -> 15.2 us  [local(): grad = lax.all_to_all(grad.reshape(near, rows // near, HEAD), NEAR, 0, 0)]
    all_to_all x1, blocking collectives: 24.3 us -> 25.7 us  [local(): lax.all_to_all(jnp.broadcast_to(grad, (far,) + grad.shape), FAR, 0, 0)]
    pallas_call x1, Pallas kernels: 1.71 us -> 0.49 us  [local(): call(functools.partial(adapter_kernel, 1.0 / math.sqrt(seq_total)), shape...]
    pallas_call x4 -> x2, Pallas kernels: 10.1 us -> 9.37 us  [the longest x1 6.91 us: attention(): call(functools.partial(late_kernel, factor, scale, kv_sides, qg_sides), [...]
  transfers between devices with their start and end apart: 3 -> 4, of which waited for: 1 -> 1; matrix products, arithmetic and copies ran while one was open for 0% -> 0% of each run, Pallas kernels for 4% -> 4%
where the time goes in v6:
time: 105 us; the launch traced here: 104 us
  blocking collectives  59.1 us (56%)
  starting transfers between devices  26.6 us (25%)
  Pallas kernels  14.4 us (14%)
  between operations  1.39 us (1%)
  waiting for transfers between devices  1.29 us (1%)
    all_to_all x1, blocking collectives, local(): lax.all_to_all(jnp.broadcast_to(grad, (far,) + grad.shape), FAR, 0, 0)  25.7 us
    all_to_all x1, blocking collectives, local(): grad = lax.all_to_all(grad.reshape(near, rows // near, HEAD), NEAR, 0, 0)  15.2 us
    ppermute x3, starting transfers between devices, attention(): arrived.append(lax.ppermute(pack, CTX, pairs))  13.5 us
    ppermute x1, starting transfers between devices, attention(): lax.ppermute(stats, CTX, behind)  13.1 us
    all_to_all x1, blocking collectives, local(): lax.all_to_all(jnp.broadcast_to(grad, (near,) + grad.shape), NEAR, 0, 0)  12 us
    pallas_call x1, Pallas kernels, attention(): call(functools.partial(late_kernel, factor, scale, kv_sides, qg_sides), [...  6.91 us
    all_gather x1, blocking collectives, local(): parts = lax.all_gather(parts, 'head')  6.15 us
    pallas_call x1, Pallas kernels, attention(): call(functools.partial(early_kernel, factor, scale), [low, full, full, sh...  3.8 us
  transfers between devices with their start and end apart: 4, of which 1 were waited for; matrix products, arithmetic and copies ran while one was open for 0% of the time, Pallas kernels for 4%

profile of v6, /device:TPU:2, one launch (start us, length us, event | category | flops | bytes accessed | tf_op | source)
XLA Modules:
  0.0 104.0 jit_solution(5604789572753698978)
XLA Ops:
  0.6 0.0 copy-start.1
  0.6 0.0 copy-start.2
  0.7 0.0 copy-start.19
  0.7 0.0 copy-start
  0.7 2.5 %shard_map.103 = (s32[1]{0:T(128)}, bf16[2,2,512,128]{3,2,1,0:T(8,128)(2,1)S(1)}, bf16[1,2,512,128]{3,2,1,0:T(8,128)(2,1)S(1)}, bf16[1,2,512,128]{3,2,1,0:T(8,128)(2,1)S(1)}) custom-call(s32[4]{0:T(128)} %flags_ref.1, bf16[512,512]{1,0:T(8,128)(2,1)} %q_ref.1, bf16[512,512]{1,0:T(8,128)(2,1)} %k_ref.1, bf16[512,512]{1,0:T(8,128)(2,1)} %v_ref.1, ...), custom_call_target="tpu_custom_call" | custom-call | tf_op jit(solution)/shard_map/pallas_call | solution.py:382
  3.8 0.0 copy-done.1
  3.8 0.0 copy-done.2
  3.8 0.0 copy-done.19
  3.8 0.0 copy-done
  3.8 39.7 %conditional.1 = (bf16[3,512,512]{2,1,0:T(8,128)(2,1)S(1)}, bf16[96,512]{1,0:T(8,128)(2,1)S(1)}) conditional(s32[]{:T(128)} %bitcast, (s32[4]{0:T(128)S(1)}, bf16[512,512]{1,0:T(8,128)(2,1)S(1)}, bf16[512,512]{1,0:T(8,128)(2,1)S(1)}, bf16[512,512]{1,0:T(8,128)(2,1)}, bf16[512,512]{1,0:T(8,128)(2,1)}, ...), branch_computations={%region_0.0_spmd, %region_1.0_spmd, %region_2.0_spmd, %region_3.0_... | conditional | flops 3271778304 | bytes 23216416 | solution.py:391
  4.1 0.0 copy-start.16
  4.1 5.2 %collective-permute-start.13 = (bf16[2,2,512,128]{3,2,1,0:T(8,128)(2,1)S(1)}, bf16[2,2,512,128]{3,2,1,0:T(8,128)(2,1)S(1)}, u32[]{:S(2)}, u32[]{:S(2)}) collective-permute-start(bf16[2,2,512,128]{3,2,1,0:T(8,128)(2,1)S(1)} %get-tuple-element.179), channel_id=1, source_target_pairs={{4,8},{12,16},{20,24},{28,32},{36,40},{44,48},{52,56},{60,64},{68,... | collective-permute-start | bytes 1572872 | tf_op jit(solution)/shard_map/cond/branch_3_fun/ppermute | solution.py:353
  9.3 3.2 %collective-permute-start.14 = (bf16[1,2,512,128]{3,2,1,0:T(8,128)(2,1)S(1)}, bf16[1,2,512,128]{3,2,1,0:T(8,128)(2,1)S(1)}, u32[]{:S(2)}, u32[]{:S(2)}) collective-permute-start(bf16[1,2,512,128]{3,2,1,0:T(8,128)(2,1)S(1)} %get-tuple-element.180), channel_id=1, source_target_pairs={{4,8},{12,16},{20,24},{28,32},{36,40},{44,48},{52,56},{60,64},{68,... | collective-permute-start | bytes 786440 | tf_op jit(solution)/shard_map/cond/branch_3_fun/ppermute | solution.py:353
  12.5 5.1 %collective-permute-start.15 = (bf16[1,2,512,128]{3,2,1,0:T(8,128)(2,1)S(1)}, bf16[1,2,512,128]{3,2,1,0:T(8,128)(2,1)S(1)}, u32[]{:S(2)}, u32[]{:S(2)}) collective-permute-start(bf16[1,2,512,128]{3,2,1,0:T(8,128)(2,1)S(1)} %get-tuple-element.181), channel_id=1, source_target_pairs={{0,4},{8,12},{16,20},{24,28},{32,36},{40,44},{48,52},{56,60},{64,6... | collective-permute-start | bytes 786440 | tf_op jit(solution)/shard_map/cond/branch_3_fun/ppermute | solution.py:353
  17.6 0.0 copy-start.6
  17.6 0.0 copy-start.11
  17.6 0.0 copy-start.23
  17.6 3.8 %branch_3_fun.2 = (bf16[3,512,128]{2,1,0:T(8,128)(2,1)S(1)}, f32[3,512,128]{2,1,0:T(8,128)S(1)}, f32[3,512,128]{2,1,0:T(8,128)S(1)}, f32[3,8,512]{2,1,0:T(8,128)S(1)}) custom-call(s32[4]{0:T(128)S(1)} %get-tuple-element.167.flags_ref, bf16[512,512]{1,0:T(8,128)(2,1)S(1)} %get-tuple-element.168.q_ref, bf16[512,512]{1,0:T(8,128)(2,1)S(1)} %get-tuple-element.169.k_ref, ...), custom_call_target="tpu_custom_call" | custom-call | flops 1 | tf_op jit(solution)/shard_map/cond/branch_3_fun/pallas_call | solution.py:355
  21.4 13.1 %collective-permute-start.12 = (f32[3,8,512]{2,1,0:T(8,128)S(1)}, f32[3,8,512]{2,1,0:T(8,128)S(1)}, u32[]{:S(2)}, u32[]{:S(2)}) collective-permute-start(f32[3,8,512]{2,1,0:T(8,128)S(1)} %get-tuple-element.173.stats_ref), channel_id=1, source_target_pairs={{0,508},{8,4},{16,12},{24,20},{32,28},{40,36},{48,44},{56,52},{64,... | collective-permute-start | bytes 147464 | tf_op jit(solution)/shard_map/cond/branch_3_fun/ppermute | solution.py:362
  34.6 0.4 convolution_convert_fusion.3
  35.0 1.3 %collective-permute-done.12.moved_ref = f32[3,8,512]{2,1,0:T(8,128)S(1)} collective-permute-done((f32[3,8,512]{2,1,0:T(8,128)S(1)}, f32[3,8,512]{2,1,0:T(8,128)S(1)}, u32[]{:S(2)}, u32[]{:S(2)}) %collective-permute-start.12) | collective-permute-done | bytes 49184 | tf_op jit(solution)/shard_map/cond/branch_3_fun/ppermute | solution.py:362
  36.3 0.0 collective-permute-done.14.refs_1_
  36.3 0.0 collective-permute-done.15.refs_2_
  36.3 0.0 collective-permute-done.13.refs_0_
  36.3 6.9 %branch_3_fun.3 = (bf16[3,512,512]{2,1,0:T(8,128)(2,1)S(1)}, bf16[48,512]{1,0:T(8,128)(2,1)S(1)}) custom-call(s32[4]{0:T(128)S(1)} %get-tuple-element.167.flags_ref, bf16[512,512]{1,0:T(8,128)(2,1)S(1)} %get-tuple-element.168.q_ref, bf16[512,512]{1,0:T(8,128)(2,1)S(1)} %get-tuple-element.169.k_ref, bf16[512,512]{1,0:T(8,128)(2,1)S(1)} %copy-done.6, ...), custom_call_target="tpu_custom_call" | custom-call | flops 2415919104 | bytes 9437184 | tf_op jit(solution)/shard_map/cond/branch_3_fun/pallas_call | solution.py:364
  43.6 0.0 copy-start.18
  43.6 6.1 %all-gather = bf16[384,512]{1,0:T(8,128)(2,1)S(1)} all-gather(bf16[96,512]{1,0:T(8,128)(2,1)S(1)} %get-tuple-element.221), channel_id=2, replica_groups=mesh['zh'=8,'zl'=2,'x'=4,'yh'=2,'head'=4] {'head'}, dimensions={0}, use_global_device_ids=true | all-gather | bytes 491520 | tf_op jit(solution)/shard_map/all_gather | solution.py:396
  49.7 0.5 shard_map.104
  50.3 15.2 %all_to_all.15 = bf16[16,36,128]{2,1,0:T(8,128)(2,1)S(1)} all-to-all(bf16[16,36,128]{2,1,0:T(8,128)(2,1)S(1)} %reshape.26), channel_id=1, replica_groups=mesh['zh'=8,'zl'=2,'x'=4,'yh'=2,'head'=4] {'zl','x','yh'}, dimensions={0} | all-to-all | bytes 294912 | tf_op jit(solution)/shard_map/all_to_all | solution.py:405
  65.5 25.7 %all_to_all.16 = bf16[8,36,128]{2,1,0:T(8,128)(2,1)S(1)} all-to-all(bf16[8,36,128]{2,1,0:T(8,128)(2,1)S(1)} %broadcast_in_dim.6), channel_id=1, replica_groups=mesh['zh'=8,'zl'=2,'x'=4,'yh'=2,'head'=4] {'zh'}, dimensions={0} | all-to-all | bytes 147456 | tf_op jit(solution)/shard_map/all_to_all | solution.py:408
  91.2 12.0 %all_to_all.17 = bf16[16,36,128]{2,1,0:T(8,128)(2,1)S(1)} all-to-all(bf16[16,36,128]{2,1,0:T(8,128)(2,1)S(1)} %broadcast_in_dim.7), channel_id=1, replica_groups=mesh['zh'=8,'zl'=2,'x'=4,'yh'=2,'head'=4] {'zl','x','yh'}, dimensions={0} | all-to-all | bytes 294912 | tf_op jit(solution)/shard_map/all_to_all | solution.py:410
  103.3 0.7 shard_map.105
  (12 shorter events, 0.2 us)
Async XLA Ops:
  0.6 3.2 %copy-start.1 = (bf16[512,512]{1,0:T(8,128)(2,1)S(1)}, bf16[512,512]{1,0:T(8,128)(2,1)}, u32[]{:S(2)}) copy-start(bf16[512,512]{1,0:T(8,128)(2,1)} %q_ref.1) | copy-start | bytes 1572868
  0.6 3.2 %copy-start.2 = (bf16[512,512]{1,0:T(8,128)(2,1)S(1)}, bf16[512,512]{1,0:T(8,128)(2,1)}, u32[]{:S(2)}) copy-start(bf16[512,512]{1,0:T(8,128)(2,1)} %k_ref.1) | copy-start | bytes 1572868
  0.7 3.2 %copy-start.19 = (s32[4]{0:T(128)S(1)}, s32[4]{0:T(128)}, u32[]{:S(2)}) copy-start(s32[4]{0:T(128)} %flags_ref.1) | copy-start | bytes 52
  0.7 3.2 %copy-start = (bf16[512,1024]{1,0:T(8,128)(2,1)S(1)}, bf16[512,1024]{1,0:T(8,128)(2,1)}, u32[]{:S(2)}) copy-start(bf16[512,1024]{1,0:T(8,128)(2,1)} %inputs_ref.1) | copy-start | bytes 3145732
  4.1 30.5 %copy-start.16 = (bf16[48,1024]{1,0:T(8,128)(2,1)S(1)}, bf16[48,1024]{1,0:T(8,128)(2,1)}, u32[]{:S(2)}) copy-start(bf16[48,1024]{1,0:T(8,128)(2,1)} %get-tuple-element.184) | copy-start | bytes 294916 | tf_op jit(solution)/shard_map/cond
  4.1 32.2 %collective-permute-start.13 = (bf16[2,2,512,128]{3,2,1,0:T(8,128)(2,1)S(1)}, bf16[2,2,512,128]{3,2,1,0:T(8,128)(2,1)S(1)}, u32[]{:S(2)}, u32[]{:S(2)}) collective-permute-start(bf16[2,2,512,128]{3,2,1,0:T(8,128)(2,1)S(1)} %get-tuple-element.179), channel_id=1, source_target_pairs={{4,8},{12,16},{20,24},{28,32},{36,40},{44,48},{52,56},{60,64},{68,... | collective-permute-start | bytes 1572872 | tf_op jit(solution)/shard_map/cond/branch_3_fun/ppermute | solution.py:353
  9.3 27.0 %collective-permute-start.14 = (bf16[1,2,512,128]{3,2,1,0:T(8,128)(2,1)S(1)}, bf16[1,2,512,128]{3,2,1,0:T(8,128)(2,1)S(1)}, u32[]{:S(2)}, u32[]{:S(2)}) collective-permute-start(bf16[1,2,512,128]{3,2,1,0:T(8,128)(2,1)S(1)} %get-tuple-element.180), channel_id=1, source_target_pairs={{4,8},{12,16},{20,24},{28,32},{36,40},{44,48},{52,56},{60,64},{68,... | collective-permute-start | bytes 786440 | tf_op jit(solution)/shard_map/cond/branch_3_fun/ppermute | solution.py:353
  12.5 23.8 %collective-permute-start.15 = (bf16[1,2,512,128]{3,2,1,0:T(8,128)(2,1)S(1)}, bf16[1,2,512,128]{3,2,1,0:T(8,128)(2,1)S(1)}, u32[]{:S(2)}, u32[]{:S(2)}) collective-permute-start(bf16[1,2,512,128]{3,2,1,0:T(8,128)(2,1)S(1)} %get-tuple-element.181), channel_id=1, source_target_pairs={{0,4},{8,12},{16,20},{24,28},{32,36},{40,44},{48,52},{56,60},{64,6... | collective-permute-start | bytes 786440 | tf_op jit(solution)/shard_map/cond/branch_3_fun/ppermute | solution.py:353
  17.6 18.7 %copy-start.6 = (bf16[512,512]{1,0:T(8,128)(2,1)S(1)}, bf16[512,512]{1,0:T(8,128)(2,1)}, u32[]{:S(2)}) copy-start(bf16[512,512]{1,0:T(8,128)(2,1)} %get-tuple-element.170.v_ref) | copy-start | bytes 1572868 | tf_op jit(solution)/shard_map/cond
  17.6 18.7 %copy-start.11 = (bf16[512,512]{1,0:T(8,128)(2,1)S(1)}, bf16[512,512]{1,0:T(8,128)(2,1)}, u32[]{:S(2)}) copy-start(bf16[512,512]{1,0:T(8,128)(2,1)} %get-tuple-element.171.g_ref) | copy-start | bytes 1572868 | tf_op jit(solution)/shard_map/cond
  17.6 18.7 %copy-start.23 = (bf16[3,16,512]{2,1,0:T(8,128)(2,1)S(1)}, bf16[3,16,512]{2,1,0:T(8,128)(2,1)}, u32[]{:S(2)}) copy-start(bf16[3,16,512]{2,1,0:T(8,128)(2,1)} %get-tuple-element.178.up_ref) | copy-start | bytes 147460 | tf_op jit(solution)/shard_map/cond
  21.4 14.9 %collective-permute-start.12 = (f32[3,8,512]{2,1,0:T(8,128)S(1)}, f32[3,8,512]{2,1,0:T(8,128)S(1)}, u32[]{:S(2)}, u32[]{:S(2)}) collective-permute-start(f32[3,8,512]{2,1,0:T(8,128)S(1)} %get-tuple-element.173.stats_ref), channel_id=1, source_target_pairs={{0,508},{8,4},{16,12},{24,20},{32,28},{40,36},{48,44},{56,52},{64,... | collective-permute-start | bytes 147464 | tf_op jit(solution)/shard_map/cond/branch_3_fun/ppermute | solution.py:362
  43.6 6.2 %copy-start.18 = (bf16[3,512,512]{2,1,0:T(8,128)(2,1)}, bf16[3,512,512]{2,1,0:T(8,128)(2,1)S(1)}, u32[]{:S(2)}) copy-start(bf16[3,512,512]{2,1,0:T(8,128)(2,1)S(1)} %get-tuple-element.213.qkv_ref) | copy-start | bytes 4718596

commit v7 on v6

--- a/solution.py
+++ b/solution.py
@@ -148,7 +148,7 @@
 
 
 def pack_kernel(flags_ref, q_ref, k_ref, v_ref, g_ref, shifted_ref, *refs):
-    *out_refs, order_ref = refs
+    *out_refs, order_ref, sems = refs
     heads = flags_ref.shape[0]
     total = jnp.int32(0)
     for head in range(heads):
@@ -162,20 +162,24 @@
 
     count = list_heads(flags_ref, order_ref, ahead)
     list_heads(flags_ref, order_ref, lambda flag: jnp.logical_not(ahead(flag)), count)
-    base = 0
-    for out_ref in out_refs:
-        for slot in range(out_ref.shape[0]):
-            head = order_ref[base + slot]
-            cols = columns_of(head)
-
-            def send(a_ref, b_ref):
-                out_ref[slot, 0] = a_ref[:, cols]
-                out_ref[slot, 1] = b_ref[:, cols]
-
-            first = is_first(flags_ref[head])
-            pl.when(first)(functools.partial(send, k_ref, v_ref))
-            pl.when(jnp.logical_not(first))(functools.partial(send, q_ref, g_ref))
-        base += out_ref.shape[0]
+    for act in ("start", "wait"):
+        base = 0
+        for out_ref in out_refs:
+            for slot in range(out_ref.shape[0]):
+                head = order_ref[base + slot]
+                cols = columns_of(head)
+
+                def send(*pair):
+                    for index in range(2):
+                        copy = pltpu.make_async_copy(
+                            pair[index].at[:, cols], out_ref.at[slot, index], sems.at[base + slot, index]
+                        )
+                        getattr(copy, act)()
+
+                first = is_first(flags_ref[head])
+                pl.when(first)(functools.partial(send, k_ref, v_ref))
+                pl.when(jnp.logical_not(first))(functools.partial(send, q_ref, g_ref))
+            base += out_ref.shape[0]
 
 
 def early_kernel(factor, scale, flags_ref, q_ref, k_ref, v_ref, g_ref, dq_ref, dk_ref, dv_ref, stats_ref, order_ref):
@@ -382,9 +386,9 @@
     shifted, *packs = pl.pallas_call(
         pack_kernel,
         out_shape=[shape((1,), jnp.int32)] + [shape((size, 2, tok_rows, HEAD), BF16) for size in sizes],
-        in_specs=[SMEM] + [VMEM] * 4,
+        in_specs=[SMEM] + [pl.BlockSpec(memory_space=pl.ANY)] * 4,
         out_specs=[SMEM] + [VMEM] * len(sizes),
-        scratch_shapes=[pltpu.SMEM((heads,), jnp.int32)],
+        scratch_shapes=[pltpu.SMEM((heads,), jnp.int32), pltpu.SemaphoreType.DMA((heads, 2))],
         compiler_params=pltpu.CompilerParams(vmem_limit_bytes=VMEM_BYTES),
     )(flags, queries, keys, values, grads)
     down_t = down.transpose(0, 2, 1).reshape(3 * RANK, width)

time: 105 us -> 106 us (level); the launches traced: 104 us -> 108 us
  blocking collectives: 59.1 us -> 64 us
    all_gather x1, blocking collectives: 6.15 us -> 11.6 us  [local(): parts = lax.all_gather(parts, 'head')]
    ppermute x1, starting transfers between devices: 13.1 us -> 11 us  [attention(): lax.ppermute(stats, CTX, behind)]
    ppermute x3, starting transfers between devices: 13.5 us -> 14.7 us  [attention(): arrived.append(lax.ppermute(pack, CTX, pairs))]
where the time goes in v7:
time: 106 us; the launch traced here: 108 us
  blocking collectives  64 us (60%)
  starting transfers between devices  25.8 us (24%)
  Pallas kernels  14.7 us (14%)
  between operations  1.39 us (1%)
    all_to_all x1, blocking collectives, local(): lax.all_to_all(jnp.broadcast_to(grad, (far,) + grad.shape), FAR, 0, 0)  25.2 us
    all_to_all x1, blocking collectives, local(): grad = lax.all_to_all(grad.reshape(near, rows // near, HEAD), NEAR, 0, 0)  15.2 us
    ppermute x3, starting transfers between devices, attention(): arrived.append(lax.ppermute(pack, CTX, pairs))  14.7 us
    all_to_all x1, blocking collectives, local(): lax.all_to_all(jnp.broadcast_to(grad, (near,) + grad.shape), NEAR, 0, 0)  12 us
    all_gather x1, blocking collectives, local(): parts = lax.all_gather(parts, 'head')  11.6 us
    ppermute x1, starting transfers between devices, attention(): lax.ppermute(stats, CTX, behind)  11 us
    pallas_call x1, Pallas kernels, attention(): call(functools.partial(late_kernel, factor, scale, kv_sides, qg_sides), [...  6.46 us
    pallas_call x1, Pallas kernels, attention(): call(functools.partial(early_kernel, factor, scale), [low, full, full, sh...  4.31 us
  transfers between devices with their start and end apart: 4, of which 1 were waited for; matrix products, arithmetic and copies ran while one was open for 0% of the time, Pallas kernels for 4%

profile of v7, /device:TPU:2, one launch (start us, length us, event | category | flops | bytes accessed | tf_op | source)
XLA Modules:
  0.0 108.1 jit_solution(3470544731470652394)
XLA Ops:
  0.6 0.0 copy-start.1
  0.6 0.0 copy-start.2
  0.7 0.0 copy-start.19
  0.7 0.0 copy-start
  0.7 2.7 %shard_map.103 = (s32[1]{0:T(128)}, bf16[2,2,512,128]{3,2,1,0:T(8,128)(2,1)S(1)}, bf16[1,2,512,128]{3,2,1,0:T(8,128)(2,1)S(1)}, bf16[1,2,512,128]{3,2,1,0:T(8,128)(2,1)S(1)}) custom-call(s32[4]{0:T(128)} %flags_ref.1, bf16[512,512]{1,0:T(8,128)(2,1)} %q_ref.1, bf16[512,512]{1,0:T(8,128)(2,1)} %k_ref.1, bf16[512,512]{1,0:T(8,128)(2,1)} %v_ref.1, ...), custom_call_target="tpu_custom_call" | custom-call | tf_op jit(solution)/shard_map/pallas_call | solution.py:386
  4.1 0.0 copy-done.1
  4.1 0.0 copy-done.2
  4.1 0.0 copy-done.19
  4.1 38.6 %conditional.1 = (bf16[3,512,512]{2,1,0:T(8,128)(2,1)S(1)}, bf16[96,512]{1,0:T(8,128)(2,1)S(1)}) conditional(s32[]{:T(128)} %bitcast, (s32[4]{0:T(128)S(1)}, bf16[512,512]{1,0:T(8,128)(2,1)S(1)}, bf16[512,512]{1,0:T(8,128)(2,1)S(1)}, bf16[512,512]{1,0:T(8,128)(2,1)}, bf16[512,512]{1,0:T(8,128)(2,1)}, ...), branch_computations={%region_0.0_spmd, %region_1.0_spmd, %region_2.0_spmd, %region_3.0_... | conditional | flops 3271778304 | bytes 23216416 | solution.py:395
  4.1 0.0 copy-start.15
  4.1 5.2 %collective-permute-start.9 = (bf16[2,2,512,128]{3,2,1,0:T(8,128)(2,1)S(1)}, bf16[2,2,512,128]{3,2,1,0:T(8,128)(2,1)S(1)}, u32[]{:S(2)}, u32[]{:S(2)}) collective-permute-start(bf16[2,2,512,128]{3,2,1,0:T(8,128)(2,1)S(1)} %get-tuple-element.160), channel_id=1, source_target_pairs={{0,4},{8,12},{16,20},{24,28},{32,36},{40,44},{48,52},{56,60},{64,6... | collective-permute-start | bytes 1572872 | tf_op jit(solution)/shard_map/cond/branch_2_fun/ppermute | solution.py:357
  9.4 3.1 %collective-permute-start.10 = (bf16[1,2,512,128]{3,2,1,0:T(8,128)(2,1)S(1)}, bf16[1,2,512,128]{3,2,1,0:T(8,128)(2,1)S(1)}, u32[]{:S(2)}, u32[]{:S(2)}) collective-permute-start(bf16[1,2,512,128]{3,2,1,0:T(8,128)(2,1)S(1)} %get-tuple-element.161), channel_id=1, source_target_pairs={{0,508},{8,4},{16,12},{24,20},{32,28},{40,36},{48,44},{56,52},{64,... | collective-permute-start | bytes 786440 | tf_op jit(solution)/shard_map/cond/branch_2_fun/ppermute | solution.py:357
  12.5 6.4 %collective-permute-start.11 = (bf16[1,2,512,128]{3,2,1,0:T(8,128)(2,1)S(1)}, bf16[1,2,512,128]{3,2,1,0:T(8,128)(2,1)S(1)}, u32[]{:S(2)}, u32[]{:S(2)}) collective-permute-start(bf16[1,2,512,128]{3,2,1,0:T(8,128)(2,1)S(1)} %get-tuple-element.162), channel_id=1, source_target_pairs={{0,508},{8,4},{16,12},{24,20},{32,28},{40,36},{48,44},{56,52},{64,... | collective-permute-start | bytes 786440 | tf_op jit(solution)/shard_map/cond/branch_2_fun/ppermute | solution.py:357
  18.9 0.0 copy-start.5
  18.9 0.0 copy-start.10
  18.9 0.0 copy-start.22
  18.9 4.3 %branch_2_fun.2 = (bf16[2,512,128]{2,1,0:T(8,128)(2,1)S(1)}, f32[2,512,128]{2,1,0:T(8,128)S(1)}, f32[2,512,128]{2,1,0:T(8,128)S(1)}, f32[2,8,512]{2,1,0:T(8,128)S(1)}) custom-call(s32[4]{0:T(128)S(1)} %get-tuple-element.148.flags_ref, bf16[512,512]{1,0:T(8,128)(2,1)S(1)} %get-tuple-element.149.q_ref, bf16[512,512]{1,0:T(8,128)(2,1)S(1)} %get-tuple-element.150.k_ref, ...), custom_call_target="tpu_custom_call" | custom-call | flops 1 | tf_op jit(solution)/shard_map/cond/branch_2_fun/pallas_call | solution.py:359
  23.3 11.0 %collective-permute-start.8 = (f32[2,8,512]{2,1,0:T(8,128)S(1)}, f32[2,8,512]{2,1,0:T(8,128)S(1)}, u32[]{:S(2)}, u32[]{:S(2)}) collective-permute-start(f32[2,8,512]{2,1,0:T(8,128)S(1)} %get-tuple-element.154.stats_ref), channel_id=1, source_target_pairs={{0,508},{8,4},{16,12},{24,20},{32,28},{40,36},{48,44},{56,52},{64,... | collective-permute-start | bytes 98312 | tf_op jit(solution)/shard_map/cond/branch_2_fun/ppermute | solution.py:366
  34.3 0.4 convolution_convert_fusion.2
  34.7 0.9 collective-permute-done.8.moved_ref
  35.7 0.0 collective-permute-done.10.refs_1_
  35.7 0.0 collective-permute-done.11.refs_2_
  35.7 0.0 collective-permute-done.9.refs_0_
  35.7 6.5 %branch_2_fun.3 = (bf16[3,512,512]{2,1,0:T(8,128)(2,1)S(1)}, bf16[48,512]{1,0:T(8,128)(2,1)S(1)}) custom-call(s32[4]{0:T(128)S(1)} %get-tuple-element.148.flags_ref, bf16[512,512]{1,0:T(8,128)(2,1)S(1)} %get-tuple-element.149.q_ref, bf16[512,512]{1,0:T(8,128)(2,1)S(1)} %get-tuple-element.150.k_ref, bf16[512,512]{1,0:T(8,128)(2,1)S(1)} %copy-done.5, ...), custom_call_target="tpu_custom_call" | custom-call | flops 1610612736 | bytes 6291456 | tf_op jit(solution)/shard_map/cond/branch_2_fun/pallas_call | solution.py:368
  42.7 0.0 copy-start.18
  42.7 11.6 %all-gather = bf16[384,512]{1,0:T(8,128)(2,1)S(1)} all-gather(bf16[96,512]{1,0:T(8,128)(2,1)S(1)} %get-tuple-element.221), channel_id=2, replica_groups=mesh['zh'=8,'zl'=2,'x'=4,'yh'=2,'head'=4] {'head'}, dimensions={0}, use_global_device_ids=true | all-gather | bytes 491520 | tf_op jit(solution)/shard_map/all_gather | solution.py:400
  54.3 0.0 copy-done.18
  54.3 0.5 shard_map.104
  54.8 15.2 %all_to_all.15 = bf16[16,36,128]{2,1,0:T(8,128)(2,1)S(1)} all-to-all(bf16[16,36,128]{2,1,0:T(8,128)(2,1)S(1)} %reshape.26), channel_id=1, replica_groups=mesh['zh'=8,'zl'=2,'x'=4,'yh'=2,'head'=4] {'zl','x','yh'}, dimensions={0} | all-to-all | bytes 294912 | tf_op jit(solution)/shard_map/all_to_all | solution.py:409
  70.1 25.2 %all_to_all.16 = bf16[8,36,128]{2,1,0:T(8,128)(2,1)S(1)} all-to-all(bf16[8,36,128]{2,1,0:T(8,128)(2,1)S(1)} %broadcast_in_dim.6), channel_id=1, replica_groups=mesh['zh'=8,'zl'=2,'x'=4,'yh'=2,'head'=4] {'zh'}, dimensions={0} | all-to-all | bytes 147456 | tf_op jit(solution)/shard_map/all_to_all | solution.py:412
  95.3 12.0 %all_to_all.17 = bf16[16,36,128]{2,1,0:T(8,128)(2,1)S(1)} all-to-all(bf16[16,36,128]{2,1,0:T(8,128)(2,1)S(1)} %broadcast_in_dim.7), channel_id=1, replica_groups=mesh['zh'=8,'zl'=2,'x'=4,'yh'=2,'head'=4] {'zl','x','yh'}, dimensions={0} | all-to-all | bytes 294912 | tf_op jit(solution)/shard_map/all_to_all | solution.py:414
  107.4 0.7 shard_map.105
  (12 shorter events, 0.2 us)
Async XLA Ops:
  0.6 3.4 %copy-start.1 = (bf16[512,512]{1,0:T(8,128)(2,1)S(1)}, bf16[512,512]{1,0:T(8,128)(2,1)}, u32[]{:S(2)}) copy-start(bf16[512,512]{1,0:T(8,128)(2,1)} %q_ref.1) | copy-start | bytes 1572868
  0.6 3.4 %copy-start.2 = (bf16[512,512]{1,0:T(8,128)(2,1)S(1)}, bf16[512,512]{1,0:T(8,128)(2,1)}, u32[]{:S(2)}) copy-start(bf16[512,512]{1,0:T(8,128)(2,1)} %k_ref.1) | copy-start | bytes 1572868
  0.7 3.4 %copy-start.19 = (s32[4]{0:T(128)S(1)}, s32[4]{0:T(128)}, u32[]{:S(2)}) copy-start(s32[4]{0:T(128)} %flags_ref.1) | copy-start | bytes 52
  0.7 3.4 %copy-start = (bf16[512,1024]{1,0:T(8,128)(2,1)S(1)}, bf16[512,1024]{1,0:T(8,128)(2,1)}, u32[]{:S(2)}) copy-start(bf16[512,1024]{1,0:T(8,128)(2,1)} %inputs_ref.1) | copy-start | bytes 3145732
  4.1 30.2 %copy-start.15 = (bf16[48,1024]{1,0:T(8,128)(2,1)S(1)}, bf16[48,1024]{1,0:T(8,128)(2,1)}, u32[]{:S(2)}) copy-start(bf16[48,1024]{1,0:T(8,128)(2,1)} %get-tuple-element.165) | copy-start | bytes 294916 | tf_op jit(solution)/shard_map/cond
  4.1 31.6 %collective-permute-start.9 = (bf16[2,2,512,128]{3,2,1,0:T(8,128)(2,1)S(1)}, bf16[2,2,512,128]{3,2,1,0:T(8,128)(2,1)S(1)}, u32[]{:S(2)}, u32[]{:S(2)}) collective-permute-start(bf16[2,2,512,128]{3,2,1,0:T(8,128)(2,1)S(1)} %get-tuple-element.160), channel_id=1, source_target_pairs={{0,4},{8,12},{16,20},{24,28},{32,36},{40,44},{48,52},{56,60},{64,6... | collective-permute-start | bytes 1572872 | tf_op jit(solution)/shard_map/cond/branch_2_fun/ppermute | solution.py:357
  9.4 26.3 %collective-permute-start.10 = (bf16[1,2,512,128]{3,2,1,0:T(8,128)(2,1)S(1)}, bf16[1,2,512,128]{3,2,1,0:T(8,128)(2,1)S(1)}, u32[]{:S(2)}, u32[]{:S(2)}) collective-permute-start(bf16[1,2,512,128]{3,2,1,0:T(8,128)(2,1)S(1)} %get-tuple-element.161), channel_id=1, source_target_pairs={{0,508},{8,4},{16,12},{24,20},{32,28},{40,36},{48,44},{56,52},{64,... | collective-permute-start | bytes 786440 | tf_op jit(solution)/shard_map/cond/branch_2_fun/ppermute | solution.py:357
  12.5 23.2 %collective-permute-start.11 = (bf16[1,2,512,128]{3,2,1,0:T(8,128)(2,1)S(1)}, bf16[1,2,512,128]{3,2,1,0:T(8,128)(2,1)S(1)}, u32[]{:S(2)}, u32[]{:S(2)}) collective-permute-start(bf16[1,2,512,128]{3,2,1,0:T(8,128)(2,1)S(1)} %get-tuple-element.162), channel_id=1, source_target_pairs={{0,508},{8,4},{16,12},{24,20},{32,28},{40,36},{48,44},{56,52},{64,... | collective-permute-start | bytes 786440 | tf_op jit(solution)/shard_map/cond/branch_2_fun/ppermute | solution.py:357
  18.9 16.8 %copy-start.5 = (bf16[512,512]{1,0:T(8,128)(2,1)S(1)}, bf16[512,512]{1,0:T(8,128)(2,1)}, u32[]{:S(2)}) copy-start(bf16[512,512]{1,0:T(8,128)(2,1)} %get-tuple-element.151.v_ref) | copy-start | bytes 1572868 | tf_op jit(solution)/shard_map/cond
  18.9 16.8 %copy-start.10 = (bf16[512,512]{1,0:T(8,128)(2,1)S(1)}, bf16[512,512]{1,0:T(8,128)(2,1)}, u32[]{:S(2)}) copy-start(bf16[512,512]{1,0:T(8,128)(2,1)} %get-tuple-element.152.g_ref) | copy-start | bytes 1572868 | tf_op jit(solution)/shard_map/cond
  18.9 16.8 %copy-start.22 = (bf16[3,16,512]{2,1,0:T(8,128)(2,1)S(1)}, bf16[3,16,512]{2,1,0:T(8,128)(2,1)}, u32[]{:S(2)}) copy-start(bf16[3,16,512]{2,1,0:T(8,128)(2,1)} %get-tuple-element.159.up_ref) | copy-start | bytes 147460 | tf_op jit(solution)/shard_map/cond
  23.3 12.4 %collective-permute-start.8 = (f32[2,8,512]{2,1,0:T(8,128)S(1)}, f32[2,8,512]{2,1,0:T(8,128)S(1)}, u32[]{:S(2)}, u32[]{:S(2)}) collective-permute-start(f32[2,8,512]{2,1,0:T(8,128)S(1)} %get-tuple-element.154.stats_ref), channel_id=1, source_target_pairs={{0,508},{8,4},{16,12},{24,20},{32,28},{40,36},{48,44},{56,52},{64,... | collective-permute-start | bytes 98312 | tf_op jit(solution)/shard_map/cond/branch_2_fun/ppermute | solution.py:366
  42.7 11.6 %copy-start.18 = (bf16[3,512,512]{2,1,0:T(8,128)(2,1)}, bf16[3,512,512]{2,1,0:T(8,128)(2,1)S(1)}, u32[]{:S(2)}) copy-start(bf16[3,512,512]{2,1,0:T(8,128)(2,1)S(1)} %get-tuple-element.213.qkv_ref) | copy-start | bytes 4718596
